TPU v7x, 32 devices: a whole 2x2x4 slice. The times are simulated.
32 devices in a mesh: clips: 8 (over y, x, core), tm: 4 (over z).
Axes of the slice: x: 2, y: 2, z: 4, core: 2. Of those that a mesh axis runs over, the one named last changes fastest.
Arguments:
- patches: bfloat16 [64, 512, 768], P('clips', 'tm'), may hold values from -6 to 6
- mask_index: int32 [64, 450], P('clips'), may hold values from 0 to 511, as said below
- mask_count: int32 [64], P('clips'), may hold values from 100 to 450, as said below
- w_qkv: bfloat16 [768, 2304], replicated, may hold values from -0.21875 to 0.21875
- q_bias: bfloat16 [768], replicated, may hold values from -3 to 3
- v_bias: bfloat16 [768], replicated, may hold values from -3 to 3
- w_out: bfloat16 [768, 768], replicated, may hold values from -0.875 to 0.875
- out_bias: bfloat16 [768], replicated, may hold values from -3 to 3
- w_up: bfloat16 [768, 3072], replicated, may hold values from -0.21875 to 0.21875
- up_bias: bfloat16 [3072], replicated, may hold values from -3 to 3
- w_down: bfloat16 [3072, 768], replicated, may hold values from -0.109375 to 0.109375
- down_bias: bfloat16 [768], replicated, may hold values from -3 to 3
- norm1_scale: bfloat16 [768], replicated, may hold values from 0.5 to 1.5
- norm1_shift: bfloat16 [768], replicated, may hold values from -3 to 3
- norm2_scale: bfloat16 [768], replicated, may hold values from 0.5 to 1.5
- norm2_shift: bfloat16 [768], replicated, may hold values from -3 to 3
- mask_embed: bfloat16 [768], replicated, may hold values from -6 to 6
- pos_embed: bfloat16 [512, 768], replicated, may hold values from -3 to 3
- cotangent: bfloat16 [64, 512, 768], P('clips', 'tm'), may hold values from -6 to 6
Outputs:
- block_out: bfloat16 [64, 512, 768], P('clips', 'tm')
- input_grad: bfloat16 [64, 512, 768], P('clips', 'tm')
- grad_w_qkv: float32 [768, 2304], replicated
- grad_q_bias: float32 [768], replicated
- grad_v_bias: float32 [768], replicated
- grad_w_out: float32 [768, 768], replicated
- grad_out_bias: float32 [768], replicated
- grad_w_up: float32 [768, 3072], replicated
- grad_up_bias: float32 [3072], replicated
- grad_w_down: float32 [3072, 768], replicated
- grad_down_bias: float32 [768], replicated
- grad_norm1_scale: float32 [768], replicated
- grad_norm1_shift: float32 [768], replicated
- grad_norm2_scale: float32 [768], replicated
- grad_norm2_shift: float32 [768], replicated
- grad_mask_embed: float32 [768], replicated
- grad_pos_embed: float32 [512, 768], replicated
Inputs may be any that keep to these rules, and one draw needn't show every extreme that they name: `mask_index`: the entries of one clip's list are distinct positions of that clip; the entries after its first mask_count ones are other positions and are not masked. `mask_count`: every draw has a clip with exactly 450 and a clip with exactly 100 masked positions.
All inputs are finite; a program needn't handle non-finite values.
Results may differ from a plain program's by a relative error of at most 0.012.
Values may be sent and summed in bfloat16 or wider, within the bound.
No kernel may reach another device: no remote copies, remote signals or barrier semaphores. Data moves between devices by JAX's collectives and lax.ppermute only.
A program may use at most 256 MiB of HBM per device.

v0:
```python
import jax
import jax.numpy as jnp
from jax import lax
from jax.sharding import PartitionSpec as P

HEADS = 12


NORM_EPS = 1e-06
ROOT_HALF = 0.7071067811865476
ROOT_TWO_PI = 2.5066282746310002


def norm_forward(values, gains, shifts):
    centred = values - jnp.mean(values, -1, keepdims=True)
    spread = jnp.mean(centred * centred, -1, keepdims=True)
    inverse = lax.rsqrt(spread + NORM_EPS)
    unit = centred * inverse
    return (unit * gains + shifts, unit, inverse)


def norm_backward(grad_norm, unit, inverse, gains):
    scaled = grad_norm * gains
    return inverse * (
        scaled
        - jnp.mean(scaled, -1, keepdims=True)
        - unit * jnp.mean(scaled * unit, -1, keepdims=True)
    )


def group_size(clip_count, seg_rows):
    for trial in range(1, clip_count + 1):
        if clip_count % trial == 0 and trial * seg_rows >= 512:
            return trial
    return clip_count


def to_blocks(values, clip_group, head_count):
    shape = values.shape
    return values.reshape(
        (shape[0] // clip_group, clip_group, shape[1], head_count, shape[2] // head_count)
    )


def stat_blocks(values, clip_group):
    shape = values.shape
    return values.reshape((shape[0] // clip_group, clip_group) + shape[1:])


def from_blocks(values):
    shape = values.shape
    return values.reshape((shape[0] * shape[1], shape[2], shape[3] * shape[4]))


def attend_forward(block_items):
    queries, key_rows, value_rows = block_items
    score_scale = queries.shape[-1] ** (-0.5)
    scores = (
        jnp.einsum("gqhe,gkhe->ghqk", queries, key_rows, preferred_element_type=jnp.float32)
        * score_scale
    )
    row_peak = jnp.max(scores, -1, keepdims=True)
    exp_scores = jnp.exp(scores - row_peak)
    denom_sum = jnp.sum(exp_scores, -1, keepdims=True)
    attn_probs = (exp_scores / denom_sum).astype(jnp.bfloat16)
    mixed_out = jnp.einsum(
        "ghqk,gkhe->gqhe", attn_probs, value_rows, preferred_element_type=jnp.float32
    )
    log_sum = jnp.swapaxes((row_peak + jnp.log(denom_sum))[..., 0], 1, 2)
    return (mixed_out, log_sum)


def attend_backward(block_items):
    queries, key_rows, value_rows, grad_mix, log_sum = block_items
    score_scale = queries.shape[-1] ** (-0.5)
    scores = (
        jnp.einsum("gqhe,gkhe->ghqk", queries, key_rows, preferred_element_type=jnp.float32)
        * score_scale
    )
    attn_probs = jnp.exp(scores - jnp.swapaxes(log_sum, 1, 2)[..., None])
    grad_probs = jnp.einsum(
        "gqhe,gkhe->ghqk", grad_mix, value_rows, preferred_element_type=jnp.float32
    )
    row_delta = jnp.sum(attn_probs * grad_probs, -1, keepdims=True)
    grad_scores = (attn_probs * (grad_probs - row_delta)).astype(jnp.bfloat16)
    grad_query = (
        jnp.einsum("ghqk,gkhe->gqhe", grad_scores, key_rows, preferred_element_type=jnp.float32)
        * score_scale
    )
    grad_keys = (
        jnp.einsum("ghqk,gqhe->gkhe", grad_scores, queries, preferred_element_type=jnp.float32)
        * score_scale
    )
    grad_values = jnp.einsum(
        "ghqk,gqhe->gkhe",
        attn_probs.astype(jnp.bfloat16),
        grad_mix,
        preferred_element_type=jnp.float32,
    )
    return (grad_query, grad_keys, grad_values)


def gather_keys(own_keys, own_values):
    return (
        lax.all_gather(own_keys, "tm", axis=1, tiled=True),
        lax.all_gather(own_values, "tm", axis=1, tiled=True),
    )


def local_backward(queries, all_keys, all_values, grad_mix, log_sum, clip_group, head_count):
    grad_query, grad_keys, grad_values = lax.map(
        attend_backward,
        (
            to_blocks(queries, clip_group, head_count),
            to_blocks(all_keys, clip_group, head_count),
            to_blocks(all_values, clip_group, head_count),
            to_blocks(grad_mix, clip_group, head_count),
            stat_blocks(log_sum, clip_group),
        ),
    )
    return (from_blocks(grad_query), from_blocks(grad_keys), from_blocks(grad_values))


def key_grads_summed(
    queries, all_keys, all_values, own_keys, own_values, grad_mix, log_sum, clip_group, head_count
):
    grad_query, grad_keys, grad_values = local_backward(
        queries, all_keys, all_values, grad_mix, log_sum, clip_group, head_count
    )
    grad_keys, grad_values = (
        lax.psum_scatter(grad_keys, "tm", scatter_dimension=1, tiled=True),
        lax.psum_scatter(grad_values, "tm", scatter_dimension=1, tiled=True),
    )
    return (grad_query, grad_keys, grad_values)


def run_layer(inputs, masked, pos_rows, grad_rows, params, share, backward):
    (
        w_qkv,
        q_bias,
        v_bias,
        w_out,
        out_bias,
        w_up,
        up_bias,
        w_down,
        down_bias,
        norm1_scale,
        norm1_shift,
        norm2_scale,
        norm2_shift,
        mask_embed,
    ) = params
    clip_count, seg_rows, model_width = inputs.shape
    head_count = HEADS
    row_count = clip_count * seg_rows
    clip_group = group_size(clip_count, seg_rows)
    shape_three = (clip_count, seg_rows, model_width)
    flat_mask = masked.reshape(row_count, 1)
    chosen = jnp.where(
        flat_mask,
        mask_embed.astype(jnp.float32)[None, :],
        inputs.reshape(row_count, model_width).astype(jnp.float32),
    )
    filled = (chosen.reshape(shape_three) + pos_rows.astype(jnp.float32)[None, :, :]).reshape(
        row_count, model_width
    )
    normed_one, unit_one, inverse_one = norm_forward(
        filled, norm1_scale.astype(jnp.float32), norm1_shift.astype(jnp.float32)
    )
    normed_one = normed_one.astype(jnp.bfloat16)
    joint_proj = jnp.dot(normed_one, w_qkv, preferred_element_type=jnp.float32)
    queries = (
        (joint_proj[:, :model_width] + q_bias.astype(jnp.float32))
        .astype(jnp.bfloat16)
        .reshape(shape_three)
    )
    own_keys = (
        joint_proj[:, model_width : 2 * model_width].astype(jnp.bfloat16).reshape(shape_three)
    )
    own_values = (
        (joint_proj[:, 2 * model_width :] + v_bias.astype(jnp.float32))
        .astype(jnp.bfloat16)
        .reshape(shape_three)
    )
    all_keys, all_values = share(own_keys, own_values)
    mixed_out, log_sum = lax.map(
        attend_forward,
        (
            to_blocks(queries, clip_group, head_count),
            to_blocks(all_keys, clip_group, head_count),
            to_blocks(all_values, clip_group, head_count),
        ),
    )
    attended = from_blocks(mixed_out).reshape(row_count, model_width).astype(jnp.bfloat16)
    log_sum = log_sum.reshape(clip_count, seg_rows, head_count)
    hidden = (
        filled
        + jnp.dot(attended, w_out, preferred_element_type=jnp.float32)
        + out_bias.astype(jnp.float32)
    )
    normed_two, unit_two, inverse_two = norm_forward(
        hidden, norm2_scale.astype(jnp.float32), norm2_shift.astype(jnp.float32)
    )
    normed_two = normed_two.astype(jnp.bfloat16)
    up_proj = jnp.dot(normed_two, w_up, preferred_element_type=jnp.float32) + up_bias.astype(
        jnp.float32
    )
    cumulative = 0.5 * (1.0 + jax.scipy.special.erf(up_proj * ROOT_HALF))
    activated = (up_proj * cumulative).astype(jnp.bfloat16)
    block_out = (
        hidden
        + jnp.dot(activated, w_down, preferred_element_type=jnp.float32)
        + down_bias.astype(jnp.float32)
    ).astype(jnp.bfloat16)
    grad_flat = grad_rows.reshape(row_count, model_width)
    grad_top = grad_flat.astype(jnp.float32)
    grad_down = jnp.dot(activated.T, grad_flat, preferred_element_type=jnp.float32)
    grad_down_bias = jnp.sum(grad_top, 0)
    grad_act = jnp.dot(grad_flat, w_down.T, preferred_element_type=jnp.float32)
    slope = cumulative + up_proj * jnp.exp(-0.5 * up_proj * up_proj) / ROOT_TWO_PI
    grad_up_in = (grad_act * slope).astype(jnp.bfloat16)
    grad_up = jnp.dot(normed_two.T, grad_up_in, preferred_element_type=jnp.float32)
    grad_up_bias = jnp.sum(grad_up_in.astype(jnp.float32), 0)
    grad_norm_two = jnp.dot(grad_up_in, w_up.T, preferred_element_type=jnp.float32)
    grad_scale_two = jnp.sum(grad_norm_two * unit_two, 0)
    grad_shift_two = jnp.sum(grad_norm_two, 0)
    grad_hidden = grad_top + norm_backward(
        grad_norm_two, unit_two, inverse_two, norm2_scale.astype(jnp.float32)
    )
    grad_branch = grad_hidden.astype(jnp.bfloat16)
    grad_out = jnp.dot(attended.T, grad_branch, preferred_element_type=jnp.float32)
    grad_out_bias = jnp.sum(grad_branch.astype(jnp.float32), 0)
    grad_mix = (
        jnp.dot(grad_branch, w_out.T, preferred_element_type=jnp.float32)
        .astype(jnp.bfloat16)
        .reshape(shape_three)
    )
    grad_query, grad_keys, grad_values = backward(
        queries,
        all_keys,
        all_values,
        own_keys,
        own_values,
        grad_mix,
        log_sum,
        clip_group,
        head_count,
    )
    grad_query = grad_query.reshape(row_count, model_width).astype(jnp.bfloat16)
    grad_values = grad_values.reshape(row_count, model_width).astype(jnp.bfloat16)
    grad_keys = grad_keys.reshape(row_count, model_width).astype(jnp.bfloat16)
    grad_joint = jnp.concatenate([grad_query, grad_keys, grad_values], axis=1)
    grad_qkv = jnp.dot(normed_one.T, grad_joint, preferred_element_type=jnp.float32)
    grad_q_bias = jnp.sum(grad_query.astype(jnp.float32), 0)
    grad_v_bias = jnp.sum(grad_values.astype(jnp.float32), 0)
    grad_norm_one = jnp.dot(grad_joint, w_qkv.T, preferred_element_type=jnp.float32)
    grad_scale_one = jnp.sum(grad_norm_one * unit_one, 0)
    grad_shift_one = jnp.sum(grad_norm_one, 0)
    grad_filled = grad_hidden + norm_backward(
        grad_norm_one, unit_one, inverse_one, norm1_scale.astype(jnp.float32)
    )
    grad_mask = jnp.sum(jnp.where(flat_mask, grad_filled, 0.0), 0)
    grad_pos = jnp.sum(grad_filled.reshape(shape_three), 0)
    input_grad = jnp.where(flat_mask, 0.0, grad_filled).astype(jnp.bfloat16).reshape(shape_three)
    weight_grads = (
        grad_qkv,
        grad_q_bias,
        grad_v_bias,
        grad_out,
        grad_out_bias,
        grad_up,
        grad_up_bias,
        grad_down,
        grad_down_bias,
        grad_scale_one,
        grad_shift_one,
        grad_scale_two,
        grad_shift_two,
        grad_mask,
        grad_pos,
    )
    return (block_out.reshape(shape_three), input_grad, weight_grads)


def sum_everywhere(weight_grads, model_width):
    ff_width = weight_grads[6].shape[0]
    small_parts = jnp.concatenate(
        [
            weight_grads[1],
            weight_grads[2],
            weight_grads[4],
            weight_grads[6],
            weight_grads[8],
            weight_grads[9],
            weight_grads[10],
            weight_grads[11],
            weight_grads[12],
            weight_grads[13],
        ]
    )
    pos_shape = weight_grads[14].shape
    share_qkv, share_out, share_up, share_down, share_small, share_pos = (
        lax.psum_scatter(
            weight_grads[0].reshape(-1), ("clips", "tm"), scatter_dimension=0, tiled=True
        ),
        lax.psum_scatter(
            weight_grads[3].reshape(-1), ("clips", "tm"), scatter_dimension=0, tiled=True
        ),
        lax.psum_scatter(
            weight_grads[5].reshape(-1), ("clips", "tm"), scatter_dimension=0, tiled=True
        ),
        lax.psum_scatter(
            weight_grads[7].reshape(-1), ("clips", "tm"), scatter_dimension=0, tiled=True
        ),
        lax.psum_scatter(small_parts, ("clips", "tm"), scatter_dimension=0, tiled=True),
        lax.psum_scatter(
            weight_grads[14].reshape(-1), ("clips", "tm"), scatter_dimension=0, tiled=True
        ),
    )
    whole_qkv, whole_out, whole_up, whole_down, whole_small, whole_pos = (
        lax.all_gather(share_qkv.astype(jnp.bfloat16), ("clips", "tm"), axis=0, tiled=True).astype(
            share_qkv.dtype
        ),
        lax.all_gather(share_out.astype(jnp.bfloat16), ("clips", "tm"), axis=0, tiled=True).astype(
            share_out.dtype
        ),
        lax.all_gather(share_up.astype(jnp.bfloat16), ("clips", "tm"), axis=0, tiled=True).astype(
            share_up.dtype
        ),
        lax.all_gather(share_down.astype(jnp.bfloat16), ("clips", "tm"), axis=0, tiled=True).astype(
            share_down.dtype
        ),
        lax.all_gather(
            share_small.astype(jnp.bfloat16), ("clips", "tm"), axis=0, tiled=True
        ).astype(share_small.dtype),
        lax.all_gather(share_pos.astype(jnp.bfloat16), ("clips", "tm"), axis=0, tiled=True).astype(
            share_pos.dtype
        ),
    )
    base = 3 * model_width + ff_width
    vec_q = whole_small[0:model_width]
    vec_v = whole_small[model_width : 2 * model_width]
    vec_out = whole_small[2 * model_width : 3 * model_width]
    vec_up = whole_small[3 * model_width : base]
    vec_down = whole_small[base : base + model_width]
    scale_one = whole_small[base + model_width : base + 2 * model_width]
    shift_one = whole_small[base + 2 * model_width : base + 3 * model_width]
    scale_two = whole_small[base + 3 * model_width : base + 4 * model_width]
    shift_two = whole_small[base + 4 * model_width : base + 5 * model_width]
    vec_mask = whole_small[base + 5 * model_width : base + 6 * model_width]
    return (
        whole_qkv.reshape(model_width, 3 * model_width),
        vec_q,
        vec_v,
        whole_out.reshape(model_width, model_width),
        vec_out,
        whole_up.reshape(model_width, ff_width),
        vec_up,
        whole_down.reshape(ff_width, model_width),
        vec_down,
        scale_one,
        shift_one,
        scale_two,
        shift_two,
        vec_mask,
        whole_pos.reshape(pos_shape),
    )


def on_device(
    patches,
    mask_index,
    mask_count,
    w_qkv,
    q_bias,
    v_bias,
    w_out,
    out_bias,
    w_up,
    up_bias,
    w_down,
    down_bias,
    norm1_scale,
    norm1_shift,
    norm2_scale,
    norm2_shift,
    mask_embed,
    pos_embed,
    cotangent,
):
    params = (
        w_qkv,
        q_bias,
        v_bias,
        w_out,
        out_bias,
        w_up,
        up_bias,
        w_down,
        down_bias,
        norm1_scale,
        norm1_shift,
        norm2_scale,
        norm2_shift,
        mask_embed,
    )
    clip_count, seg_rows, model_width = patches.shape
    length = seg_rows * lax.axis_size("tm")
    slots = jnp.arange(mask_index.shape[1], dtype=jnp.int32)
    places = jnp.arange(length, dtype=jnp.int32)
    live = slots[None, :] < mask_count[:, None]
    masked_full = jnp.any(
        (mask_index[:, :, None] == places[None, None, :]) & live[:, :, None], axis=1
    )
    start = lax.axis_index("tm") * seg_rows
    masked = lax.dynamic_slice_in_dim(masked_full, start, seg_rows, 1)
    pos_rows = lax.dynamic_slice_in_dim(pos_embed, start, seg_rows, 0)
    block_out, input_grad, weight_grads = run_layer(
        patches, masked, pos_rows, cotangent, params, gather_keys, key_grads_summed
    )
    pos_term = lax.dynamic_update_slice_in_dim(
        jnp.zeros((length, model_width), jnp.float32), weight_grads[14], start, 0
    )
    weight_grads = weight_grads[:14] + (pos_term,)
    summed = sum_everywhere(weight_grads, model_width)
    return (block_out, input_grad) + summed


def solution(mesh):
    in_specs = (
        P("clips", "tm", None),
        P("clips", None),
        P("clips"),
        P(),
        P(),
        P(),
        P(),
        P(),
        P(),
        P(),
        P(),
        P(),
        P(),
        P(),
        P(),
        P(),
        P(),
        P(),
        P("clips", "tm", None),
    )
    out_specs = (
        P("clips", "tm", None),
        P("clips", "tm", None),
        P(),
        P(),
        P(),
        P(),
        P(),
        P(),
        P(),
        P(),
        P(),
        P(),
        P(),
        P(),
        P(),
        P(),
        P(),
    )
    return jax.shard_map(
        on_device, mesh=mesh, in_specs=in_specs, out_specs=out_specs, check_vma=False
    )
```

profile of v0, /device:TPU:0, one launch (start us, length us, event | category | flops | bytes accessed | tf_op | source)
XLA Modules:
  0.0 1667.7 jit_solution(9954434703406368921)
XLA Ops:
  12.2 3.5 fusion.48
  22.3 3.8 fusion.65
  31.0 3.2 slice.73
  37.6 3.9 reshape_reshape.4
  41.5 3.2 copy.84
  46.5 102.6 %all-gather.7.cloned.1.call-done = bf16[8,512,768]{2,1,0:T(8,128)(2,1)} async-done(((bf16[8,128,768]{2,1,0:T(8,128)(2,1)}), bf16[8,512,768]{2,1,0:T(8,128)(2,1)}) %all-gather.7.cloned.1.call-update) | async-done | bytes 6291472 | tf_op jit(solution)/shard_map/all_gather | solution.py:106
  149.1 8.7 copy.81
  157.8 107.0 %all-gather.9.cloned.1.call-done = bf16[8,512,768]{2,1,0:T(8,128)(2,1)} async-done(((bf16[8,128,768]{2,1,0:T(8,128)(2,1)}), bf16[8,512,768]{2,1,0:T(8,128)(2,1)}) %all-gather.9.cloned.1.call-update) | async-done | bytes 6291472 | tf_op jit(solution)/shard_map/all_gather | solution.py:105
  264.8 8.6 copy.83
  275.0 27.4 %while.26 = (s32[]{:T(128)}, bf16[2,4,128,12,64]{2,4,3,1,0:T(8,128)(2,1)}, f32[2,4,128,12]{2,3,1,0:T(8,128)}, bf16[2,4,512,12,64]{2,4,3,1,0:T(8,128)(2,1)}, bf16...) while((s32[]{:T(128)}, bf16[2,4,128,12,64]{2,4,3,1,0:T(8,128)(2,1)}, ...), condition=%wide.region_6.7_spmd, body=%wide.region_3.6_spmd.sunk | while | flops 833611776 | bytes 84781288 | solution.py:187
  275.0 4.1 multiply_reduce_fusion.12
  279.1 3.1 fusion.99
  282.3 5.2 bitcast_dynamic-update-slice_fusion.10
  288.7 4.1 multiply_reduce_fusion.12
  292.8 3.1 fusion.99
  296.0 5.2 bitcast_dynamic-update-slice_fusion.10
  302.3 3.8 copy.85
  306.1 3.8 convert_element_type.162
  309.9 4.3 fusion.64
  315.1 13.5 multiply_convert_fusion.1
  328.6 12.6 convert_reduce_fusion
  341.2 6.1 multiply_reduce_fusion.2
  356.2 3.8 reshape_reshape.10
  361.6 67.6 %while.27 = (s32[]{:T(128)}, bf16[2,4,128,12,64]{2,4,3,1,0:T(8,128)(2,1)}, f32[2,4,512,12,64]{2,4,3,1,0:T(8,128)}, f32[2,4,512,12,64]{2,4,3,1,0:T(8,128)}, bf16[...) while((s32[]{:T(128)}, ...), condition=%wide.region_13.14_spmd, body=%wide.region_11.13_spmd.sunk | while | flops 2052974592 | bytes 154512704 | solution.py:111
  362.0 4.1 fusion.107
  366.5 8.7 multiply_reduce_fusion.13
  375.2 6.6 multiply_convert_fusion.3
  381.9 4.5 bitcast_dynamic-update-slice_fusion.12
  387.5 3.7 bitcast_dynamic-update-slice_fusion.13
  391.2 4.3 bitcast_dynamic-update-slice_fusion.14
  395.6 4.1 fusion.107
  400.1 8.7 multiply_reduce_fusion.13
  408.8 6.6 multiply_convert_fusion.3
  415.4 4.5 bitcast_dynamic-update-slice_fusion.12
  421.1 3.7 bitcast_dynamic-update-slice_fusion.13
  424.7 4.4 bitcast_dynamic-update-slice_fusion.14
  433.4 4.2 copy.89
  437.6 3.9 convert_element_type.176
  443.9 5.2 fusion.58
  449.1 3.2 reshape.249
  452.4 9.1 convolution_bitcast_fusion
  461.5 5.9 copy.95
  467.4 10.1 fusion.66
  477.5 10.8 reshape.255
  489.6 149.8 %reduce-scatter.5.cloned.1.call-done = f32[8,128,768]{1,2,0:T(8,128)} async-done(((f32[8,512,768]{1,2,0:T(8,128)}), f32[8,128,768]{1,2,0:T(8,128)}) %reduce-scatter.5.cloned.1.call-update) | async-done | bytes 3145744 | tf_op jit(solution)/shard_map/reduce_scatter | solution.py:132
  639.4 4.0 convert_reduce_fusion.3
  648.6 206.0 %reduce-scatter.3.cloned.1.call-done = f32[8,128,768]{1,2,0:T(8,128)} async-done(((f32[8,512,768]{1,2,0:T(8,128)}), f32[8,128,768]{1,2,0:T(8,128)}) %reduce-scatter.3.cloned.1.call-update) | async-done | bytes 3145744 | tf_op jit(solution)/shard_map/reduce_scatter | solution.py:131
  854.6 3.3 convert_element_type.177
  863.1 9.4 multiply_reduce_fusion.3
  872.5 9.1 fusion.53
  882.8 7.9 reshape.246
  901.2 5.7 select_reduce_fusion
  915.7 485.0 %all-reduce.9 = (bf16[1769472]{0:T(1024)(128)(2,1)}, bf16[9984]{0:T(1024)(128)(2,1)}, bf16[589824]{0:T(1024)(128)(2,1)}, bf16[2359296]{0:T(1024)(128)(2,1)}, bf1...) all-reduce(f32[1769472]{0:T(1024)} %reshape.246, ...), channel_id=4, replica_groups=mesh['clips'=8,'tm'=4] {'clips','tm'}, use_global_device_ids=true, to_apply=%region_18.19.clone | all-reduce | flops 7481088 | bytes 44886528
  1407.1 9.9 add_convert_fusion
  1419.8 38.2 %all-reduce = bf16[9984]{0:T(1024)(128)(2,1)} all-reduce(bf16[9984]{0:T(1024)(128)(2,1)} %dynamic-update-slice), channel_id=1, replica_groups=mesh['clips'=8,'tm'=4] {'clips','tm'}, use_global_device_ids=true, to_apply=%add | all-reduce | flops 9984 | bytes 39936
  1460.0 81.1 %all_gather.31 = bf16[393216]{0:T(1024)(128)(2,1)} all-gather(bf16[12288]{0:T(1024)(128)(2,1)S(1)} %dynamic-slice.16), channel_id=1, replica_groups=mesh['clips'=8,'tm'=4] {'clips','tm'}, dimensions={0}, use_global_device_ids=true | all-gather | bytes 811008 | tf_op jit(solution)/shard_map/all_gather | solution.py:337
  1541.1 2.9 reshape.271
  1545.5 3.4 select_convert_fusion
  1548.9 3.3 reshape.265
  1552.2 7.9 reshape.263
  1560.2 25.0 %all-gather.15.cloned.1.call-done = bf16[2359296]{0:T(1024)(128)(2,1)} async-done(((bf16[73728]{0:T(1024)(128)(2,1)}), bf16[2359296]{0:T(1024)(128)(2,1)}) %all-gather.15.cloned.1.call-update) | async-done | bytes 4718608 | tf_op jit(solution)/shard_map/all_gather | solution.py:328
  1585.2 8.7 reshape.267
  1593.9 56.4 %all-gather.17.cloned.1.call-done = bf16[2359296]{0:T(1024)(128)(2,1)} async-done(((bf16[73728]{0:T(1024)(128)(2,1)}), bf16[2359296]{0:T(1024)(128)(2,1)}) %all-gather.17.cloned.1.call-update) | async-done | bytes 4718608 | tf_op jit(solution)/shard_map/all_gather | solution.py:331
  1650.4 10.0 reshape.269
  (238 shorter events, 91.0 us)
Async XLA Ops:
  7.2 15.2 copy-start
  7.2 141.9 %all-gather.7.cloned.1.call-start = ((), (), s32[]{:S(2)}) async-start(), calls=%async_computation.2 | async-start | bytes 7864320 | tf_op jit(solution)/shard_map/all_gather | solution.py:106
  11.1 6.8 copy-start.17
  15.7 3.2 copy-start.43
  15.7 3.2 copy-start.47
  15.7 3.2 copy-start.48
  15.7 3.2 copy-start.49
  15.7 3.3 copy-start.50
  17.9 3.2 copy-start.34
  26.2 4.7 copy-start.12
  30.9 3.6 copy-start.51
  30.9 233.9 %all-gather.9.cloned.1.call-start = ((), (), s32[]{:S(2)}) async-start(), calls=%async_computation.3 | async-start | bytes 7864320 | tf_op jit(solution)/shard_map/all_gather | solution.py:105
  34.2 605.2 %reduce-scatter.5.cloned.1.call-start = ((), (), s32[]{:S(2)}) async-start(), calls=%async_computation.5 | async-start | bytes 15728640 | tf_op jit(solution)/shard_map/reduce_scatter | solution.py:132
  37.6 7.1 copy-start.45
  37.6 7.7 copy-start.52
  37.6 8.3 copy-start.53
  279.1 3.2 copy-start.15
  282.3 5.2 copy-start.23
  292.8 3.2 copy-start.15
  296.0 5.2 copy-start.23
  302.3 7.6 copy-start.46
  314.2 33.1 %copy-start.5 = (f32[1024,768]{1,0:T(8,128)}, f32[1024,768]{1,0:T(8,128)S(1)}, u32[]{:S(2)}) copy-start(f32[1024,768]{1,0:T(8,128)S(1)} %get-tuple-element.249) | copy-start | bytes 9437188
  314.3 33.1 %copy-start.26 = (f32[1024]{0:T(1024)}, f32[1024]{0:T(1024)S(1)}, u32[]{:S(2)}) copy-start(f32[1024]{0:T(1024)S(1)} %broadcast_multiply_fusion.4) | copy-start | bytes 12292
  314.3 14.3 slice-start.2
  315.1 32.3 %copy-start.28 = (f32[1024]{0:T(1024)}, f32[1024]{0:T(1024)S(1)}, u32[]{:S(2)}) copy-start(f32[1024]{0:T(1024)S(1)} %add_rsqrt_fusion) | copy-start | bytes 12292
  315.1 13.5 copy-start.13
  315.1 13.5 slice-start.3
  315.1 26.1 %slice-start = ((s8[4718592]{0:T(1024)(128)(4,1)}), s8[4194304]{0:T(1024)(128)(4,1)S(1)}, s32[]{:S(2)}) async-start(s8[4718592]{0:T(1024)(128)(4,1)} %bitcast.178), calls=%async_computation.10 | async-start | bytes 8388608
  328.6 12.6 slice-start.1
  341.2 6.1 copy-start.11
  347.4 3.7 copy-start.55
  362.0 4.1 copy-start.25
  362.0 4.1 copy-start.7
  366.5 8.7 copy-start.1
  375.2 6.7 copy-start.8
  381.9 5.6 copy-start.3
  387.5 3.7 copy-start.2
  395.6 4.1 copy-start.25
  395.6 4.1 copy-start.7
  400.1 8.7 copy-start.1
  408.8 6.7 copy-start.8
  415.4 5.6 copy-start.3
  421.1 3.7 copy-start.2
  429.2 425.4 %reduce-scatter.3.cloned.1.call-start = ((), (), s32[]{:S(2)}) async-start(), calls=%async_computation.4 | async-start | bytes 15728640 | tf_op jit(solution)/shard_map/reduce_scatter | solution.py:131
  429.8 1119.1 %all-gather.13.cloned.1.call-start = ((), (), s32[]{:S(2)}) async-start(), calls=%async_computation.7 | async-start | bytes 1216512 | tf_op jit(solution)/shard_map/all_gather | solution.py:325
  449.1 3.3 copy-start.27
  449.1 3.3 copy-start.29
  449.1 3.3 copy-start.31
  449.1 3.3 copy-start.33
  461.4 6.0 copy-start.14
  477.5 10.8 copy-start.41
  857.8 5.2 copy-start.35
  857.8 5.2 copy-start.37
  857.8 5.2 copy-start.39
  863.0 9.4 copy-start.18
  863.1 9.4 copy-start.19
  863.1 9.4 copy-start.20
  863.1 9.4 copy-start.22
  882.8 9.2 copy-start.40
  915.7 491.4 %copy-start.54 = (bf16[768]{0:T(1024)(128)(2,1)S(1)}, bf16[768]{0:T(1024)(128)(2,1)}, u32[]{:S(2)}) copy-start(bf16[768]{0:T(1024)(128)(2,1)} %param.34) | copy-start | bytes 4612
  1402.1 150.1 %all-gather.11.cloned.1.call-start = ((), (), s32[]{:S(2)}) async-start(), calls=%async_computation.6 | async-start | bytes 3649536 | tf_op jit(solution)/shard_map/all_gather | solution.py:322
  1403.8 181.4 %all-gather.15.cloned.1.call-start = ((), (), s32[]{:S(2)}) async-start(), calls=%async_computation.8 | async-start | bytes 4866048 | tf_op jit(solution)/shard_map/all_gather | solution.py:328
  1405.4 244.9 %all-gather.17.cloned.1.call-start = ((), (), s32[]{:S(2)}) async-start(), calls=%async_computation.9 | async-start | bytes 4866048 | tf_op jit(solution)/shard_map/all_gather | solution.py:331
  1417.0 128.4 %copy-start.44 = (pred[1024]{0:T(1024)(128)(4,1)S(1)}, pred[1024]{0:T(1024)(128)(4,1)}, u32[]{:S(2)}) copy-start(pred[1024]{0:T(1024)(128)(4,1)} %fusion.87) | copy-start | bytes 3076
  (16 other events, 24.1 us)
Sparse Core Ops, SparseCore 0:
  31.0 118.0 all-gather.6
  151.3 113.5 all-gather.8
  429.3 210.0 reduce-scatter.4
  641.6 212.8 reduce-scatter.2
  1402.3 53.3 all-gather.12
  1458.9 60.2 all-gather.10
  1522.5 62.6 all-gather.14
  1588.0 62.3 all-gather.16
where the time goes:
time: 1680 us; the launch traced here: 1670 us
  waiting for transfers between devices  648 us (39%)
  blocking collectives  604 us (36%)
  local copies, waits for them, and re-layouts  172 us (10%)
  matrix products  165 us (10%)
  other arithmetic  61.9 us (4%)
    unnamed x2, blocking collectives  523 us
    reduce_scatter x1, waiting for transfers between devices, key_grads_summed(): lax.psum_scatter(grad_keys, 'tm', scatter_dimension=1, tiled=True)  206 us
    reduce_scatter x1, waiting for transfers between devices, key_grads_summed(): lax.psum_scatter(grad_values, 'tm', scatter_dimension=1, tiled=True)  150 us
    all_gather x1, waiting for transfers between devices, gather_keys(): lax.all_gather(own_keys, 'tm', axis=1, tiled=True)  107 us
    all_gather x1, waiting for transfers between devices, gather_keys(): lax.all_gather(own_values, 'tm', axis=1, tiled=True)  103 us
    all_gather x1, blocking collectives, sum_everywhere(): lax.all_gather(share_pos.astype(jnp.bfloat16), ('clips', 'tm'), axis=0, t...  81.1 us
    all_gather x1, waiting for transfers between devices, sum_everywhere(): lax.all_gather(share_down.astype(jnp.bfloat16), ('clips', 'tm'), axis=0,...  56.4 us
    unnamed x115, local copies, waits for them, and re-layouts  35.8 us
  transfers between devices with their start and end apart: 8, of which 6 were waited for; matrix products, arithmetic and copies ran while one was open for 8% of the time, Pallas kernels for 0%

commit v1 on v0

v1 whole, which is shorter than its diff:
```python
import jax
import jax.numpy as jnp
from jax import lax
from jax.sharding import PartitionSpec as P

HEADS = 12
NORM_EPS = 1e-06
ROOT_HALF = 0.7071067811865476
ROOT_TWO_PI = 2.5066282746310002
F32 = jnp.float32
BF16 = jnp.bfloat16


def bits_of(size):
    return size.bit_length() - 1


def hop(value, axis, bit):
    size = lax.axis_size(axis)
    return lax.ppermute(value, axis, [(i, i ^ bit) for i in range(size)])


def unshuffle(blocks, axis_name):
    me = lax.axis_index(axis_name)
    blocks = list(blocks)
    for b in range(bits_of(len(blocks))):
        odd = ((me >> b) & 1) == 1
        blocks = [jnp.where(odd, blocks[i ^ (1 << b)], blocks[i]) for i in range(len(blocks))]
    return blocks


def take_clip(values, group):
    tm = lax.axis_size("tm")
    me = lax.axis_index("tm")
    out = []
    for d in range(tm):
        block = lax.dynamic_index_in_dim(values, group * tm + (me ^ d), 0, keepdims=False)
        out.append(hop(block, "tm", d) if d else block)
    return out


def give_back(parts):
    tm = lax.axis_size("tm")
    out = []
    for part in parts:
        blocks = jnp.split(part, tm, 0)
        blocks = [hop(block, "tm", d) if d else block for d, block in enumerate(blocks)]
        out.extend(unshuffle(blocks, "tm"))
    return jnp.stack(out)


def stages():
    clip_bits = [("clips", 1 << b) for b in range(bits_of(lax.axis_size("clips")))]
    time_bits = [("tm", 1 << b) for b in range(bits_of(lax.axis_size("tm")))]
    return clip_bits + time_bits


def scatter_sum(flat, order):
    for axis, bit in order:
        halves = flat.reshape((2, flat.shape[0] // 2) + flat.shape[1:])
        mine = (lax.axis_index(axis) // bit) % 2
        away = lax.dynamic_index_in_dim(halves, 1 - mine, 0, keepdims=False)
        kept = lax.dynamic_index_in_dim(halves, mine, 0, keepdims=False)
        flat = (kept.astype(F32) + hop(away, axis, bit).astype(F32)).astype(BF16)
    return flat


def gather_back(share, order):
    for axis, bit in reversed(order):
        other = hop(share, axis, bit)
        high = ((lax.axis_index(axis) // bit) % 2) == 1
        share = jnp.concatenate(
            [jnp.where(high, other, share), jnp.where(high, share, other)], 0
        )
    return share


def sum_all(flat):
    order = stages()
    first, rest = order[:1], order[1:]
    swapped = list(rest)
    if len(swapped) > 1:
        swapped[0], swapped[1] = swapped[1], swapped[0]
    half = scatter_sum(flat, first)
    cut = half.shape[0] // 2
    left = gather_back(scatter_sum(half[:cut], rest), rest)
    right = gather_back(scatter_sum(half[cut:], swapped), swapped)
    return gather_back(jnp.concatenate([left, right], 0), first)


def norm_forward(values, gains, shifts):
    centred = values - jnp.mean(values, -1, keepdims=True)
    spread = jnp.mean(centred * centred, -1, keepdims=True)
    inverse = lax.rsqrt(spread + NORM_EPS)
    unit = centred * inverse
    return (unit * gains + shifts, unit, inverse)


def norm_backward(grad_norm, unit, inverse, gains):
    scaled = grad_norm * gains
    return inverse * (
        scaled
        - jnp.mean(scaled, -1, keepdims=True)
        - unit * jnp.mean(scaled * unit, -1, keepdims=True)
    )


def dot(a, b):
    return jnp.dot(a, b, preferred_element_type=F32)


def dot_nt(a, b):
    return lax.dot_general(a, b, (((1,), (1,)), ((), ())), preferred_element_type=F32)


def dot_tn(a, b):
    return lax.dot_general(a, b, (((0,), (0,)), ((), ())), preferred_element_type=F32)


def heads_of(values):
    return values.reshape(values.shape[0], HEADS, values.shape[1] // HEADS)


def attend(queries, keys, values):
    scale = (queries.shape[1] // HEADS) ** (-0.5)
    scores = jnp.einsum("qhe,khe->hqk", heads_of(queries), heads_of(keys), preferred_element_type=F32) * scale
    peak = jnp.max(scores, -1, keepdims=True)
    raised = jnp.exp(scores - peak)
    total = jnp.sum(raised, -1, keepdims=True)
    probs = (raised / total).astype(BF16)
    mixed = jnp.einsum("hqk,khe->qhe", probs, heads_of(values), preferred_element_type=F32)
    return mixed.reshape(queries.shape).astype(BF16), peak + jnp.log(total)


def attend_back(queries, keys, values, grad_mix, log_sum):
    scale = (queries.shape[1] // HEADS) ** (-0.5)
    q, k, v, g = map(heads_of, (queries, keys, values, grad_mix))
    scores = jnp.einsum("qhe,khe->hqk", q, k, preferred_element_type=F32) * scale
    probs = jnp.exp(scores - log_sum)
    grad_probs = jnp.einsum("qhe,khe->hqk", g, v, preferred_element_type=F32)
    delta = jnp.sum(probs * grad_probs, -1, keepdims=True)
    grad_scores = (probs * (grad_probs - delta)).astype(BF16)
    grad_q = jnp.einsum("hqk,khe->qhe", grad_scores, k, preferred_element_type=F32) * scale
    grad_k = jnp.einsum("hqk,qhe->khe", grad_scores, q, preferred_element_type=F32) * scale
    grad_v = jnp.einsum("hqk,qhe->khe", probs.astype(BF16), g, preferred_element_type=F32)
    return tuple(x.reshape(queries.shape).astype(BF16) for x in (grad_q, grad_k, grad_v))


def on_device(
    patches, mask_index, mask_count, w_qkv, q_bias, v_bias, w_out, out_bias, w_up, up_bias,
    w_down, down_bias, norm1_scale, norm1_shift, norm2_scale, norm2_shift, mask_embed, pos_embed,
    cotangent,
):
    clip_count, seg, width = patches.shape
    ff = w_up.shape[1]
    tm = lax.axis_size("tm")
    me = lax.axis_index("tm")
    length = seg * tm
    groups = clip_count // tm
    q_bias, v_bias, out_bias, up_bias, down_bias = (
        x.astype(F32) for x in (q_bias, v_bias, out_bias, up_bias, down_bias)
    )
    gain1, shift1, gain2, shift2, embed = (
        x.astype(F32) for x in (norm1_scale, norm1_shift, norm2_scale, norm2_shift, mask_embed)
    )

    starts = (me ^ jnp.arange(tm, dtype=jnp.int32)) * seg
    places = (starts[:, None] + jnp.arange(seg, dtype=jnp.int32)[None, :]).reshape(length)
    pos = jnp.concatenate(
        [lax.dynamic_slice_in_dim(pos_embed, (me ^ d) * seg, seg, 0) for d in range(tm)], 0
    ).astype(F32)
    slots = jnp.arange(mask_index.shape[1], dtype=jnp.int32)

    parts = [take_clip(patches, g) for g in range(groups)]
    cots = [take_clip(cotangent, g) for g in range(groups)]

    saved = []
    for g in range(groups):
        index_row = lax.dynamic_index_in_dim(mask_index, g * tm + me, 0, keepdims=False)
        count = lax.dynamic_index_in_dim(mask_count, g * tm + me, 0, keepdims=False)
        live = slots < count
        masked = jnp.any((places[:, None] == index_row[None, :]) & live[None, :], axis=1)[:, None]
        filled = jnp.where(masked, embed[None, :], jnp.concatenate(parts[g], 0).astype(F32)) + pos
        normed_one, unit_one, inverse_one = norm_forward(filled, gain1, shift1)
        normed_one = normed_one.astype(BF16)
        joint = dot(normed_one, w_qkv)
        queries = (joint[:, :width] + q_bias).astype(BF16)
        keys = joint[:, width : 2 * width].astype(BF16)
        values = (joint[:, 2 * width :] + v_bias).astype(BF16)
        attended, log_sum = attend(queries, keys, values)
        hidden = filled + dot(attended, w_out) + out_bias
        normed_two, unit_two, inverse_two = norm_forward(hidden, gain2, shift2)
        normed_two = normed_two.astype(BF16)
        up_proj = dot(normed_two, w_up) + up_bias
        cumulative = 0.5 * (1.0 + lax.erf(up_proj * ROOT_HALF))
        activated = (up_proj * cumulative).astype(BF16)
        slope = cumulative + up_proj * jnp.exp(-0.5 * up_proj * up_proj) / ROOT_TWO_PI
        block_out = (hidden + dot(activated, w_down) + down_bias).astype(BF16)
        saved.append((masked, normed_one, unit_one, inverse_one, queries, keys, values, attended,
                      log_sum, normed_two, unit_two, inverse_two, activated, slope, block_out))
    (masked, normed_one, unit_one, inverse_one, queries, keys, values, attended, log_sum,
     normed_two, unit_two, inverse_two, activated, slope, block_out) = zip(*saved)
    block_out = give_back(block_out)

    cot = jnp.concatenate([jnp.concatenate(c, 0) for c in cots], 0)
    rows = lambda xs: jnp.concatenate(xs, 0)
    masked, normed_one, unit_one, inverse_one, attended, normed_two, unit_two, inverse_two, activated, slope = map(
        rows, (masked, normed_one, unit_one, inverse_one, attended, normed_two, unit_two, inverse_two, activated, slope))
    top = cot.astype(F32)
    grad_down = dot_tn(activated, cot).astype(BF16)
    grad_up_in = (dot_nt(cot, w_down) * slope).astype(BF16)
    grad_up = dot_tn(normed_two, grad_up_in).astype(BF16)
    flat_one = jnp.concatenate([grad_down] + jnp.split(grad_up, ff // width, 1), 0)
    sum_one = sum_all(flat_one)

    grad_norm_two = dot_nt(grad_up_in, w_up)
    grad_hidden = top + norm_backward(grad_norm_two, unit_two, inverse_two, gain2)
    branch = grad_hidden.astype(BF16)
    grad_out = dot_tn(attended, branch).astype(BF16)
    mix = dot_nt(branch, w_out).astype(BF16)
    back = [
        attend_back(queries[g], keys[g], values[g], mix[g * length : (g + 1) * length], log_sum[g])
        for g in range(groups)
    ]
    grad_joint = jnp.concatenate([jnp.concatenate(b, 1) for b in back], 0)
    grad_qkv = dot_tn(normed_one, grad_joint).astype(BF16)
    grad_norm_one = dot_nt(grad_joint, w_qkv)
    grad_filled = grad_hidden + norm_backward(grad_norm_one, unit_one, inverse_one, gain1)
    input_grad = jnp.where(masked, 0.0, grad_filled).astype(BF16)
    input_grad = give_back(jnp.split(input_grad, groups, 0))

    joint_sums = jnp.sum(grad_joint.astype(F32), 0)
    pos_sum = jnp.sum(grad_filled.reshape(groups, length, width), 0)
    pos_sum = jnp.concatenate(unshuffle(jnp.split(pos_sum, tm, 0), "tm"), 0)
    small = [
        joint_sums[:width],
        joint_sums[2 * width :],
        jnp.sum(branch.astype(F32), 0),
        jnp.sum(grad_up_in.astype(F32), 0),
        jnp.sum(top, 0),
        jnp.sum(grad_norm_one * unit_one, 0),
        jnp.sum(grad_norm_one, 0),
        jnp.sum(grad_norm_two * unit_two, 0),
        jnp.sum(grad_norm_two, 0),
        jnp.sum(jnp.where(masked, grad_filled, 0.0), 0),
    ]
    small = jnp.concatenate([x.reshape(-1, width) for x in small], 0)
    used = 4 * width + length + small.shape[0]
    devices = tm * lax.axis_size("clips")
    step = 8 * devices
    spare = -used % step
    flat_two = jnp.concatenate(
        [
            grad_out,
            *jnp.split(grad_qkv, 3, 1),
            pos_sum.astype(BF16),
            small.astype(BF16),
            jnp.zeros((spare, width), BF16),
        ],
        0,
    )
    sum_two = sum_all(flat_two).astype(F32)
    sum_one = sum_one.astype(F32)
    w_down_sum = sum_one[:ff]
    w_up_sum = jnp.concatenate(jnp.split(sum_one[ff:], ff // width, 0), 1)
    w_out_sum = sum_two[:width]
    w_qkv_sum = jnp.concatenate(jnp.split(sum_two[width : 4 * width], 3, 0), 1)
    at = 4 * width
    pos_total = sum_two[at : at + length]
    at += length
    vectors = []
    for n in (1, 1, 1, ff // width, 1, 1, 1, 1, 1, 1):
        vectors.append(sum_two[at : at + n].reshape(-1))
        at += n
    v = vectors
    return (block_out, input_grad, w_qkv_sum, v[0], v[1], w_out_sum, v[2], w_up_sum, v[3], w_down_sum, v[4],
            v[5], v[6], v[7], v[8], v[9], pos_total)


def solution(mesh):
    rows = P("clips", "tm", None)
    in_specs = (rows, P("clips", None), P("clips")) + (P(),) * 15 + (rows,)
    out_specs = (rows, rows) + (P(),) * 15
    return jax.shard_map(on_device, mesh=mesh, in_specs=in_specs, out_specs=out_specs, check_vma=False)
```

time: 1680 us -> 624 us (0.37)
  blocking collectives: 604 us -> 0 us
  waiting for transfers between devices: 648 us -> 145 us
  starting transfers between devices: 0.54 us -> 92.8 us
  local copies, waits for them, and re-layouts: 172 us -> 103 us
  other arithmetic: 61.9 us -> 126 us
  matrix products: 165 us -> 146 us
    unnamed x2 -> x0, blocking collectives: 523 us -> none
    reduce_scatter x2 -> x0, waiting for transfers between devices: 356 us -> none  [the longest x1 206 us: key_grads_summed(): lax.psum_scatter(grad_keys, 'tm', scatter_dimension=1, tiled=True)]
    all_gather x6 -> x0, waiting for transfers between devices: 291 us -> none  [the longest x1 107 us: gather_keys(): lax.all_gather(own_keys, 'tm', axis=1, tiled=True)]
    ppermute x0 -> x60, waiting for transfers between devices: none -> 145 us  [hop(): return lax.ppermute(value, axis, [(i, i ^ bit) for i in range(size)])]
    ppermute x0 -> x60, starting transfers between devices: none -> 92.8 us  [hop(): return lax.ppermute(value, axis, [(i, i ^ bit) for i in range(size)])]
    all_gather x1 -> x0, blocking collectives: 81.1 us -> none  [sum_everywhere(): lax.all_gather(share_pos.astype(jnp.bfloat16), ('clips', 'tm'), axis=0, t...]
    reshape x9 -> x13, local copies, waits for them, and re-layouts: 57.3 us -> 3.06 us  [the longest x10 2.36 us: on_device(): small = jnp.concatenate([x.reshape(-1, width) for x in small], 0)]
    concatenate x1 -> x2, local copies, waits for them, and re-layouts: 0.59 us -> 34.9 us  [the longest x1 34.8 us: on_device(): jnp.concatenate([grad_out, *jnp.split(grad_qkv, 3, 1), pos_sum.astype(BF1...]
  transfers between devices with their start and end apart: 8 -> 60, of which waited for: 6 -> 30; matrix products, arithmetic and copies ran while one was open for 8% -> 28% of each run, Pallas kernels for 0% -> 0%
where the time goes in v1:
time: 624 us; the launch traced here: 616 us
  matrix products  146 us (23%)
  waiting for transfers between devices  145 us (23%)
  other arithmetic  126 us (20%)
  local copies, waits for them, and re-layouts  103 us (17%)
  starting transfers between devices  92.8 us (15%)
    ppermute x60, waiting for transfers between devices, hop(): return lax.ppermute(value, axis, [(i, i ^ bit) for i in range(size)])  145 us
    ppermute x60, starting transfers between devices, hop(): return lax.ppermute(value, axis, [(i, i ^ bit) for i in range(size)])  92.8 us
    dot_general x4, matrix products, dot_tn(): lax.dot_general(a, b, (((0,), (0,)), ((), ())), preferred_element_type=F32)  42.2 us
    concatenate x1, local copies, waits for them, and re-layouts, on_device(): jnp.concatenate([grad_out, *jnp.split(grad_qkv, 3, 1), pos_sum.astype(BF1...  34.8 us
    dot_general x8, matrix products, dot(): return jnp.dot(a, b, preferred_element_type=F32)  31.7 us
    dot_general x4, matrix products, dot_nt(): lax.dot_general(a, b, (((1,), (1,)), ((), ())), preferred_element_type=F32)  27 us
    unnamed x297, local copies, waits for them, and re-layouts  25.5 us
    dot_general x2, matrix products, attend_back(): grad_probs = jnp.einsum('qhe,khe->hqk', g, v, preferred_element_type=F32)  16.9 us
  transfers between devices with their start and end apart: 60, of which 30 were waited for; matrix products, arithmetic and copies ran while one was open for 28% of the time, Pallas kernels for 0%

profile of v1, /device:TPU:0, one launch (start us, length us, event | category | flops | bytes accessed | tf_op | source)
XLA Modules:
  0.0 616.1 jit_solution(18084840113402631827)
XLA Ops:
  3.4 3.0 collective-permute-start
  10.0 3.5 collective-permute-start.7
  17.2 3.0 collective-permute-start.8
  34.7 3.1 dynamic-slice_reduce_fusion.1
  39.4 3.0 collective-permute-start.14
  43.0 14.1 %collective-permute-start.16 = (bf16[128,768]{1,0:T(8,128)(2,1)}, bf16[128,768]{1,0:T(8,128)(2,1)}, u32[]{:S(2)}, u32[]{:S(2)}) collective-permute-start(bf16[128,768]{1,0:T(8,128)(2,1)} %get-tuple-element.88), channel_id=1, source_target_pairs={{0,2},{1,3},{2,0},{3,1},{4,6},{5,7},{6,4},{7,5},{8,10},{9,11},{10,... | collective-permute-start | bytes 589832 | tf_op jit(solution)/shard_map/ppermute | solution.py:20
  57.1 3.4 fusion.68
  64.1 3.4 add_convert_fusion.2
  69.7 3.6 add_convert_fusion.5
  86.2 3.2 multiply_reduce_fusion.3
  94.1 3.0 fusion.64
  108.0 3.2 multiply_reduce_fusion.2
  123.9 5.4 fusion.111
  129.3 10.4 %fusion.13 = (f32[512,3072]{1,0:T(8,128)}, bf16[512,3072]{1,0:T(8,128)(2,1)}, bf16[512,3072]{1,0:T(8,128)(2,1)}, f32[512,3072]{1,0:T(8,128)}) fusion(f32[3072]{0:T(1024)S(1)} %copy-done.107, f32[512,3072]{1,0:T(8,128)S(1)} %fusion.111, bf16[512,768]{1,0:T(8,128)(2,1)S(1)} %get-tuple-element.165, bf16[768,3072]{1,0:T(8,128)(2,1)S(1)} %bitcast.303), kind=kOutput, calls=%fused_computation.29 | convolution fusion | flops 2450522112 | bytes 30683136 | tf_op jit(solution)/shard_map/dot_general | solution.py:109
  149.6 11.6 %fusion.108 = (bf16[3072]{0:T(1024)(128)(2,1)}, bf16[1024,3072]{1,0:T(8,128)(2,1)}) fusion(f32[512,3072]{1,0:T(8,128)} %get-tuple-element.162, f32[512,3072]{1,0:T(8,128)} %get-tuple-element.62, bf16[1024,768]{1,0:T(8,128)(2,1)S(1)} %get-tuple-element.158, bf16[3072,768]{1,0:T(8,128)(2,1)} %param.29), kind=kOutput, calls=%fused_computation.368 | convolution fusion | flops 4844418048 | bytes 25171968 | tf_op jit(solution)/shard_map/dot_general | solution.py:113
  161.2 8.1 %multiply_reduce_fusion.4 = (bf16[768]{0:T(1024)(128)(2,1)S(1)}, f32[1024]{0:T(1024)S(1)}, f32[1024]{0:T(1024)S(1)}, bf16[768]{0:T(1024)(128)(2,1)S(1)}, f32[1024,768]{1,0:T(8,128)S(1)}) fusion(f32[512,768]{1,0:T(8,128)S(1)} %get-tuple-element.45, f32[512,768]{1,0:T(8,128)S(1)} %get-tuple-element.166, f32[768]{0:T(1024)S(1)} %convert_element_type.442, ...), kind=kOutput, calls=%fused_computation.65 | convolution fusion | flops 4838125568 | bytes 17315840 | tf_op jit(solution)/shard_map/dot_general | solution.py:113
  175.4 6.1 multiply_reduce_fusion.1
  181.5 6.9 %multiply_convert_fusion.1 = bf16[12,512,512]{1,2,0:T(8,128)(2,1)S(1)} fusion(f32[12,512,512]{1,2,0:T(8,128)} %get-tuple-element.183, f32[12,512,512]{1,2,0:T(8,128)S(1)} %bitcast.260, f32[12,512]{1,0:T(8,128)S(1)} %get-tuple-element.182, f32[12,512]{1,0:T(8,128)S(1)} %log_add_fusion.1), kind=kLoop, calls=%fused_computation.5 | loop fusion | flops 15728640 | bytes 31506432 | tf_op jit(solution)/shard_map/convert_element_type | solution.py:142
  190.6 2.9 multiply_convert_fusion.6
  193.5 3.2 fusion.57
  196.8 10.8 %multiply_reduce_fusion = (f32[12,512]{1,0:T(8,128)S(1)}, f32[12,512,512]{1,2,0:T(8,128)}) fusion(f32[12,512,512]{1,2,0:T(8,128)} %copy-done.3, f32[12,512]{1,0:T(8,128)S(1)} %log_add_fusion, bf16[512,12,64]{0,2,1:T(8,128)(2,1)S(1)} %bitcast.278, bf16[512,12,64]{0,2,1:T(8,128)(2,1)S(1)} %bitcast.307), kind=kOutput, calls=%fused_computation.3 | convolution fusion | flops 415229952 | bytes 26787840 | tf_op jit(solution)/shard_map/qhe,khe->hqk/dot_general | solution.py:140
  209.4 6.9 %multiply_convert_fusion = bf16[12,512,512]{1,2,0:T(8,128)(2,1)S(1)} fusion(f32[12,512,512]{1,2,0:T(8,128)} %get-tuple-element.181, f32[12,512,512]{1,2,0:T(8,128)S(1)} %bitcast.262, f32[12,512]{1,0:T(8,128)S(1)} %get-tuple-element.180, f32[12,512]{1,0:T(8,128)S(1)} %log_add_fusion), kind=kLoop, calls=%fused_computation.2 | loop fusion | flops 15728640 | bytes 31506432 | tf_op jit(solution)/shard_map/convert_element_type | solution.py:142
  226.5 20.8 %convolution_convert_fusion.1 = bf16[768,2304]{1,0:T(8,128)(2,1)S(1)} fusion(bf16[512,768]{1,0:T(8,128)(2,1)S(1)} %copy-done.76, bf16[512,768]{1,0:T(8,128)(2,1)S(1)} %copy-done.78, bf16[512,768]{0,1:T(8,128)(2,1)} %bitcast.312, bf16[512,768]{0,1:T(8,128)(2,1)S(1)} %bitcast.319, bf16[512,768]{0,1:T(8,128)(2,1)S(1)} %bitcast.290, ...), kind=kOutput, calls=%fused_computation.54 | convolution fusion | flops 3657105408 | bytes 9830400 | tf_op jit(solution)/shard_map/dot_general | solution.py:117
  247.3 3.7 fusion.52
  250.9 9.9 %convolution_convert_fusion = bf16[768,3072]{1,0:T(8,128)(2,1)} fusion(bf16[1024,3072]{1,0:T(8,128)(2,1)} %get-tuple-element.186, bf16[512,768]{1,0:T(8,128)(2,1)S(1)} %copy-done.64, bf16[512,768]{1,0:T(8,128)(2,1)S(1)} %copy-done.80), kind=kOutput, calls=%fused_computation.51 | convolution fusion | flops 4837343232 | bytes 12582912 | tf_op jit(solution)/shard_map/dot_general | solution.py:117
  264.3 5.8 multiply_reduce_fusion.5
  278.0 34.8 %concatenate.131 = bf16[3840,768]{1,0:T(8,128)(2,1)} concatenate(bf16[768,768]{1,0:T(8,128)(2,1)} %fusion.52, bf16[768,768]{1,0:T(8,128)(2,1)} %get-tuple-element.76, bf16[768,768]{1,0:T(8,128)(2,1)} %get-tuple-element.75, bf16[768,768]{1,0:T(8,128)(2,1)} %get-tuple-element.74, bf16[128,768]{1,0:T(8,128)(2,1)} %get-tuple-element.114, bf16[128,768]{1,0:T(8,128)(2,1)} %get-tuple-element.115, ...), dimensions={0} | concatenate | bytes 11796480 | tf_op jit(solution)/shard_map/concatenate | solution.py:252
  315.2 7.8 %fusion.32 = bf16[6144,768]{1,0:T(8,128)(2,1)S(1)} fusion(bf16[1024,768]{1,0:T(8,128)(2,1)S(1)} %copy-done.73, bf16[512,3072]{1,0:T(8,128)(2,1)} %get-tuple-element.161, bf16[512,3072]{1,0:T(8,128)(2,1)} %get-tuple-element.63), kind=kOutput, calls=%fused_computation.53 | convolution fusion | flops 4846780416 | bytes 12582912 | tf_op jit(solution)/shard_map/dot_general | solution.py:117
  326.1 3.8 copy-done.18
  330.1 4.5 add_convert_fusion.3
  334.7 3.5 collective-permute-start.3
  345.8 3.5 collective-permute-start.18
  349.3 13.9 %collective-permute-done.4 = bf16[128,768]{1,0:T(8,128)(2,1)S(1)} collective-permute-done((bf16[128,768]{1,0:T(8,128)(2,1)S(1)}, bf16[128,768]{1,0:T(8,128)(2,1)S(1)}, u32[]{:S(2)}, u32[]{:S(2)}) %collective-permute-start.4) | collective-permute-done | bytes 196640 | tf_op jit(solution)/shard_map/ppermute | solution.py:20
  368.2 2.9 collective-permute-done.19
  373.8 8.2 %collective-permute-done.25 = bf16[480,768]{1,0:T(8,128)(2,1)S(1)} collective-permute-done((bf16[480,768]{1,0:T(8,128)(2,1)S(1)}, bf16[480,768]{1,0:T(8,128)(2,1)S(1)}, u32[]{:S(2)}, u32[]{:S(2)}) %collective-permute-start.25) | collective-permute-done | bytes 737312 | tf_op jit(solution)/shard_map/ppermute | solution.py:20
  386.4 4.9 collective-permute-done.26
  394.1 4.7 collective-permute-done.27
  404.6 5.1 collective-permute-done.28
  412.9 3.5 collective-permute-done.29
  417.1 5.0 fusion.3
  432.3 19.2 %collective-permute-done.43 = bf16[768,768]{1,0:T(8,128)(2,1)S(1)} collective-permute-done((bf16[768,768]{1,0:T(8,128)(2,1)S(1)}, bf16[768,768]{1,0:T(8,128)(2,1)S(1)}, u32[]{:S(2)}, u32[]{:S(2)}) %collective-permute-start.43) | collective-permute-done | bytes 1179680 | tf_op jit(solution)/shard_map/ppermute | solution.py:20
  454.1 3.5 collective-permute-done.31
  459.6 4.3 collective-permute-done.44
  465.5 6.1 collective-permute-done.52
  473.6 3.6 collective-permute-start.46
  477.2 6.1 collective-permute-done.53
  483.5 3.0 collective-permute-start.47
  486.5 4.4 collective-permute-done.54
  493.9 4.0 collective-permute-done.55
  498.0 3.0 collective-permute-done.48
  507.1 10.4 %collective-permute-done.49 = bf16[384,768]{1,0:T(8,128)(2,1)S(1)} collective-permute-done((bf16[384,768]{1,0:T(8,128)(2,1)S(1)}, bf16[384,768]{1,0:T(8,128)(2,1)S(1)}, u32[]{:S(2)}, u32[]{:S(2)}) %collective-permute-start.49) | collective-permute-done | bytes 589856 | tf_op jit(solution)/shard_map/ppermute | solution.py:20
  524.0 6.0 collective-permute-done.40
  530.0 3.4 collective-permute-start.9
  534.6 8.0 %collective-permute-done.58 = bf16[768,768]{1,0:T(8,128)(2,1)S(1)} collective-permute-done((bf16[768,768]{1,0:T(8,128)(2,1)S(1)}, bf16[768,768]{1,0:T(8,128)(2,1)S(1)}, u32[]{:S(2)}, u32[]{:S(2)}) %collective-permute-start.58) | collective-permute-done | bytes 1179680 | tf_op jit(solution)/shard_map/ppermute | solution.py:20
  546.8 3.4 collective-permute-start.21
  552.9 3.5 collective-permute-done.21
  556.5 11.9 %collective-permute-done.22 = bf16[128,768]{1,0:T(8,128)(2,1)S(1)} collective-permute-done((bf16[128,768]{1,0:T(8,128)(2,1)S(1)}, bf16[128,768]{1,0:T(8,128)(2,1)S(1)}, u32[]{:S(2)}, u32[]{:S(2)}) %collective-permute-start.22) | collective-permute-done | bytes 196640 | tf_op jit(solution)/shard_map/ppermute | solution.py:20
  580.9 5.3 maximum_convert_fusion
  586.2 6.1 fusion.90
  592.3 3.8 pad_maximum_fusion.1
  597.2 4.1 broadcast_select_fusion.1
  601.4 4.5 fusion.35
  605.8 5.7 maximum_convert_fusion.4
  611.6 4.2 pad_maximum_fusion
  (577 shorter events, 206.7 us)
Async XLA Ops:
  0.7 66.9 %copy-start = (bf16[768,2304]{1,0:T(8,128)(2,1)S(1)}, bf16[768,2304]{1,0:T(8,128)(2,1)}, u32[]{:S(2)}) copy-start(bf16[768,2304]{1,0:T(8,128)(2,1)} %param.22) | copy-start | bytes 10616836
  3.4 13.7 %collective-permute-start = (bf16[128,768]{1,0:T(8,128)(2,1)S(1)}, bf16[128,768]{1,0:T(8,128)(2,1)}, u32[]{:S(2)}, u32[]{:S(2)}) collective-permute-start(bf16[128,768]{1,0:T(8,128)(2,1)S(1)} %get-tuple-element.102), channel_id=1, source_target_pairs={{0,1},{1,0},{2,3},{3,2},{4,5},{5,4},{6,7},{7,6},{8,9},{9,8},{10,11... | collective-permute-start | bytes 589832 | tf_op jit(solution)/shard_map/ppermute | solution.py:20
  6.5 31.4 %collective-permute-start.1 = (bf16[128,768]{1,0:T(8,128)(2,1)}, bf16[128,768]{1,0:T(8,128)(2,1)}, u32[]{:S(2)}, u32[]{:S(2)}) collective-permute-start(bf16[128,768]{1,0:T(8,128)(2,1)} %get-tuple-element.101), channel_id=1, source_target_pairs={{0,2},{1,3},{2,0},{3,1},{4,6},{5,7},{6,4},{7,5},{8,10},{9,11},{10,... | collective-permute-start | bytes 589832 | tf_op jit(solution)/shard_map/ppermute | solution.py:20
  9.1 28.9 %collective-permute-start.2 = (bf16[128,768]{1,0:T(8,128)(2,1)}, bf16[128,768]{1,0:T(8,128)(2,1)}, u32[]{:S(2)}, u32[]{:S(2)}) collective-permute-start(bf16[128,768]{1,0:T(8,128)(2,1)} %get-tuple-element.100), channel_id=1, source_target_pairs={{0,3},{1,2},{2,1},{3,0},{4,7},{5,6},{6,5},{7,4},{8,11},{9,10},{10,... | collective-permute-start | bytes 589832 | tf_op jit(solution)/shard_map/ppermute | solution.py:20
  9.1 30.3 %collective-permute-start.6 = (bf16[128,768]{1,0:T(8,128)(2,1)}, bf16[128,768]{1,0:T(8,128)(2,1)}, u32[]{:S(2)}, u32[]{:S(2)}) collective-permute-start(bf16[128,768]{1,0:T(8,128)(2,1)} %get-tuple-element.98), channel_id=1, source_target_pairs={{0,1},{1,0},{2,3},{3,2},{4,5},{5,4},{6,7},{7,6},{8,9},{9,8},{10,11... | collective-permute-start | bytes 589832 | tf_op jit(solution)/shard_map/ppermute | solution.py:20
  10.0 32.4 %collective-permute-start.7 = (bf16[128,768]{1,0:T(8,128)(2,1)}, bf16[128,768]{1,0:T(8,128)(2,1)}, u32[]{:S(2)}, u32[]{:S(2)}) collective-permute-start(bf16[128,768]{1,0:T(8,128)(2,1)} %get-tuple-element.104), channel_id=1, source_target_pairs={{0,2},{1,3},{2,0},{3,1},{4,6},{5,7},{6,4},{7,5},{8,10},{9,11},{10,... | collective-permute-start | bytes 589832 | tf_op jit(solution)/shard_map/ppermute | solution.py:20
  17.2 25.8 %collective-permute-start.8 = (bf16[128,768]{1,0:T(8,128)(2,1)}, bf16[128,768]{1,0:T(8,128)(2,1)}, u32[]{:S(2)}, u32[]{:S(2)}) collective-permute-start(bf16[128,768]{1,0:T(8,128)(2,1)} %get-tuple-element.103), channel_id=1, source_target_pairs={{0,3},{1,2},{2,1},{3,0},{4,7},{5,6},{6,5},{7,4},{8,11},{9,10},{10,... | collective-permute-start | bytes 589832 | tf_op jit(solution)/shard_map/ppermute | solution.py:20
  21.7 47.8 %copy-start.93 = (f32[768]{0:T(1024)}, f32[768]{0:T(1024)S(1)}, u32[]{:S(2)}) copy-start(f32[768]{0:T(1024)S(1)} %convert_element_type.430) | copy-start | bytes 9220
  37.8 31.8 %copy-start.23 = (bf16[128,768]{1,0:T(8,128)(2,1)}, bf16[128,768]{1,0:T(8,128)(2,1)S(1)}, u32[]{:S(2)}) copy-start(bf16[128,768]{1,0:T(8,128)(2,1)S(1)} %get-tuple-element.123) | copy-start | bytes 589828
  37.9 101.9 %collective-permute-start.12 = (bf16[128,768]{1,0:T(8,128)(2,1)}, bf16[128,768]{1,0:T(8,128)(2,1)}, u32[]{:S(2)}, u32[]{:S(2)}) collective-permute-start(bf16[128,768]{1,0:T(8,128)(2,1)} %get-tuple-element.86), channel_id=1, source_target_pairs={{0,1},{1,0},{2,3},{3,2},{4,5},{5,4},{6,7},{7,6},{8,9},{9,8},{10,11... | collective-permute-start | bytes 589832 | tf_op jit(solution)/shard_map/ppermute | solution.py:20
  38.0 103.8 %collective-permute-start.13 = (bf16[128,768]{1,0:T(8,128)(2,1)}, bf16[128,768]{1,0:T(8,128)(2,1)}, u32[]{:S(2)}, u32[]{:S(2)}) collective-permute-start(bf16[128,768]{1,0:T(8,128)(2,1)} %get-tuple-element.85), channel_id=1, source_target_pairs={{0,2},{1,3},{2,0},{3,1},{4,6},{5,7},{6,4},{7,5},{8,10},{9,11},{10,... | collective-permute-start | bytes 589832 | tf_op jit(solution)/shard_map/ppermute | solution.py:20
  39.4 103.9 %collective-permute-start.14 = (bf16[128,768]{1,0:T(8,128)(2,1)}, bf16[128,768]{1,0:T(8,128)(2,1)}, u32[]{:S(2)}, u32[]{:S(2)}) collective-permute-start(bf16[128,768]{1,0:T(8,128)(2,1)} %get-tuple-element.84), channel_id=1, source_target_pairs={{0,3},{1,2},{2,1},{3,0},{4,7},{5,6},{6,5},{7,4},{8,11},{9,10},{10,... | collective-permute-start | bytes 589832 | tf_op jit(solution)/shard_map/ppermute | solution.py:20
  42.3 103.5 %collective-permute-start.15 = (bf16[128,768]{1,0:T(8,128)(2,1)}, bf16[128,768]{1,0:T(8,128)(2,1)}, u32[]{:S(2)}, u32[]{:S(2)}) collective-permute-start(bf16[128,768]{1,0:T(8,128)(2,1)} %get-tuple-element.83), channel_id=1, source_target_pairs={{0,1},{1,0},{2,3},{3,2},{4,5},{5,4},{6,7},{7,6},{8,9},{9,8},{10,11... | collective-permute-start | bytes 589832 | tf_op jit(solution)/shard_map/ppermute | solution.py:20
  43.0 104.4 %collective-permute-start.16 = (bf16[128,768]{1,0:T(8,128)(2,1)}, bf16[128,768]{1,0:T(8,128)(2,1)}, u32[]{:S(2)}, u32[]{:S(2)}) collective-permute-start(bf16[128,768]{1,0:T(8,128)(2,1)} %get-tuple-element.88), channel_id=1, source_target_pairs={{0,2},{1,3},{2,0},{3,1},{4,6},{5,7},{6,4},{7,5},{8,10},{9,11},{10,... | collective-permute-start | bytes 589832 | tf_op jit(solution)/shard_map/ppermute | solution.py:20
  139.8 9.2 %collective-permute-start.17 = (bf16[128,768]{1,0:T(8,128)(2,1)S(1)}, bf16[128,768]{1,0:T(8,128)(2,1)S(1)}, u32[]{:S(2)}, u32[]{:S(2)}) collective-permute-start(bf16[128,768]{1,0:T(8,128)(2,1)S(1)} %copy-done.88), channel_id=1, source_target_pairs={{0,3},{1,2},{2,1},{3,0},{4,7},{5,6},{6,5},{7,4},{8,11},{9,10},{10,... | collective-permute-start | bytes 589832 | tf_op jit(solution)/shard_map/ppermute | solution.py:20
  315.1 48.4 %collective-permute-start.24 = (bf16[1920,768]{1,0:T(8,128)(2,1)S(1)}, bf16[1920,768]{1,0:T(8,128)(2,1)S(1)}, u32[]{:S(2)}, u32[]{:S(2)}) collective-permute-start(bf16[1920,768]{1,0:T(8,128)(2,1)S(1)} %dynamic-slice_bitcast_fusion.1), channel_id=1, source_target_pairs={{0,4},{4,0},{8,12},{12,8},{16,20},{20,16},{24,28},{28,24},{1,5},{5... | collective-permute-start | bytes 8847368 | tf_op jit(solution)/shard_map/ppermute | solution.py:20
  329.9 87.2 %collective-permute-start.42 = (bf16[3072,768]{1,0:T(8,128)(2,1)}, bf16[3072,768]{1,0:T(8,128)(2,1)}, u32[]{:S(2)}, u32[]{:S(2)}) collective-permute-start(bf16[3072,768]{1,0:T(8,128)(2,1)} %dynamic-slice_bitcast_fusion), channel_id=1, source_target_pairs={{0,4},{4,0},{8,12},{12,8},{16,20},{20,16},{24,28},{28,24},{1,5},{5... | collective-permute-start | bytes 14155784 | tf_op jit(solution)/shard_map/ppermute | solution.py:20
  334.7 11.1 %collective-permute-start.3 = (bf16[128,768]{1,0:T(8,128)(2,1)S(1)}, bf16[128,768]{1,0:T(8,128)(2,1)S(1)}, u32[]{:S(2)}, u32[]{:S(2)}) collective-permute-start(bf16[128,768]{1,0:T(8,128)(2,1)S(1)} %get-tuple-element.122), channel_id=1, source_target_pairs={{0,3},{1,2},{2,1},{3,0},{4,7},{5,6},{6,5},{7,4},{8,11},{9,10},{10,... | collective-permute-start | bytes 589832 | tf_op jit(solution)/shard_map/ppermute | solution.py:20
  338.2 25.0 %collective-permute-start.4 = (bf16[128,768]{1,0:T(8,128)(2,1)S(1)}, bf16[128,768]{1,0:T(8,128)(2,1)S(1)}, u32[]{:S(2)}, u32[]{:S(2)}) collective-permute-start(bf16[128,768]{1,0:T(8,128)(2,1)S(1)} %get-tuple-element.121), channel_id=1, source_target_pairs={{0,2},{1,3},{2,0},{3,1},{4,6},{5,7},{6,4},{7,5},{8,10},{9,11},{10,... | collective-permute-start | bytes 589832 | tf_op jit(solution)/shard_map/ppermute | solution.py:20
  338.2 25.0 %collective-permute-start.5 = (bf16[128,768]{1,0:T(8,128)(2,1)S(1)}, bf16[128,768]{1,0:T(8,128)(2,1)S(1)}, u32[]{:S(2)}, u32[]{:S(2)}) collective-permute-start(bf16[128,768]{1,0:T(8,128)(2,1)S(1)} %get-tuple-element.120), channel_id=1, source_target_pairs={{0,1},{1,0},{2,3},{3,2},{4,5},{5,4},{6,7},{7,6},{8,9},{9,8},{10,11... | collective-permute-start | bytes 589832 | tf_op jit(solution)/shard_map/ppermute | solution.py:20
  339.4 46.2 %copy-start.6 = (bf16[1024,768]{1,0:T(8,128)(2,1)}, bf16[1024,768]{1,0:T(8,128)(2,1)S(1)}, u32[]{:S(2)}) copy-start(bf16[1024,768]{1,0:T(8,128)(2,1)S(1)} %select_convert_fusion) | copy-start | bytes 4718596
  345.8 20.6 %collective-permute-start.18 = (bf16[128,768]{1,0:T(8,128)(2,1)S(1)}, bf16[128,768]{1,0:T(8,128)(2,1)S(1)}, u32[]{:S(2)}, u32[]{:S(2)}) collective-permute-start(bf16[128,768]{1,0:T(8,128)(2,1)S(1)} %get-tuple-element.94), channel_id=1, source_target_pairs={{0,3},{1,2},{2,1},{3,0},{4,7},{5,6},{6,5},{7,4},{8,11},{9,10},{10,... | collective-permute-start | bytes 589832 | tf_op jit(solution)/shard_map/ppermute | solution.py:20
  363.2 7.9 %collective-permute-start.19 = (bf16[128,768]{1,0:T(8,128)(2,1)S(1)}, bf16[128,768]{1,0:T(8,128)(2,1)S(1)}, u32[]{:S(2)}, u32[]{:S(2)}) collective-permute-start(bf16[128,768]{1,0:T(8,128)(2,1)S(1)} %get-tuple-element.93), channel_id=1, source_target_pairs={{0,2},{1,3},{2,0},{3,1},{4,6},{5,7},{6,4},{7,5},{8,10},{9,11},{10,... | collective-permute-start | bytes 589832 | tf_op jit(solution)/shard_map/ppermute | solution.py:20
  363.2 9.8 %collective-permute-start.20 = (bf16[128,768]{1,0:T(8,128)(2,1)S(1)}, bf16[128,768]{1,0:T(8,128)(2,1)S(1)}, u32[]{:S(2)}, u32[]{:S(2)}) collective-permute-start(bf16[128,768]{1,0:T(8,128)(2,1)S(1)} %get-tuple-element.92), channel_id=1, source_target_pairs={{0,1},{1,0},{2,3},{3,2},{4,5},{5,4},{6,7},{7,6},{8,9},{9,8},{10,11... | collective-permute-start | bytes 589832 | tf_op jit(solution)/shard_map/ppermute | solution.py:20
  364.7 17.3 %collective-permute-start.25 = (bf16[480,768]{1,0:T(8,128)(2,1)S(1)}, bf16[480,768]{1,0:T(8,128)(2,1)S(1)}, u32[]{:S(2)}, u32[]{:S(2)}) collective-permute-start(bf16[480,768]{1,0:T(8,128)(2,1)S(1)} %dynamic-slice_bitcast_fusion.5), channel_id=1, source_target_pairs={{0,8},{4,12},{8,0},{12,4},{16,24},{20,28},{24,16},{28,20},{1,9},{5... | collective-permute-start | bytes 2211848 | tf_op jit(solution)/shard_map/ppermute | solution.py:20
  366.5 17.5 %collective-permute-start.33 = (bf16[480,768]{1,0:T(8,128)(2,1)S(1)}, bf16[480,768]{1,0:T(8,128)(2,1)S(1)}, u32[]{:S(2)}, u32[]{:S(2)}) collective-permute-start(bf16[480,768]{1,0:T(8,128)(2,1)S(1)} %dynamic-slice_bitcast_fusion.4), channel_id=1, source_target_pairs={{0,16},{4,20},{8,24},{12,28},{16,0},{20,4},{24,8},{28,12},{1,17},{... | collective-permute-start | bytes 2211848 | tf_op jit(solution)/shard_map/ppermute | solution.py:20
  371.1 175.7 %collective-permute-start.10 = (bf16[128,768]{1,0:T(8,128)(2,1)}, bf16[128,768]{1,0:T(8,128)(2,1)}, u32[]{:S(2)}, u32[]{:S(2)}) collective-permute-start(bf16[128,768]{1,0:T(8,128)(2,1)} %get-tuple-element.118), channel_id=1, source_target_pairs={{0,2},{1,3},{2,0},{3,1},{4,6},{5,7},{6,4},{7,5},{8,10},{9,11},{10,... | collective-permute-start | bytes 589832 | tf_op jit(solution)/shard_map/ppermute | solution.py:20
  382.2 9.1 %collective-permute-start.26 = (bf16[240,768]{1,0:T(8,128)(2,1)S(1)}, bf16[240,768]{1,0:T(8,128)(2,1)S(1)}, u32[]{:S(2)}, u32[]{:S(2)}) collective-permute-start(bf16[240,768]{1,0:T(8,128)(2,1)S(1)} %dynamic-slice_bitcast_fusion.9), channel_id=1, source_target_pairs={{0,16},{4,20},{8,24},{12,28},{16,0},{20,4},{24,8},{28,12},{1,17},{... | collective-permute-start | bytes 1105928 | tf_op jit(solution)/shard_map/ppermute | solution.py:20
  384.2 9.1 %collective-permute-start.34 = (bf16[240,768]{1,0:T(8,128)(2,1)S(1)}, bf16[240,768]{1,0:T(8,128)(2,1)S(1)}, u32[]{:S(2)}, u32[]{:S(2)}) collective-permute-start(bf16[240,768]{1,0:T(8,128)(2,1)S(1)} %dynamic-slice_bitcast_fusion.8), channel_id=1, source_target_pairs={{0,8},{4,12},{8,0},{12,4},{16,24},{20,28},{24,16},{28,20},{1,9},{5... | collective-permute-start | bytes 1105928 | tf_op jit(solution)/shard_map/ppermute | solution.py:20
  391.5 7.3 %collective-permute-start.27 = (bf16[120,768]{1,0:T(8,128)(2,1)S(1)}, bf16[120,768]{1,0:T(8,128)(2,1)S(1)}, u32[]{:S(2)}, u32[]{:S(2)}) collective-permute-start(bf16[120,768]{1,0:T(8,128)(2,1)S(1)} %dynamic-slice_bitcast_fusion.27), channel_id=1, source_target_pairs={{0,1},{1,0},{2,3},{3,2},{4,5},{5,4},{6,7},{7,6},{8,9},{9,8},{10,11... | collective-permute-start | bytes 552968 | tf_op jit(solution)/shard_map/ppermute | solution.py:20
  393.4 8.4 %collective-permute-start.35 = (bf16[120,768]{1,0:T(8,128)(2,1)S(1)}, bf16[120,768]{1,0:T(8,128)(2,1)S(1)}, u32[]{:S(2)}, u32[]{:S(2)}) collective-permute-start(bf16[120,768]{1,0:T(8,128)(2,1)S(1)} %dynamic-slice_bitcast_fusion.26), channel_id=1, source_target_pairs={{0,1},{1,0},{2,3},{3,2},{4,5},{5,4},{6,7},{7,6},{8,9},{9,8},{10,11... | collective-permute-start | bytes 552968 | tf_op jit(solution)/shard_map/ppermute | solution.py:20
  398.9 10.9 %collective-permute-start.28 = (bf16[60,768]{1,0:T(8,128)(2,1)S(1)}, bf16[60,768]{1,0:T(8,128)(2,1)S(1)}, u32[]{:S(2)}, u32[]{:S(2)}) collective-permute-start(bf16[60,768]{1,0:T(8,128)(2,1)S(1)} %dynamic-slice_bitcast_fusion.31), channel_id=1, source_target_pairs={{0,2},{1,3},{2,0},{3,1},{4,6},{5,7},{6,4},{7,5},{8,10},{9,11},{10,... | collective-permute-start | bytes 276488 | tf_op jit(solution)/shard_map/ppermute | solution.py:20
  401.9 9.6 %collective-permute-start.36 = (bf16[60,768]{1,0:T(8,128)(2,1)S(1)}, bf16[60,768]{1,0:T(8,128)(2,1)S(1)}, u32[]{:S(2)}, u32[]{:S(2)}) collective-permute-start(bf16[60,768]{1,0:T(8,128)(2,1)S(1)} %dynamic-slice_bitcast_fusion.30), channel_id=1, source_target_pairs={{0,2},{1,3},{2,0},{3,1},{4,6},{5,7},{6,4},{7,5},{8,10},{9,11},{10,... | collective-permute-start | bytes 276488 | tf_op jit(solution)/shard_map/ppermute | solution.py:20
  409.8 6.6 %collective-permute-start.29 = (bf16[60,768]{1,0:T(8,128)(2,1)S(1)}, bf16[60,768]{1,0:T(8,128)(2,1)S(1)}, u32[]{:S(2)}, u32[]{:S(2)}) collective-permute-start(bf16[60,768]{1,0:T(8,128)(2,1)S(1)} %fusion.78), channel_id=1, source_target_pairs={{0,2},{1,3},{2,0},{3,1},{4,6},{5,7},{6,4},{7,5},{8,10},{9,11},{10,... | collective-permute-start | bytes 276488 | tf_op jit(solution)/shard_map/ppermute | solution.py:20
  411.6 11.0 %collective-permute-start.37 = (bf16[60,768]{1,0:T(8,128)(2,1)S(1)}, bf16[60,768]{1,0:T(8,128)(2,1)S(1)}, u32[]{:S(2)}, u32[]{:S(2)}) collective-permute-start(bf16[60,768]{1,0:T(8,128)(2,1)S(1)} %fusion.77), channel_id=1, source_target_pairs={{0,2},{1,3},{2,0},{3,1},{4,6},{5,7},{6,4},{7,5},{8,10},{9,11},{10,... | collective-permute-start | bytes 276488 | tf_op jit(solution)/shard_map/ppermute | solution.py:20
  416.5 9.9 %collective-permute-start.30 = (bf16[120,768]{1,0:T(8,128)(2,1)S(1)}, bf16[120,768]{1,0:T(8,128)(2,1)S(1)}, u32[]{:S(2)}, u32[]{:S(2)}) collective-permute-start(bf16[120,768]{1,0:T(8,128)(2,1)S(1)} %pad_maximum_fusion.20), channel_id=1, source_target_pairs={{0,1},{1,0},{2,3},{3,2},{4,5},{5,4},{6,7},{7,6},{8,9},{9,8},{10,11... | collective-permute-start | bytes 552968 | tf_op jit(solution)/shard_map/ppermute | solution.py:20
  422.5 29.0 %collective-permute-start.43 = (bf16[768,768]{1,0:T(8,128)(2,1)S(1)}, bf16[768,768]{1,0:T(8,128)(2,1)S(1)}, u32[]{:S(2)}, u32[]{:S(2)}) collective-permute-start(bf16[768,768]{1,0:T(8,128)(2,1)S(1)} %dynamic-slice_bitcast_fusion.3), channel_id=1, source_target_pairs={{0,8},{4,12},{8,0},{12,4},{16,24},{20,28},{24,16},{28,20},{1,9},{5... | collective-permute-start | bytes 3538952 | tf_op jit(solution)/shard_map/ppermute | solution.py:20
  422.7 30.7 %collective-permute-start.51 = (bf16[768,768]{1,0:T(8,128)(2,1)S(1)}, bf16[768,768]{1,0:T(8,128)(2,1)S(1)}, u32[]{:S(2)}, u32[]{:S(2)}) collective-permute-start(bf16[768,768]{1,0:T(8,128)(2,1)S(1)} %dynamic-slice_bitcast_fusion.2), channel_id=1, source_target_pairs={{0,16},{4,20},{8,24},{12,28},{16,0},{20,4},{24,8},{28,12},{1,17},{... | collective-permute-start | bytes 3538952 | tf_op jit(solution)/shard_map/ppermute | solution.py:20
  424.3 5.6 collective-permute-start.38
  426.4 31.2 %collective-permute-start.31 = (bf16[240,768]{1,0:T(8,128)(2,1)S(1)}, bf16[240,768]{1,0:T(8,128)(2,1)S(1)}, u32[]{:S(2)}, u32[]{:S(2)}) collective-permute-start(bf16[240,768]{1,0:T(8,128)(2,1)S(1)} %pad_maximum_fusion.16), channel_id=1, source_target_pairs={{0,16},{4,20},{8,24},{12,28},{16,0},{20,4},{24,8},{28,12},{1,17},{... | collective-permute-start | bytes 1105928 | tf_op jit(solution)/shard_map/ppermute | solution.py:20
  430.2 75.0 %collective-permute-start.39 = (bf16[240,768]{1,0:T(8,128)(2,1)S(1)}, bf16[240,768]{1,0:T(8,128)(2,1)S(1)}, u32[]{:S(2)}, u32[]{:S(2)}) collective-permute-start(bf16[240,768]{1,0:T(8,128)(2,1)S(1)} %pad_maximum_fusion.17), channel_id=1, source_target_pairs={{0,8},{4,12},{8,0},{12,4},{16,24},{20,28},{24,16},{28,20},{1,9},{5... | collective-permute-start | bytes 1105928 | tf_op jit(solution)/shard_map/ppermute | solution.py:20
  451.8 12.1 %collective-permute-start.44 = (bf16[384,768]{1,0:T(8,128)(2,1)S(1)}, bf16[384,768]{1,0:T(8,128)(2,1)S(1)}, u32[]{:S(2)}, u32[]{:S(2)}) collective-permute-start(bf16[384,768]{1,0:T(8,128)(2,1)S(1)} %dynamic-slice_bitcast_fusion.7), channel_id=1, source_target_pairs={{0,16},{4,20},{8,24},{12,28},{16,0},{20,4},{24,8},{28,12},{1,17},{... | collective-permute-start | bytes 1769480 | tf_op jit(solution)/shard_map/ppermute | solution.py:20
  453.8 17.8 %collective-permute-start.52 = (bf16[384,768]{1,0:T(8,128)(2,1)S(1)}, bf16[384,768]{1,0:T(8,128)(2,1)S(1)}, u32[]{:S(2)}, u32[]{:S(2)}) collective-permute-start(bf16[384,768]{1,0:T(8,128)(2,1)S(1)} %dynamic-slice_bitcast_fusion.6), channel_id=1, source_target_pairs={{0,8},{4,12},{8,0},{12,4},{16,24},{20,28},{24,16},{28,20},{1,9},{5... | collective-permute-start | bytes 1769480 | tf_op jit(solution)/shard_map/ppermute | solution.py:20
  457.8 63.7 %collective-permute-start.32 = (bf16[480,768]{1,0:T(8,128)(2,1)S(1)}, bf16[480,768]{1,0:T(8,128)(2,1)S(1)}, u32[]{:S(2)}, u32[]{:S(2)}) collective-permute-start(bf16[480,768]{1,0:T(8,128)(2,1)S(1)} %pad_maximum_fusion.12), channel_id=1, source_target_pairs={{0,8},{4,12},{8,0},{12,4},{16,24},{20,28},{24,16},{28,20},{1,9},{5... | collective-permute-start | bytes 2211848 | tf_op jit(solution)/shard_map/ppermute | solution.py:20
  464.1 9.3 %collective-permute-start.45 = (bf16[192,768]{1,0:T(8,128)(2,1)S(1)}, bf16[192,768]{1,0:T(8,128)(2,1)S(1)}, u32[]{:S(2)}, u32[]{:S(2)}) collective-permute-start(bf16[192,768]{1,0:T(8,128)(2,1)S(1)} %dynamic-slice_bitcast_fusion.11), channel_id=1, source_target_pairs={{0,1},{1,0},{2,3},{3,2},{4,5},{5,4},{6,7},{7,6},{8,9},{9,8},{10,11... | collective-permute-start | bytes 884744 | tf_op jit(solution)/shard_map/ppermute | solution.py:20
  471.8 11.5 %collective-permute-start.53 = (bf16[192,768]{1,0:T(8,128)(2,1)S(1)}, bf16[192,768]{1,0:T(8,128)(2,1)S(1)}, u32[]{:S(2)}, u32[]{:S(2)}) collective-permute-start(bf16[192,768]{1,0:T(8,128)(2,1)S(1)} %dynamic-slice_bitcast_fusion.10), channel_id=1, source_target_pairs={{0,1},{1,0},{2,3},{3,2},{4,5},{5,4},{6,7},{7,6},{8,9},{9,8},{10,11... | collective-permute-start | bytes 884744 | tf_op jit(solution)/shard_map/ppermute | solution.py:20
  473.6 9.9 %collective-permute-start.46 = (bf16[96,768]{1,0:T(8,128)(2,1)S(1)}, bf16[96,768]{1,0:T(8,128)(2,1)S(1)}, u32[]{:S(2)}, u32[]{:S(2)}) collective-permute-start(bf16[96,768]{1,0:T(8,128)(2,1)S(1)} %dynamic-slice_bitcast_fusion.29), channel_id=1, source_target_pairs={{0,2},{1,3},{2,0},{3,1},{4,6},{5,7},{6,4},{7,5},{8,10},{9,11},{10,... | collective-permute-start | bytes 442376 | tf_op jit(solution)/shard_map/ppermute | solution.py:20
  483.4 7.5 %collective-permute-start.54 = (bf16[96,768]{1,0:T(8,128)(2,1)S(1)}, bf16[96,768]{1,0:T(8,128)(2,1)S(1)}, u32[]{:S(2)}, u32[]{:S(2)}) collective-permute-start(bf16[96,768]{1,0:T(8,128)(2,1)S(1)} %dynamic-slice_bitcast_fusion.28), channel_id=1, source_target_pairs={{0,2},{1,3},{2,0},{3,1},{4,6},{5,7},{6,4},{7,5},{8,10},{9,11},{10,... | collective-permute-start | bytes 442376 | tf_op jit(solution)/shard_map/ppermute | solution.py:20
  483.5 10.2 %collective-permute-start.47 = (bf16[96,768]{1,0:T(8,128)(2,1)S(1)}, bf16[96,768]{1,0:T(8,128)(2,1)S(1)}, u32[]{:S(2)}, u32[]{:S(2)}) collective-permute-start(bf16[96,768]{1,0:T(8,128)(2,1)S(1)} %fusion.76), channel_id=1, source_target_pairs={{0,2},{1,3},{2,0},{3,1},{4,6},{5,7},{6,4},{7,5},{8,10},{9,11},{10,... | collective-permute-start | bytes 442376 | tf_op jit(solution)/shard_map/ppermute | solution.py:20
  491.0 7.0 %collective-permute-start.55 = (bf16[96,768]{1,0:T(8,128)(2,1)S(1)}, bf16[96,768]{1,0:T(8,128)(2,1)S(1)}, u32[]{:S(2)}, u32[]{:S(2)}) collective-permute-start(bf16[96,768]{1,0:T(8,128)(2,1)S(1)} %fusion.75), channel_id=1, source_target_pairs={{0,2},{1,3},{2,0},{3,1},{4,6},{5,7},{6,4},{7,5},{8,10},{9,11},{10,... | collective-permute-start | bytes 442376 | tf_op jit(solution)/shard_map/ppermute | solution.py:20
  493.8 7.2 %collective-permute-start.48 = (bf16[192,768]{1,0:T(8,128)(2,1)S(1)}, bf16[192,768]{1,0:T(8,128)(2,1)S(1)}, u32[]{:S(2)}, u32[]{:S(2)}) collective-permute-start(bf16[192,768]{1,0:T(8,128)(2,1)S(1)} %pad_maximum_fusion.18), channel_id=1, source_target_pairs={{0,1},{1,0},{2,3},{3,2},{4,5},{5,4},{6,7},{7,6},{8,9},{9,8},{10,11... | collective-permute-start | bytes 884744 | tf_op jit(solution)/shard_map/ppermute | solution.py:20
  498.0 6.8 %collective-permute-start.56 = (bf16[192,768]{1,0:T(8,128)(2,1)S(1)}, bf16[192,768]{1,0:T(8,128)(2,1)S(1)}, u32[]{:S(2)}, u32[]{:S(2)}) collective-permute-start(bf16[192,768]{1,0:T(8,128)(2,1)S(1)} %pad_maximum_fusion.19), channel_id=1, source_target_pairs={{0,1},{1,0},{2,3},{3,2},{4,5},{5,4},{6,7},{7,6},{8,9},{9,8},{10,11... | collective-permute-start | bytes 884744 | tf_op jit(solution)/shard_map/ppermute | solution.py:20
  501.2 16.3 %collective-permute-start.49 = (bf16[384,768]{1,0:T(8,128)(2,1)S(1)}, bf16[384,768]{1,0:T(8,128)(2,1)S(1)}, u32[]{:S(2)}, u32[]{:S(2)}) collective-permute-start(bf16[384,768]{1,0:T(8,128)(2,1)S(1)} %pad_maximum_fusion.14), channel_id=1, source_target_pairs={{0,16},{4,20},{8,24},{12,28},{16,0},{20,4},{24,8},{28,12},{1,17},{... | collective-permute-start | bytes 1769480 | tf_op jit(solution)/shard_map/ppermute | solution.py:20
  504.9 13.9 %collective-permute-start.57 = (bf16[384,768]{1,0:T(8,128)(2,1)S(1)}, bf16[384,768]{1,0:T(8,128)(2,1)S(1)}, u32[]{:S(2)}, u32[]{:S(2)}) collective-permute-start(bf16[384,768]{1,0:T(8,128)(2,1)S(1)} %pad_maximum_fusion.15), channel_id=1, source_target_pairs={{0,8},{4,12},{8,0},{12,4},{16,24},{20,28},{24,16},{28,20},{1,9},{5... | collective-permute-start | bytes 1769480 | tf_op jit(solution)/shard_map/ppermute | solution.py:20
  505.3 24.6 %collective-permute-start.40 = (bf16[480,768]{1,0:T(8,128)(2,1)S(1)}, bf16[480,768]{1,0:T(8,128)(2,1)S(1)}, u32[]{:S(2)}, u32[]{:S(2)}) collective-permute-start(bf16[480,768]{1,0:T(8,128)(2,1)S(1)} %pad_maximum_fusion.13), channel_id=1, source_target_pairs={{0,16},{4,20},{8,24},{12,28},{16,0},{20,4},{24,8},{28,12},{1,17},{... | collective-permute-start | bytes 2211848 | tf_op jit(solution)/shard_map/ppermute | solution.py:20
  517.8 16.3 %collective-permute-start.50 = (bf16[768,768]{1,0:T(8,128)(2,1)S(1)}, bf16[768,768]{1,0:T(8,128)(2,1)S(1)}, u32[]{:S(2)}, u32[]{:S(2)}) collective-permute-start(bf16[768,768]{1,0:T(8,128)(2,1)S(1)} %pad_maximum_fusion.7), channel_id=1, source_target_pairs={{0,8},{4,12},{8,0},{12,4},{16,24},{20,28},{24,16},{28,20},{1,9},{5... | collective-permute-start | bytes 3538952 | tf_op jit(solution)/shard_map/ppermute | solution.py:20
  519.1 23.5 %collective-permute-start.58 = (bf16[768,768]{1,0:T(8,128)(2,1)S(1)}, bf16[768,768]{1,0:T(8,128)(2,1)S(1)}, u32[]{:S(2)}, u32[]{:S(2)}) collective-permute-start(bf16[768,768]{1,0:T(8,128)(2,1)S(1)} %pad_maximum_fusion.8), channel_id=1, source_target_pairs={{0,16},{4,20},{8,24},{12,28},{16,0},{20,4},{24,8},{28,12},{1,17},{... | collective-permute-start | bytes 3538952 | tf_op jit(solution)/shard_map/ppermute | solution.py:20
  521.5 28.7 %collective-permute-start.11 = (bf16[128,768]{1,0:T(8,128)(2,1)S(1)}, bf16[128,768]{1,0:T(8,128)(2,1)S(1)}, u32[]{:S(2)}, u32[]{:S(2)}) collective-permute-start(bf16[128,768]{1,0:T(8,128)(2,1)S(1)} %copy-done.87), channel_id=1, source_target_pairs={{0,1},{1,0},{2,3},{3,2},{4,5},{5,4},{6,7},{7,6},{8,9},{9,8},{10,11... | collective-permute-start | bytes 589832 | tf_op jit(solution)/shard_map/ppermute | solution.py:20
  530.0 20.5 %collective-permute-start.9 = (bf16[128,768]{1,0:T(8,128)(2,1)S(1)}, bf16[128,768]{1,0:T(8,128)(2,1)S(1)}, u32[]{:S(2)}, u32[]{:S(2)}) collective-permute-start(bf16[128,768]{1,0:T(8,128)(2,1)S(1)} %copy-done.86), channel_id=1, source_target_pairs={{0,3},{1,2},{2,1},{3,0},{4,7},{5,6},{6,5},{7,4},{8,11},{9,10},{10,... | collective-permute-start | bytes 589832 | tf_op jit(solution)/shard_map/ppermute | solution.py:20
  534.1 40.1 %collective-permute-start.41 = (bf16[1920,768]{1,0:T(8,128)(2,1)S(1)}, bf16[1920,768]{1,0:T(8,128)(2,1)S(1)}, u32[]{:S(2)}, u32[]{:S(2)}) collective-permute-start(bf16[1920,768]{1,0:T(8,128)(2,1)S(1)} %pad_maximum_fusion.6), channel_id=1, source_target_pairs={{0,4},{4,0},{8,12},{12,8},{16,20},{20,16},{24,28},{28,24},{1,5},{5... | collective-permute-start | bytes 8847368 | tf_op jit(solution)/shard_map/ppermute | solution.py:20
  546.0 50.2 %collective-permute-start.59 = (bf16[3072,768]{1,0:T(8,128)(2,1)}, bf16[3072,768]{1,0:T(8,128)(2,1)}, u32[]{:S(2)}, u32[]{:S(2)}) collective-permute-start(bf16[3072,768]{1,0:T(8,128)(2,1)} %pad_maximum_fusion.3), channel_id=1, source_target_pairs={{0,4},{4,0},{8,12},{12,8},{16,20},{20,16},{24,28},{28,24},{1,5},{5... | collective-permute-start | bytes 14155784 | tf_op jit(solution)/shard_map/ppermute | solution.py:20
  546.8 9.6 %collective-permute-start.21 = (bf16[128,768]{1,0:T(8,128)(2,1)S(1)}, bf16[128,768]{1,0:T(8,128)(2,1)S(1)}, u32[]{:S(2)}, u32[]{:S(2)}) collective-permute-start(bf16[128,768]{1,0:T(8,128)(2,1)S(1)} %copy-done.85), channel_id=1, source_target_pairs={{0,3},{1,2},{2,1},{3,0},{4,7},{5,6},{6,5},{7,4},{8,11},{9,10},{10,... | collective-permute-start | bytes 589832 | tf_op jit(solution)/shard_map/ppermute | solution.py:20
  550.2 18.2 %collective-permute-start.22 = (bf16[128,768]{1,0:T(8,128)(2,1)S(1)}, bf16[128,768]{1,0:T(8,128)(2,1)S(1)}, u32[]{:S(2)}, u32[]{:S(2)}) collective-permute-start(bf16[128,768]{1,0:T(8,128)(2,1)S(1)} %copy-done.84), channel_id=1, source_target_pairs={{0,2},{1,3},{2,0},{3,1},{4,6},{5,7},{6,4},{7,5},{8,10},{9,11},{10,... | collective-permute-start | bytes 589832 | tf_op jit(solution)/shard_map/ppermute | solution.py:20
  550.5 17.9 %collective-permute-start.23 = (bf16[128,768]{1,0:T(8,128)(2,1)S(1)}, bf16[128,768]{1,0:T(8,128)(2,1)S(1)}, u32[]{:S(2)}, u32[]{:S(2)}) collective-permute-start(bf16[128,768]{1,0:T(8,128)(2,1)S(1)} %copy-done.83), channel_id=1, source_target_pairs={{0,1},{1,0},{2,3},{3,2},{4,5},{5,4},{6,7},{7,6},{8,9},{9,8},{10,11... | collective-permute-start | bytes 589832 | tf_op jit(solution)/shard_map/ppermute | solution.py:20
  (142 other events, 944.1 us)

commit v2 on v1

v2 whole, which is shorter than its diff:
```python
import functools

import jax
import jax.numpy as jnp
from jax import lax
from jax.experimental import pallas as pl
from jax.experimental.pallas import tpu as pltpu
from jax.sharding import PartitionSpec as P

HEADS = 12
LANES = 128
NORM_EPS = 1e-06
ROOT_HALF = 0.7071067811865476
ROOT_TWO_PI = 2.5066282746310002
LOG2_E = 1.4426950408889634
F32 = jnp.float32
BF16 = jnp.bfloat16


def bits_of(size):
    return size.bit_length() - 1


def hop(value, axis, bit):
    size = lax.axis_size(axis)
    return lax.ppermute(value, axis, [(i, i ^ bit) for i in range(size)])


def tie(*values):
    return lax.optimization_barrier(values)


def take_clips(values):
    tm = lax.axis_size("tm")
    me = lax.axis_index("tm")
    out = []
    for d in range(tm):
        block = lax.dynamic_index_in_dim(values, me ^ d, 1, keepdims=False)
        out.append(hop(block, "tm", d) if d else block)
    return jnp.concatenate(out, 1)


def give_clips(values):
    tm = lax.axis_size("tm")
    blocks = jnp.split(values, tm, 1)
    blocks = [hop(block, "tm", d) if d else block for d, block in enumerate(blocks)]
    return jnp.stack(unshuffle(blocks), 1)


def unshuffle(blocks):
    me = lax.axis_index("tm")
    blocks = list(blocks)
    for b in range(bits_of(len(blocks))):
        odd = ((me >> b) & 1) == 1
        blocks = [jnp.where(odd, blocks[i ^ (1 << b)], blocks[i]) for i in range(len(blocks))]
    return blocks


def axis_bits(axis):
    return [(axis, 1 << b) for b in range(bits_of(lax.axis_size(axis)))]


def own_bit(axis, bit):
    return (lax.axis_index(axis) // bit) % 2


def add_low(a, b):
    return (a.astype(F32) + b.astype(F32)).astype(BF16)


def halve(value, names, name):
    at = names.index(name)
    mine = own_bit(*name)
    away = lax.dynamic_index_in_dim(value, 1 - mine, at, keepdims=False)
    kept = lax.dynamic_index_in_dim(value, mine, at, keepdims=False)
    return add_low(kept, hop(away, *name)), names[:at] + names[at + 1 :]


def scatter_rounds(merge):
    clip_bits, time_bits = axis_bits("clips")[1:], axis_bits("tm")
    names = clip_bits[::-1] + time_bits[::-1]
    swapped = clip_bits[1:] + clip_bits[:1]

    def sides(index):
        def step(state):
            out = []
            for side, order in zip(state, (clip_bits, swapped)):
                now = [n for n in names if n not in order[:index]]
                out.append(halve(side, now, order[index])[0])
            return (merge(*out),) if index == len(clip_bits) - 1 else tuple(out)

        return step

    def last(index):
        def step(state):
            return (halve(state[0], time_bits[index:][::-1], time_bits[index])[0],)

        return step

    return [sides(i) for i in range(len(clip_bits))] + [last(i) for i in range(len(time_bits))]


def split_share(value):
    count = bits_of(lax.axis_size("clips")) + bits_of(lax.axis_size("tm")) - 1
    rows = value.shape[0] + -value.shape[0] % (1 << count)
    value = jnp.pad(value, ((0, rows - value.shape[0]), (0, 0)))
    return value.reshape((2,) * count + (rows >> count, value.shape[1]))


def fold(value, width):
    return jnp.concatenate(jnp.split(value, value.shape[-1] // width, -1), -2)


def gather(share):
    return lax.all_gather(share, ("clips", "tm"), axis=0, tiled=False)


def by_core(whole):
    whole = whole.reshape((-1, 2, lax.axis_size("tm")) + whole.shape[1:])
    return jnp.swapaxes(whole, 0, 1)


def unfold(whole, parts):
    others, tm, rows, width = whole.shape
    whole = whole.reshape(others, tm, parts, rows // parts, width)
    return jnp.swapaxes(whole, 2, 3).reshape(others * tm * rows // parts, parts * width)


def place_kernel(in_ref, *out_refs):
    share = in_ref[0].astype(F32)
    width = share.shape[1]
    at = 0
    for out_ref in out_refs:
        rows, columns = out_ref.shape
        for part in range(columns // width):
            out_ref[:, part * width : (part + 1) * width] = share[at : at + rows]
            at += rows


def place(whole, blocks):
    devices, rows, width = whole.shape
    tm = lax.axis_size("tm")
    half = devices // 2

    def spot(d):
        return (d // (2 * tm)) * tm + d % tm, (d // tm) % 2

    def by_row(d):
        other, core = spot(d)
        return core * half + other, 0

    return pl.pallas_call(
        place_kernel,
        grid=(devices,),
        in_specs=[pl.BlockSpec((1, rows, width), lambda d: (d, 0, 0))],
        out_specs=[pl.BlockSpec((n, p * width), spot if column else by_row) for n, p, column in blocks],
        out_shape=[
            jax.ShapeDtypeStruct((n * half, 2 * p * width) if column else (n * devices, p * width), F32)
            for n, p, column in blocks
        ],
        cost_estimate=pl.CostEstimate(flops=0, bytes_accessed=6 * devices * rows * width, transcendentals=0),
    )(whole)


def contract(a, b, da, db):
    return lax.dot_general(a, b, (((da,), (db,)), ((), ())), preferred_element_type=F32)


def own_lanes(value, i, head):
    lane = lax.broadcasted_iota(jnp.int32, value.shape, 1)
    return jnp.where((lane >= i * head) & (lane < (i + 1) * head), value, jnp.zeros_like(value))


def attend_kernel(q_ref, k_ref, v_ref, o_ref, log_ref, *, head):
    q, k, v = q_ref[...], k_ref[...], v_ref[...]
    factor = head**-0.5 * LOG2_E
    outs = []
    for i in range(q.shape[1] // head):
        scores = contract(k, own_lanes(q, i, head), 1, 1)
        peak = jnp.max(scores, 0, keepdims=True)
        raised = jnp.exp2((scores - peak) * factor)
        total = jnp.sum(raised, 0, keepdims=True)
        mixed = contract(v, raised.astype(BF16), 0, 0)
        outs.append(mixed[i * head : (i + 1) * head] * (1.0 / total))
        log_ref[0, i : i + 1, :] = peak * factor + jnp.log2(total)
    o_ref[...] = jnp.concatenate(outs, 0).T.astype(BF16)


def attend_back_kernel(q_ref, k_ref, v_ref, g_ref, log_ref, dq_ref, dk_ref, dv_ref, *, head):
    q, k, v, g = q_ref[...], k_ref[...], v_ref[...], g_ref[...]
    scale = head**-0.5
    grad_q, grad_k, grad_v = [], 0.0, 0.0
    for i in range(q.shape[1] // head):
        q_own, g_own = own_lanes(q, i, head), own_lanes(g, i, head)
        scores = contract(k, q_own, 1, 1)
        probs = jnp.exp2(scores * (scale * LOG2_E) - log_ref[0, i : i + 1, :])
        grad_probs = contract(v, g_own, 1, 1)
        delta = jnp.sum(probs * grad_probs, 0, keepdims=True)
        grad_scores = (probs * (grad_probs - delta)).astype(BF16)
        grad_q.append(contract(k, grad_scores, 0, 0)[i * head : (i + 1) * head])
        grad_k = grad_k + contract(grad_scores, q_own, 1, 0)
        grad_v = grad_v + contract(probs.astype(BF16), g_own, 1, 0)
    dq_ref[...] = (jnp.concatenate(grad_q, 0) * scale).T.astype(BF16)
    dk_ref[...] = (grad_k * scale).astype(BF16)
    dv_ref[...] = grad_v.astype(BF16)


def attend(joint, width):
    rows = joint.shape[0]
    head = width // HEADS
    pairs, per = width // LANES, LANES // head
    block = lambda off: pl.BlockSpec((rows, LANES), lambda h: (0, h + off))
    return pl.pallas_call(
        functools.partial(attend_kernel, head=head),
        grid=(pairs,),
        in_specs=[block(0), block(pairs), block(2 * pairs)],
        out_specs=[block(0), pl.BlockSpec((1, per, rows), lambda h: (h, 0, 0))],
        out_shape=[
            jax.ShapeDtypeStruct((rows, width), BF16),
            jax.ShapeDtypeStruct((pairs, per, rows), F32),
        ],
        cost_estimate=pl.CostEstimate(
            flops=16 * rows * rows * width, bytes_accessed=8 * rows * width, transcendentals=rows * rows * HEADS
        ),
        compiler_params=pltpu.CompilerParams(vmem_limit_bytes=32 * 2**20),
    )(joint, joint, joint)


def attend_back(joint, mix, log_sum):
    rows, width = mix.shape
    head = width // HEADS
    pairs, per = width // LANES, LANES // head
    block = lambda off: pl.BlockSpec((rows, LANES), lambda h: (0, h + off))
    return pl.pallas_call(
        functools.partial(attend_back_kernel, head=head),
        grid=(pairs,),
        in_specs=[
            block(0),
            block(pairs),
            block(2 * pairs),
            block(0),
            pl.BlockSpec((1, per, rows), lambda h: (h, 0, 0)),
        ],
        out_specs=[block(0)] * 3,
        out_shape=[jax.ShapeDtypeStruct((rows, width), BF16)] * 3,
        cost_estimate=pl.CostEstimate(
            flops=40 * rows * rows * width, bytes_accessed=16 * rows * width, transcendentals=rows * rows * HEADS
        ),
        compiler_params=pltpu.CompilerParams(vmem_limit_bytes=32 * 2**20),
    )(joint, joint, joint, mix, log_sum)


def norm_parts(values):
    centred = values - jnp.mean(values, -1, keepdims=True)
    spread = jnp.mean(centred * centred, -1, keepdims=True)
    inverse = lax.rsqrt(spread + NORM_EPS)
    return centred * inverse, inverse


def norm_backward(grad_norm, unit, inverse, gains):
    scaled = grad_norm * gains
    return inverse * (
        scaled
        - jnp.mean(scaled, -1, keepdims=True)
        - unit * jnp.mean(scaled * unit, -1, keepdims=True)
    )


def dot(a, b):
    return jnp.dot(a, b, preferred_element_type=F32)


def dot_nt(a, b):
    return contract(a, b, 1, 1)


def dot_tn(a, b):
    return contract(a, b, 0, 0)


def on_device(
    patches, mask_index, mask_count, w_qkv, q_bias, v_bias, w_out, out_bias, w_up, up_bias,
    w_down, down_bias, norm1_scale, norm1_shift, norm2_scale, norm2_shift, mask_embed, pos_embed,
    cotangent,
):
    clip_count, seg, width = patches.shape
    ff = w_up.shape[1]
    tm = lax.axis_size("tm")
    me = lax.axis_index("tm")
    devices = tm * lax.axis_size("clips")
    length = seg * tm
    groups = clip_count // tm
    joint_bias = jnp.concatenate([q_bias, jnp.zeros_like(q_bias), v_bias]).astype(F32)
    out_bias, up_bias, down_bias = (x.astype(F32) for x in (out_bias, up_bias, down_bias))
    gain1, shift1, gain2, shift2, embed = (
        x.astype(F32) for x in (norm1_scale, norm1_shift, norm2_scale, norm2_shift, mask_embed)
    )

    by_group = (groups, tm, seg, width)
    arrived = [take_clips(patches.reshape(by_group)[g : g + 1])[0] for g in range(groups)]
    cot = take_clips(cotangent.reshape(by_group))

    starts = (me ^ jnp.arange(tm, dtype=jnp.int32)) * seg
    places = (starts[:, None] + jnp.arange(seg, dtype=jnp.int32)[None, :]).reshape(length)
    pos = jnp.concatenate(
        [lax.dynamic_slice_in_dim(pos_embed, (me ^ d) * seg, seg, 0) for d in range(tm)], 0
    ).astype(F32)
    slots = jnp.arange(mask_index.shape[1], dtype=jnp.int32)

    saved = []
    for g in range(groups):
        index_row = lax.dynamic_index_in_dim(mask_index, g * tm + me, 0, keepdims=False)
        count = lax.dynamic_index_in_dim(mask_count, g * tm + me, 0, keepdims=False)
        live = slots < count
        masked = jnp.any((places[:, None] == index_row[None, :]) & live[None, :], axis=1)[:, None]
        filled = jnp.where(masked, embed[None, :], arrived[g].astype(F32)) + pos
        unit_one, inverse_one = norm_parts(filled)
        normed_one = (unit_one * gain1 + shift1).astype(BF16)
        joint = (dot(normed_one, w_qkv) + joint_bias).astype(BF16)
        attended, log_sum = attend(joint, width)
        hidden = filled + dot(attended, w_out) + out_bias
        unit_two, inverse_two = norm_parts(hidden)
        normed_two = (unit_two * gain2 + shift2).astype(BF16)
        saved.append((masked, unit_one, inverse_one, normed_one, joint, attended, log_sum, hidden,
                      unit_two, inverse_two, normed_two))
    masked, unit_one, inverse_one, normed_one, joint, attended, log_sum, hidden, unit_two, inverse_two, normed_two = (
        zip(*saved)
    )
    rows = lambda xs: jnp.concatenate(xs, 0)
    masked, unit_one, inverse_one, normed_one, attended, hidden, unit_two, inverse_two, normed_two = map(
        rows, (masked, unit_one, inverse_one, normed_one, attended, hidden, unit_two, inverse_two, normed_two)
    )
    cot = cot.reshape(groups * length, width)
    up_proj = dot(normed_two, w_up) + up_bias
    cumulative = 0.5 * (1.0 + lax.erf(up_proj * ROOT_HALF))
    activated = (up_proj * cumulative).astype(BF16)
    slope = cumulative + up_proj * jnp.exp(-0.5 * up_proj * up_proj) / ROOT_TWO_PI
    grad_up_in = (dot_nt(cot, w_down) * slope).astype(BF16)
    core = own_bit("clips", 1)

    def half(values, side):
        return lax.dynamic_slice_in_dim(values, side * (values.shape[1] // 2), values.shape[1] // 2, 1)

    down_got = hop(dot_tn(half(activated, 1 - core), cot).astype(BF16), "clips", 1)
    up_got = hop(dot_tn(normed_two, half(grad_up_in, 1 - core)).astype(BF16), "clips", 1)
    down = (dot_tn(half(activated, core), cot) + down_got.astype(F32)).astype(BF16)
    up = (dot_tn(normed_two, half(grad_up_in, core)) + up_got.astype(F32)).astype(BF16)
    rounds = iter(
        scatter_rounds(lambda a, b: jnp.concatenate([a, fold(b, width)], -2))
    )
    state = next(rounds)((split_share(down), split_share(up)))

    block_out = (hidden + dot(activated, w_down) + down_bias).astype(BF16)
    top = cot.astype(F32)
    grad_norm_two = dot_nt(grad_up_in, w_up)
    grad_hidden = top + norm_backward(grad_norm_two, unit_two, inverse_two, gain2)
    branch = grad_hidden.astype(BF16)
    grad_out = dot_tn(attended, branch).astype(BF16)
    mix = dot_nt(branch, w_out).astype(BF16)
    mix, block_out = tie(mix, block_out)
    block_out = give_clips(block_out.reshape(groups, length, width)).reshape(patches.shape)

    back = []
    for g in range(groups):
        back.append(attend_back(joint[g], mix[g * length : (g + 1) * length], log_sum[g]))
        if g < groups - 1:
            mix, *state = tie(mix, *state)
            state = next(rounds)(state)
    grad_joint = jnp.concatenate([jnp.concatenate(b, 1) for b in back], 0)
    grad_joint, block_out, *state = tie(grad_joint, block_out, *state)
    state = next(rounds)(state)

    qkv_got = hop(dot_tn(half(normed_one, 1 - core), grad_joint).astype(BF16), "clips", 1)
    qkv = (dot_tn(half(normed_one, core), grad_joint) + qkv_got.astype(F32)).astype(BF16)
    grad_norm_one = dot_nt(grad_joint, w_qkv)
    grad_norm_one, qkv, *state = tie(grad_norm_one, qkv, *state)
    for step in rounds:
        state = step(state)
    grad_filled = grad_hidden + norm_backward(grad_norm_one, unit_one, inverse_one, gain1)
    input_grad = jnp.where(masked, 0.0, grad_filled).astype(BF16)

    joint_sums = jnp.sum(grad_joint.astype(F32), 0)
    pos_sum = jnp.sum(grad_filled.reshape(groups, length, width), 0)
    pos_sum = jnp.concatenate(unshuffle(jnp.split(pos_sum.astype(BF16), tm, 0)), 0)
    small = [
        joint_sums[:width],
        joint_sums[2 * width :],
        jnp.sum(branch.astype(F32), 0),
        jnp.sum(grad_up_in.astype(F32), 0),
        jnp.sum(top, 0),
        jnp.sum(grad_norm_one * unit_one, 0),
        jnp.sum(grad_norm_one, 0),
        jnp.sum(grad_norm_two * unit_two, 0),
        jnp.sum(grad_norm_two, 0),
        jnp.sum(jnp.where(masked, grad_filled, 0.0), 0),
    ]
    small = jnp.concatenate([x.reshape(-1, width) for x in small], 0).astype(BF16)
    small = jnp.pad(small, ((0, width - length - small.shape[0]), (0, 0)))
    rest = jnp.concatenate([pos_sum, small], 0)
    rest_got = hop(jnp.where(core == 1, grad_out, rest), "clips", 1)
    rest = add_low(jnp.where(core == 1, rest, grad_out), rest_got)
    input_grad, rest, qkv, *state = tie(input_grad, rest, qkv, *state)
    whole_one = gather(state[0])
    input_grad = give_clips(input_grad.reshape(groups, length, width)).reshape(patches.shape)
    state = (split_share(qkv), split_share(rest))
    for step in scatter_rounds(lambda a, b: jnp.concatenate([fold(a, width), b], -2)):
        state = step(state)
    share_two, whole_one = tie(state[0], whole_one)
    whole_two = gather(share_two)

    rows_one, rows_two = ff // devices, width // devices
    up_rows = width // (devices // 2)
    if rows_two % 8 == 0:
        w_down_sum, w_up_sum = place(whole_one, ((rows_one, 1, False), (up_rows, ff // (2 * width), True)))
        w_qkv_sum, rest = place(whole_two, ((rows_two, 3, False), (up_rows, 1, False)))
    else:
        whole_one, whole_two = by_core(whole_one), by_core(whole_two)
        w_down_sum = whole_one[..., :rows_one, :].reshape(ff, width).astype(F32)
        w_up_sum = jnp.concatenate([unfold(x[..., rows_one:, :], ff // (2 * width)) for x in whole_one], 1)
        w_up_sum = w_up_sum.astype(F32)
        w_qkv_sum = jnp.concatenate([unfold(x[..., : 3 * rows_two, :], 3) for x in whole_two], 0).astype(F32)
        rest = whole_two[..., 3 * rows_two :, :].reshape(2 * width, width).astype(F32)
    w_out_sum, rest = rest[:width], rest[width:]
    pos_total = rest[:length]
    v = []
    at = length
    for n in (1, 1, 1, ff // width, 1, 1, 1, 1, 1, 1):
        v.append(rest[at : at + n].reshape(-1))
        at += n
    return (block_out, input_grad, w_qkv_sum, v[0], v[1], w_out_sum, v[2], w_up_sum, v[3], w_down_sum, v[4],
            v[5], v[6], v[7], v[8], v[9], pos_total)


def solution(mesh):
    rows = P("clips", "tm", None)
    in_specs = (rows, P("clips", None), P("clips")) + (P(),) * 15 + (rows,)
    out_specs = (rows, rows) + (P(),) * 15
    return jax.shard_map(on_device, mesh=mesh, in_specs=in_specs, out_specs=out_specs, check_vma=False)
```

time: 624 us -> 570 us (0.913)
  Pallas kernels: 0 us -> 83.5 us
  local copies, waits for them, and re-layouts: 103 us -> 45 us
  matrix products: 146 us -> 92.5 us
  starting transfers between devices: 92.8 us -> 44.6 us
  waiting for transfers between devices: 145 us -> 187 us
  other arithmetic: 126 us -> 96.7 us
  between operations: 3.45 us -> 15.5 us
    pallas_call x0 -> x6, Pallas kernels: none -> 83.5 us  [the longest x2 40.2 us: place(): pl.pallas_call(place_kernel, grid=(devices,), in_specs=[pl.BlockSpec((1,...]
    ppermute x60 -> x31, starting transfers between devices: 92.8 us -> 44.5 us  [hop(): return lax.ppermute(value, axis, [(i, i ^ bit) for i in range(size)])]
    dot_general x20 -> x11, matrix products: 114 us -> 66.1 us  [contract(): lax.dot_general(a, b, (((da,), (db,)), ((), ())), preferred_element_type=...]
    all_gather x0 -> x2, waiting for transfers between devices: none -> 43.7 us  [gather(): return lax.all_gather(share, ('clips', 'tm'), axis=0, tiled=False)]
    concatenate x2, local copies, waits for them, and re-layouts: 34.9 us -> 4.21 us  [the longest x1 2.7 us: on_device(): jnp.concatenate([x.reshape(-1, width) for x in small], 0).astype(BF16)]
    convert_element_type x26 -> x17, other arithmetic: 41.1 us -> 15.8 us  [the longest x13 7.11 us: add_low(): return (a.astype(F32) + b.astype(F32)).astype(BF16)]
    unnamed x297 -> x134, local copies, waits for them, and re-layouts: 25.5 us -> 4.09 us
    concatenate x16 -> x4, other arithmetic: 11.3 us -> 31.3 us  [the longest x1 30 us: on_device(): grad_joint = jnp.concatenate([jnp.concatenate(b, 1) for b in back], 0)]
  transfers between devices with their start and end apart: 60 -> 33, of which waited for: 30 -> 15; matrix products, arithmetic and copies ran while one was open for 28% -> 27% of each run, Pallas kernels for 0% -> 11%
where the time goes in v2:
time: 570 us; the launch traced here: 565 us
  waiting for transfers between devices  187 us (33%)
  other arithmetic  96.7 us (17%)
  matrix products  92.5 us (16%)
  Pallas kernels  83.5 us (15%)
  local copies, waits for them, and re-layouts  45 us (8%)
  starting transfers between devices  44.6 us (8%)
  between operations  15.5 us (3%)
    ppermute x31, waiting for transfers between devices, hop(): return lax.ppermute(value, axis, [(i, i ^ bit) for i in range(size)])  143 us
    dot_general x11, matrix products, contract(): lax.dot_general(a, b, (((da,), (db,)), ((), ())), preferred_element_type=...  66.1 us
    ppermute x31, starting transfers between devices, hop(): return lax.ppermute(value, axis, [(i, i ^ bit) for i in range(size)])  44.5 us
    all_gather x2, waiting for transfers between devices, gather(): return lax.all_gather(share, ('clips', 'tm'), axis=0, tiled=False)  43.7 us
    pallas_call x2, Pallas kernels, place(): pl.pallas_call(place_kernel, grid=(devices,), in_specs=[pl.BlockSpec((1,...  40.2 us
    concatenate x1, other arithmetic, on_device(): grad_joint = jnp.concatenate([jnp.concatenate(b, 1) for b in back], 0)  30 us
    dot_general x6, matrix products, dot(): return jnp.dot(a, b, preferred_element_type=F32)  26.4 us
    pallas_call x2, Pallas kernels, attend_back(): pl.pallas_call(functools.partial(attend_back_kernel, head=head), grid=(pa...  25.8 us
  transfers between devices with their start and end apart: 33, of which 15 were waited for; matrix products, arithmetic and copies ran while one was open for 27% of the time, Pallas kernels for 11%

profile of v2, /device:TPU:0, one launch (start us, length us, event | category | flops | bytes accessed | tf_op | source)
XLA Modules:
  0.0 564.9 jit_solution(8424473829076267791)
XLA Ops:
  7.3 2.8 fusion.62
  10.0 2.2 constant_dynamic-slice_fusion.11
  12.2 5.0 collective-permute-start.8
  18.7 3.8 collective-permute-start.2
  25.7 6.7 %collective-permute-start = (bf16[1,128,768]{2,1,0:T(8,128)(2,1)}, bf16[1,128,768]{2,1,0:T(8,128)(2,1)}, u32[]{:S(2)}, u32[]{:S(2)}) collective-permute-start(bf16[1,128,768]{2,1,0:T(8,128)(2,1)} %get-tuple-element.152), channel_id=1, source_target_pairs={{0,1},{1,0},{2,3},{3,2},{4,5},{5,4},{6,7},{7,6},{8,9},{9,8},{10,11... | collective-permute-start | bytes 589832 | tf_op jit(solution)/shard_map/ppermute | solution.py:26
  44.0 2.2 dynamic-slice_reduce_fusion
  46.2 2.1 collective-permute-start.5
  48.4 2.3 collective-permute-start.3
  50.7 18.3 %collective-permute-done.1 = bf16[1,128,768]{2,1,0:T(8,128)(2,1)} collective-permute-done((bf16[1,128,768]{2,1,0:T(8,128)(2,1)}, bf16[1,128,768]{2,1,0:T(8,128)(2,1)}, u32[]{:S(2)}, u32[]{:S(2)}) %collective-permute-start.1) | collective-permute-done | bytes 196640 | tf_op jit(solution)/shard_map/ppermute | solution.py:26
  69.0 3.6 fusion.31
  76.2 3.4 add_convert_fusion.6
  79.6 2.0 fusion.7.q_ref.k_ref.v_ref
  81.7 8.6 %shard_map.315 = (bf16[512,768]{1,0:T(8,128)(2,1)S(1)}, f32[6,2,512]{2,1,0:T(2,128)S(1)}) custom-call(bf16[512,2304]{1,0:T(8,128)(2,1)S(1)} %fusion.7.q_ref.k_ref.v_ref, bf16[512,2304]{1,0:T(8,128)(2,1)S(1)} %fusion.7.q_ref.k_ref.v_ref, bf16[512,2304]{1,0:T(8,128)(2,1)S(1)} %fusion.7.q_ref.k_ref.v_ref), custom_call_target="tpu_custom_call" | custom-call | flops 3221225472 | bytes 3145728 | tf_op jit(solution)/shard_map/pallas_call | solution.py:213
  90.3 2.3 fusion.68
  93.0 3.4 add_convert_fusion.7
  97.3 2.0 fusion.6.q_ref.k_ref.v_ref
  99.4 8.8 %shard_map.314 = (bf16[512,768]{1,0:T(8,128)(2,1)S(1)}, f32[6,2,512]{2,1,0:T(2,128)S(1)}) custom-call(bf16[512,2304]{1,0:T(8,128)(2,1)S(1)} %fusion.6.q_ref.k_ref.v_ref, bf16[512,2304]{1,0:T(8,128)(2,1)S(1)} %fusion.6.q_ref.k_ref.v_ref, bf16[512,2304]{1,0:T(8,128)(2,1)S(1)} %fusion.6.q_ref.k_ref.v_ref), custom_call_target="tpu_custom_call" | custom-call | flops 3221225472 | bytes 3145728 | tf_op jit(solution)/shard_map/pallas_call | solution.py:213
  108.2 2.4 fusion.67
  112.0 10.2 %multiply_convert_fusion = (bf16[1024,3072]{1,0:T(8,128)(2,1)}, f32[1024,3072]{1,0:T(8,128)}) fusion(f32[3072]{0:T(1024)S(1)} %copy-done.50, bf16[768,3072]{1,0:T(8,128)(2,1)S(1)} %bitcast.203, bf16[512,768]{1,0:T(8,128)(2,1)S(1)} %get-tuple-element.160, bf16[512,768]{1,0:T(8,128)(2,1)S(1)} %get-tuple-element.104), kind=kOutput, calls=%fused_computation.7 | convolution fusion | flops 4853858304 | bytes 25178112 | tf_op jit(solution)/shard_map/dot_general | solution.py:270
  122.3 7.5 %fusion.9 = bf16[1024,768]{1,0:T(8,128)(2,1)S(1)} fusion(f32[512,768]{1,0:T(8,128)S(1)} %get-tuple-element.169, f32[512,768]{1,0:T(8,128)S(1)} %get-tuple-element.167, bf16[1024,3072]{1,0:T(8,128)(2,1)} %get-tuple-element.171, bf16[3072,768]{1,0:T(8,128)(2,1)S(1)} %bitcast.201, f32[768]{0:T(1024)S(1)} %copy-done.55), kind=kOutput, calls=%fused_computation.23 | convolution fusion | flops 4834983936 | bytes 15731712 | tf_op jit(solution)/shard_map/dot_general | solution.py:270
  130.8 14.5 %fusion.69 = (bf16[3072]{0:T(1024)(128)(2,1)}, bf16[1024,3072]{1,0:T(8,128)(2,1)}) fusion(f32[1024,3072]{1,0:T(8,128)} %get-tuple-element.172, f32[3072]{0:T(1024)S(1)} %copy-done.50, bf16[1024,768]{1,0:T(8,128)(2,1)S(1)} %bitcast.175, bf16[3072,768]{1,0:T(8,128)(2,1)S(1)} %bitcast.201), kind=kOutput, calls=%fused_computation.233 | convolution fusion | flops 4869583872 | bytes 25184256 | tf_op jit(solution)/shard_map/dot_general | solution.py:166
  145.3 6.2 %convolution_convert_fusion.2 = bf16[1536,768]{1,0:T(8,128)(2,1)} fusion(bf16[1024,768]{1,0:T(8,128)(2,1)S(1)} %bitcast.176, bf16[1024,3072]{1,0:T(8,128)(2,1)} %get-tuple-element.171, s32[]{:T(128)S(6)} %select_n.318), kind=kOutput, calls=%fused_computation.19 | convolution fusion | flops 2417098752 | bytes 7077892 | tf_op jit(solution)/shard_map/dot_general | solution.py:166
  151.5 4.1 convolution_convert_fusion.1
  156.0 9.3 %multiply_reduce_fusion = (bf16[768]{0:T(1024)(128)(2,1)}, f32[1024]{0:T(1024)S(1)}, f32[1024]{0:T(1024)S(1)}, bf16[768]{0:T(1024)(128)(2,1)}, f32[1024,768]{1,0:T(8,128)S(1)}) fusion(f32[512,768]{1,0:T(8,128)S(1)} %get-tuple-element.161, f32[512,768]{1,0:T(8,128)S(1)} %get-tuple-element.105, f32[768]{0:T(1024)S(1)} %convert_element_type.301, ...), kind=kOutput, calls=%fused_computation.26 | convolution fusion | flops 4838125568 | bytes 17315840 | tf_op jit(solution)/shard_map/dot_general | solution.py:166
  165.3 2.3 convert_reduce_fusion
  171.3 3.2 collective-permute-start.14
  179.5 5.8 %add_convert_fusion.1 = bf16[1536,768]{1,0:T(8,128)(2,1)S(1)} fusion(bf16[1536,768]{1,0:T(8,128)(2,1)} %collective-permute-done.9, bf16[1024,768]{1,0:T(8,128)(2,1)} %bitcast.177, bf16[1024,3072]{1,0:T(8,128)(2,1)} %get-tuple-element.171, s32[]{:T(128)S(6)} %select_n.317), kind=kOutput, calls=%fused_computation.13 | convolution fusion | flops 2419458048 | bytes 9437188 | tf_op jit(solution)/shard_map/dot_general | solution.py:166
  187.2 5.1 add_convert_fusion
  194.2 13.0 %shard_map.316 = (bf16[512,768]{1,0:T(8,128)(2,1)S(1)}, bf16[512,768]{1,0:T(8,128)(2,1)S(1)}, bf16[512,768]{1,0:T(8,128)(2,1)S(1)}) custom-call(bf16[512,2304]{1,0:T(8,128)(2,1)S(1)} %copy-done.7, bf16[512,2304]{1,0:T(8,128)(2,1)S(1)} %copy-done.7, bf16[512,2304]{1,0:T(8,128)(2,1)S(1)} %copy-done.7, bf16[512,768]{1,0:T(8,128)(2,1)S(1)} %copy-done.1, ...), custom_call_target="tpu_custom_call" | custom-call | flops 8053063680 | bytes 6291456 | tf_op jit(solution)/shard_map/pallas_call | solution.py:234
  210.2 2.5 collective-permute-done.10
  213.0 6.4 %collective-permute-done.12 = bf16[2,2,2,48,1536]{4,3,1,2,0:T(8,128)(2,1)S(1)} collective-permute-done((bf16[2,2,2,48,1536]{4,3,1,2,0:T(8,128)(2,1)S(1)}, bf16[2,2,2,48,1536]{4,3,1,2,0:T(8,128)(2,1)S(1)}, u32[]{:S(2)}, u32[]{:S(2)}) %collective-permute-start.12) | collective-permute-done | bytes 1179680 | tf_op jit(solution)/shard_map/ppermute | solution.py:26
  223.0 12.8 %shard_map.317 = (bf16[512,768]{1,0:T(8,128)(2,1)S(1)}, bf16[512,768]{1,0:T(8,128)(2,1)S(1)}, bf16[512,768]{1,0:T(8,128)(2,1)S(1)}) custom-call(bf16[512,2304]{1,0:T(8,128)(2,1)S(1)} %copy-done.5, bf16[512,2304]{1,0:T(8,128)(2,1)S(1)} %copy-done.5, bf16[512,2304]{1,0:T(8,128)(2,1)S(1)} %copy-done.5, bf16[512,768]{1,0:T(8,128)(2,1)S(1)} %slice.73.g_ref, ...), custom_call_target="tpu_custom_call" | custom-call | flops 8053063680 | bytes 6291456 | tf_op jit(solution)/shard_map/pallas_call | solution.py:234
  235.8 30.0 %maximum_maximum_fusion = bf16[1024,2304]{1,0:T(8,128)(2,1)S(1)} fusion(bf16[512,768]{1,0:T(8,128)(2,1)S(1)} %get-tuple-element.59, bf16[512,768]{1,0:T(8,128)(2,1)S(1)} %get-tuple-element.58, bf16[512,768]{1,0:T(8,128)(2,1)S(1)} %get-tuple-element.57, bf16[512,768]{1,0:T(8,128)(2,1)S(1)} %get-tuple-element.54, bf16[512,768]{1,0:T(8,128)(2,1)S(1)} %get-tuple-element.53, ...), kind=kLoop, calls=%fused_computation.11 | loop fusion | flops 28311552 | bytes 9437184 | tf_op jit(solution)/shard_map/concatenate | solution.py:369
  268.8 3.3 convolution_convert_fusion
  277.1 3.6 reduce.1
  284.0 6.1 %fusion.70 = f32[1024,768]{1,0:T(8,128)S(1)} fusion(bf16[1024,2304]{1,0:T(8,128)(2,1)} %copy-done.13, bf16[768,2304]{1,0:T(8,128)(2,1)S(1)} %copy-done), kind=kOutput, calls=%fused_computation.234 | convolution fusion | flops 3623878656 | bytes 11403264 | tf_op jit(solution)/shard_map/dot_general | solution.py:166
  290.1 9.6 %collective-permute-done.19 = bf16[2,192,768]{2,1,0:T(8,128)(2,1)S(1)} collective-permute-done((bf16[2,192,768]{2,1,0:T(8,128)(2,1)S(1)}, bf16[2,192,768]{2,1,0:T(8,128)(2,1)S(1)}, u32[]{:S(2)}, u32[]{:S(2)}) %collective-permute-start.19) | collective-permute-done | bytes 589856 | tf_op jit(solution)/shard_map/ppermute | solution.py:26
  300.7 4.9 add_convert_fusion.2
  307.9 3.0 select_reduce_fusion
  311.5 3.2 reduce_sum.210
  314.7 2.1 select_dynamic-update-slice_fusion.3
  316.7 2.0 select_dynamic-update-slice_fusion.2
  320.3 2.7 concatenate.85
  324.5 5.5 broadcast_select_fusion
  332.6 3.3 select_convert_fusion
  335.9 11.9 %collective-permute-done.21 = bf16[192,768]{1,0:T(8,128)(2,1)S(1)} collective-permute-done((bf16[192,768]{1,0:T(8,128)(2,1)S(1)}, bf16[192,768]{1,0:T(8,128)(2,1)S(1)}, u32[]{:S(2)}, u32[]{:S(2)}) %collective-permute-start.21) | collective-permute-done | bytes 294944 | tf_op jit(solution)/shard_map/ppermute | solution.py:26
  348.6 3.1 add_convert_fusion.3
  355.2 15.5 %collective-permute-done.27 = bf16[2,2,2,48,768]{4,3,1,2,0:T(8,128)(2,1)S(1)} collective-permute-done((bf16[2,2,2,48,768]{4,3,1,2,0:T(8,128)(2,1)S(1)}, bf16[2,2,2,48,768]{4,3,1,2,0:T(8,128)(2,1)S(1)}, u32[]{:S(2)}, u32[]{:S(2)}) %collective-permute-start.27) | collective-permute-done | bytes 589856 | tf_op jit(solution)/shard_map/ppermute | solution.py:26
  371.4 7.3 %collective-permute-done.25 = bf16[2,2,2,24,2304]{4,3,1,2,0:T(8,128)(2,1)S(1)} collective-permute-done((bf16[2,2,2,24,2304]{4,3,1,2,0:T(8,128)(2,1)S(1)}, bf16[2,2,2,24,2304]{4,3,1,2,0:T(8,128)(2,1)S(1)}, u32[]{:S(2)}, u32[]{:S(2)}) %collective-permute-start.25) | collective-permute-done | bytes 884768 | tf_op jit(solution)/shard_map/ppermute | solution.py:26
  380.5 7.1 %collective-permute-done.28 = bf16[2,2,48,768]{3,2,0,1:T(8,128)(2,1)S(1)} collective-permute-done((bf16[2,2,48,768]{3,2,0,1:T(8,128)(2,1)S(1)}, bf16[2,2,48,768]{3,2,0,1:T(8,128)(2,1)S(1)}, u32[]{:S(2)}, u32[]{:S(2)}) %collective-permute-start.28) | collective-permute-done | bytes 294944 | tf_op jit(solution)/shard_map/ppermute | solution.py:26
  387.7 5.2 collective-permute-done.26
  393.2 11.9 %collective-permute-done.29 = bf16[2,120,768]{2,1,0:T(8,128)(2,1)S(1)} collective-permute-done((bf16[2,120,768]{2,1,0:T(8,128)(2,1)S(1)}, bf16[2,120,768]{2,1,0:T(8,128)(2,1)S(1)}, u32[]{:S(2)}, u32[]{:S(2)}) %collective-permute-start.29) | collective-permute-done | bytes 368672 | tf_op jit(solution)/shard_map/ppermute | solution.py:26
  405.3 2.7 collective-permute-start.30
  408.0 19.5 %collective-permute-done.30 = bf16[120,768]{1,0:T(8,128)(2,1)S(1)} collective-permute-done((bf16[120,768]{1,0:T(8,128)(2,1)S(1)}, bf16[120,768]{1,0:T(8,128)(2,1)S(1)}, u32[]{:S(2)}, u32[]{:S(2)}) %collective-permute-start.30) | collective-permute-done | bytes 184352 | tf_op jit(solution)/shard_map/ppermute | solution.py:26
  428.3 15.4 %all-gather.5.cloned.1.call-done = bf16[6144,768]{1,0:T(8,128)(2,1)} async-done(((bf16[192,768]{1,0:T(8,128)(2,1)}), bf16[6144,768]{1,0:T(8,128)(2,1)}) %all-gather.5.cloned.1.call-update) | async-done | bytes 9437200 | tf_op jit(solution)/shard_map/all_gather | solution.py:115
  445.1 1.9 collective-permute-start.23
  447.1 2.5 collective-permute-start.22
  449.5 16.3 %collective-permute-done.24 = bf16[2,128,768]{2,1,0:T(8,128)(2,1)S(1)} collective-permute-done((bf16[2,128,768]{2,1,0:T(8,128)(2,1)S(1)}, bf16[2,128,768]{2,1,0:T(8,128)(2,1)S(1)}, u32[]{:S(2)}, u32[]{:S(2)}) %collective-permute-start.24) | collective-permute-done | bytes 393248 | tf_op jit(solution)/shard_map/ppermute | solution.py:26
  465.8 12.0 %collective-permute-done.23 = bf16[2,128,768]{2,1,0:T(8,128)(2,1)S(1)} collective-permute-done((bf16[2,128,768]{2,1,0:T(8,128)(2,1)S(1)}, bf16[2,128,768]{2,1,0:T(8,128)(2,1)S(1)}, u32[]{:S(2)}, u32[]{:S(2)}) %collective-permute-start.23) | collective-permute-done | bytes 393248 | tf_op jit(solution)/shard_map/ppermute | solution.py:26
  480.3 20.9 %shard_map.319 = (f32[3072,768]{1,0:T(8,128)}, f32[768,3072]{1,0:T(8,128)}) custom-call(bf16[32,192,768]{2,1,0:T(8,128)(2,1)} %bitcast.172), custom_call_target="tpu_custom_call" | custom-call | bytes 28311552 | tf_op jit(solution)/shard_map/pallas_call | solution.py:152
  501.3 28.3 %all-gather.7.cloned.1.call-done = bf16[3840,768]{1,0:T(8,128)(2,1)} async-done(((bf16[120,768]{1,0:T(8,128)(2,1)}), bf16[3840,768]{1,0:T(8,128)(2,1)}) %all-gather.7.cloned.1.call-update) | async-done | bytes 5898256 | tf_op jit(solution)/shard_map/all_gather | solution.py:115
  529.5 19.3 %shard_map.318 = (f32[768,2304]{1,0:T(8,128)}, f32[1536,768]{1,0:T(8,128)}) custom-call(bf16[32,120,768]{2,1,0:T(8,128)(2,1)} %bitcast.178), custom_call_target="tpu_custom_call" | custom-call | bytes 17694720 | tf_op jit(solution)/shard_map/pallas_call | solution.py:152
  551.3 2.7 slice.87
  553.9 3.2 slice.78
  (287 shorter events, 78.8 us)
Async XLA Ops:
  7.2 72.4 %copy-start = (bf16[768,2304]{1,0:T(8,128)(2,1)S(1)}, bf16[768,2304]{1,0:T(8,128)(2,1)}, u32[]{:S(2)}) copy-start(bf16[768,2304]{1,0:T(8,128)(2,1)} %param.22) | copy-start | bytes 10616836
  7.2 436.5 %all-gather.5.cloned.1.call-start = ((), (), s32[]{:S(2)}) async-start(), calls=%async_computation | async-start | bytes 9732096 | tf_op jit(solution)/shard_map/all_gather | solution.py:115
  10.0 7.8 %copy-start.22 = (bf16[4,128,768]{2,1,0:T(8,128)(2,1)S(1)}, bf16[4,128,768]{2,1,0:T(8,128)(2,1)}, u32[]{:S(2)}) copy-start(bf16[4,128,768]{2,1,0:T(8,128)(2,1)} %get-tuple-element.138) | copy-start | bytes 2359300
  10.0 12.6 %copy-start.58 = (s32[8]{0:T(128)S(1)}, s32[8]{0:T(128)}, u32[]{:S(2)}) copy-start(s32[8]{0:T(128)} %param.21) | copy-start | bytes 100
  10.0 22.4 %copy-start.57 = (bf16[768]{0:T(1024)(128)(2,1)S(1)}, bf16[768]{0:T(1024)(128)(2,1)}, u32[]{:S(2)}) copy-start(bf16[768]{0:T(1024)(128)(2,1)} %param.24) | copy-start | bytes 4612
  12.2 13.5 %collective-permute-start.8 = (bf16[1,128,768]{2,1,0:T(8,128)(2,1)}, bf16[1,128,768]{2,1,0:T(8,128)(2,1)}, u32[]{:S(2)}, u32[]{:S(2)}) collective-permute-start(bf16[1,128,768]{2,1,0:T(8,128)(2,1)} %get-tuple-element.142), channel_id=1, source_target_pairs={{0,3},{1,2},{2,1},{3,0},{4,7},{5,6},{6,5},{7,4},{8,11},{9,10},{10,... | collective-permute-start | bytes 589832 | tf_op jit(solution)/shard_map/ppermute | solution.py:26
  17.2 29.0 %collective-permute-start.7 = (bf16[1,128,768]{2,1,0:T(8,128)(2,1)}, bf16[1,128,768]{2,1,0:T(8,128)(2,1)}, u32[]{:S(2)}, u32[]{:S(2)}) collective-permute-start(bf16[1,128,768]{2,1,0:T(8,128)(2,1)} %get-tuple-element.143), channel_id=1, source_target_pairs={{0,2},{1,3},{2,0},{3,1},{4,6},{5,7},{6,4},{7,5},{8,10},{9,11},{10,... | collective-permute-start | bytes 589832 | tf_op jit(solution)/shard_map/ppermute | solution.py:26
  17.3 31.1 %collective-permute-start.6 = (bf16[1,128,768]{2,1,0:T(8,128)(2,1)}, bf16[1,128,768]{2,1,0:T(8,128)(2,1)}, u32[]{:S(2)}, u32[]{:S(2)}) collective-permute-start(bf16[1,128,768]{2,1,0:T(8,128)(2,1)} %get-tuple-element.144), channel_id=1, source_target_pairs={{0,1},{1,0},{2,3},{3,2},{4,5},{5,4},{6,7},{7,6},{8,9},{9,8},{10,11... | collective-permute-start | bytes 589832 | tf_op jit(solution)/shard_map/ppermute | solution.py:26
  18.7 29.7 %collective-permute-start.2 = (bf16[1,128,768]{2,1,0:T(8,128)(2,1)}, bf16[1,128,768]{2,1,0:T(8,128)(2,1)}, u32[]{:S(2)}, u32[]{:S(2)}) collective-permute-start(bf16[1,128,768]{2,1,0:T(8,128)(2,1)} %get-tuple-element.150), channel_id=1, source_target_pairs={{0,3},{1,2},{2,1},{3,0},{4,7},{5,6},{6,5},{7,4},{8,11},{9,10},{10,... | collective-permute-start | bytes 589832 | tf_op jit(solution)/shard_map/ppermute | solution.py:26
  22.5 46.4 %collective-permute-start.1 = (bf16[1,128,768]{2,1,0:T(8,128)(2,1)}, bf16[1,128,768]{2,1,0:T(8,128)(2,1)}, u32[]{:S(2)}, u32[]{:S(2)}) collective-permute-start(bf16[1,128,768]{2,1,0:T(8,128)(2,1)} %get-tuple-element.151), channel_id=1, source_target_pairs={{0,2},{1,3},{2,0},{3,1},{4,6},{5,7},{6,4},{7,5},{8,10},{9,11},{10,... | collective-permute-start | bytes 589832 | tf_op jit(solution)/shard_map/ppermute | solution.py:26
  25.6 8.7 %copy-start.43 = (pred[512]{0:T(512)(128)(4,1)}, pred[512]{0:T(512)(128)(4,1)S(1)}, u32[]{:S(2)}) copy-start(pred[512]{0:T(512)(128)(4,1)S(1)} %get-tuple-element.98) | copy-start | bytes 1540
  25.6 9.2 %copy-start.45 = (pred[512]{0:T(512)(128)(4,1)}, pred[512]{0:T(512)(128)(4,1)S(1)}, u32[]{:S(2)}) copy-start(pred[512]{0:T(512)(128)(4,1)S(1)} %get-tuple-element.99) | copy-start | bytes 1540
  25.7 43.3 %collective-permute-start = (bf16[1,128,768]{2,1,0:T(8,128)(2,1)}, bf16[1,128,768]{2,1,0:T(8,128)(2,1)}, u32[]{:S(2)}, u32[]{:S(2)}) collective-permute-start(bf16[1,128,768]{2,1,0:T(8,128)(2,1)} %get-tuple-element.152), channel_id=1, source_target_pairs={{0,1},{1,0},{2,3},{3,2},{4,5},{5,4},{6,7},{7,6},{8,9},{9,8},{10,11... | collective-permute-start | bytes 589832 | tf_op jit(solution)/shard_map/ppermute | solution.py:26
  46.1 22.8 %copy-start.20 = (bf16[1,128,768]{2,1,0:T(8,128)(2,1)S(1)}, bf16[1,128,768]{2,1,0:T(8,128)(2,1)}, u32[]{:S(2)}) copy-start(bf16[1,128,768]{2,1,0:T(8,128)(2,1)} %get-tuple-element.149) | copy-start | bytes 589828
  46.1 22.8 %copy-start.21 = (bf16[1,128,768]{2,1,0:T(8,128)(2,1)S(1)}, bf16[1,128,768]{2,1,0:T(8,128)(2,1)}, u32[]{:S(2)}) copy-start(bf16[1,128,768]{2,1,0:T(8,128)(2,1)} %get-tuple-element.141) | copy-start | bytes 589828
  46.1 22.8 %copy-start.44 = (pred[512]{0:T(512)(128)(4,1)S(1)}, pred[512]{0:T(512)(128)(4,1)}, u32[]{:S(2)}) copy-start(pred[512]{0:T(512)(128)(4,1)} %copy-done.43) | copy-start | bytes 1540
  46.1 22.8 %copy-start.46 = (pred[512]{0:T(512)(128)(4,1)S(1)}, pred[512]{0:T(512)(128)(4,1)}, u32[]{:S(2)}) copy-start(pred[512]{0:T(512)(128)(4,1)} %copy-done.45) | copy-start | bytes 1540
  46.2 83.5 %collective-permute-start.5 = (bf16[2,128,768]{2,1,0:T(8,128)(2,1)S(1)}, bf16[2,128,768]{2,1,0:T(8,128)(2,1)S(1)}, u32[]{:S(2)}, u32[]{:S(2)}) collective-permute-start(bf16[2,128,768]{2,1,0:T(8,128)(2,1)S(1)} %get-tuple-element.130), channel_id=1, source_target_pairs={{0,3},{1,2},{2,1},{3,0},{4,7},{5,6},{6,5},{7,4},{8,11},{9,10},{10,... | collective-permute-start | bytes 1179656 | tf_op jit(solution)/shard_map/ppermute | solution.py:26
  48.4 81.4 %collective-permute-start.4 = (bf16[2,128,768]{2,1,0:T(8,128)(2,1)S(1)}, bf16[2,128,768]{2,1,0:T(8,128)(2,1)S(1)}, u32[]{:S(2)}, u32[]{:S(2)}) collective-permute-start(bf16[2,128,768]{2,1,0:T(8,128)(2,1)S(1)} %get-tuple-element.131), channel_id=1, source_target_pairs={{0,2},{1,3},{2,0},{3,1},{4,6},{5,7},{6,4},{7,5},{8,10},{9,11},{10,... | collective-permute-start | bytes 1179656 | tf_op jit(solution)/shard_map/ppermute | solution.py:26
  48.4 81.4 %collective-permute-start.3 = (bf16[2,128,768]{2,1,0:T(8,128)(2,1)S(1)}, bf16[2,128,768]{2,1,0:T(8,128)(2,1)S(1)}, u32[]{:S(2)}, u32[]{:S(2)}) collective-permute-start(bf16[2,128,768]{2,1,0:T(8,128)(2,1)S(1)} %get-tuple-element.132), channel_id=1, source_target_pairs={{0,1},{1,0},{2,3},{3,2},{4,5},{5,4},{6,7},{7,6},{8,9},{9,8},{10,11... | collective-permute-start | bytes 1179656 | tf_op jit(solution)/shard_map/ppermute | solution.py:26
  81.6 8.7 %copy-start.4 = (bf16[512,2304]{1,0:T(8,128)(2,1)}, bf16[512,2304]{1,0:T(8,128)(2,1)S(1)}, u32[]{:S(2)}) copy-start(bf16[512,2304]{1,0:T(8,128)(2,1)S(1)} %fusion.7.q_ref.k_ref.v_ref) | copy-start | bytes 7077892
  81.6 8.7 %copy-start.56 = (f32[768]{0:T(1024)S(1)}, f32[768]{0:T(1024)}, u32[]{:S(2)}) copy-start(f32[768]{0:T(1024)} %convert_element_type.296) | copy-start | bytes 9220
  81.6 8.7 %copy-start.59 = (bf16[768,768]{1,0:T(8,128)(2,1)S(1)}, bf16[768,768]{1,0:T(8,128)(2,1)}, u32[]{:S(2)}) copy-start(bf16[768,768]{1,0:T(8,128)(2,1)} %param.25) | copy-start | bytes 3538948
  99.3 8.8 %copy-start.6 = (bf16[512,2304]{1,0:T(8,128)(2,1)}, bf16[512,2304]{1,0:T(8,128)(2,1)S(1)}, u32[]{:S(2)}) copy-start(bf16[512,2304]{1,0:T(8,128)(2,1)S(1)} %fusion.6.q_ref.k_ref.v_ref) | copy-start | bytes 7077892
  99.4 12.6 %slice-start.4 = ((s8[4718592]{0:T(1024)(128)(4,1)}), s8[4194304]{0:T(1024)(128)(4,1)S(1)}, s32[]{:S(2)}) async-start(s8[4718592]{0:T(1024)(128)(4,1)} %bitcast.202), calls=%async_computation.6 | async-start | bytes 8388608
  111.3 10.9 %slice-start.2 = ((s8[4718592]{0:T(1024)(128)(4,1)}), s8[4194304]{0:T(1024)(128)(4,1)S(1)}, s32[]{:S(2)}) async-start(s8[4718592]{0:T(1024)(128)(4,1)} %bitcast.200), calls=%async_computation.4 | async-start | bytes 8388608
  111.9 39.5 %copy-start.38 = (bf16[512,768]{1,0:T(8,128)(2,1)}, bf16[512,768]{1,0:T(8,128)(2,1)S(1)}, u32[]{:S(2)}) copy-start(bf16[512,768]{1,0:T(8,128)(2,1)S(1)} %get-tuple-element.104) | copy-start | bytes 2359300
  112.0 39.5 %copy-start.40 = (bf16[512,768]{1,0:T(8,128)(2,1)}, bf16[512,768]{1,0:T(8,128)(2,1)S(1)}, u32[]{:S(2)}) copy-start(bf16[512,768]{1,0:T(8,128)(2,1)S(1)} %get-tuple-element.160) | copy-start | bytes 2359300
  112.0 10.2 %copy-start.55 = (f32[768]{0:T(1024)S(1)}, f32[768]{0:T(1024)}, u32[]{:S(2)}) copy-start(f32[768]{0:T(1024)} %convert_element_type.310) | copy-start | bytes 9220
  112.0 10.2 %slice-start.3 = ((s8[4718592]{0:T(1024)(128)(4,1)}), s8[524288]{0:T(1024)(128)(4,1)S(1)}, s32[]{:S(2)}) async-start(s8[4718592]{0:T(1024)(128)(4,1)} %bitcast.200), calls=%async_computation.5 | async-start | bytes 1048576
  129.7 40.5 %copy-start.30 = (bf16[1024,768]{1,0:T(8,128)(2,1)}, bf16[1024,768]{1,0:T(8,128)(2,1)S(1)}, u32[]{:S(2)}) copy-start(bf16[1024,768]{1,0:T(8,128)(2,1)S(1)} %fusion.9) | copy-start | bytes 4718596
  130.8 34.5 %copy-start.18 = (bf16[2,512,768]{2,1,0:T(8,128)(2,1)}, bf16[2,512,768]{2,1,0:T(8,128)(2,1)S(1)}, u32[]{:S(2)}) copy-start(bf16[2,512,768]{2,1,0:T(8,128)(2,1)S(1)} %pad_maximum_fusion.2) | copy-start | bytes 4718596
  145.3 6.2 %copy-start.60 = (bf16[1024,3072]{1,0:T(8,128)(2,1)S(1)}, bf16[1024,3072]{1,0:T(8,128)(2,1)}, u32[]{:S(2)}) copy-start(bf16[1024,3072]{1,0:T(8,128)(2,1)} %get-tuple-element.174) | copy-start | bytes 18874372
  155.5 24.0 %collective-permute-start.9 = (bf16[1536,768]{1,0:T(8,128)(2,1)}, bf16[1536,768]{1,0:T(8,128)(2,1)}, u32[]{:S(2)}, u32[]{:S(2)}) collective-permute-start(bf16[1536,768]{1,0:T(8,128)(2,1)} %convolution_convert_fusion.2), channel_id=1, source_target_pairs={{0,4},{4,0},{8,12},{12,8},{16,20},{20,16},{24,28},{28,24},{1,5},{5... | collective-permute-start | bytes 7077896 | tf_op jit(solution)/shard_map/ppermute | solution.py:26
  155.5 31.6 %collective-permute-start.11 = (bf16[768,1536]{1,0:T(8,128)(2,1)}, bf16[768,1536]{1,0:T(8,128)(2,1)}, u32[]{:S(2)}, u32[]{:S(2)}) collective-permute-start(bf16[768,1536]{1,0:T(8,128)(2,1)} %convolution_convert_fusion.1), channel_id=1, source_target_pairs={{0,4},{4,0},{8,12},{12,8},{16,20},{20,16},{24,28},{28,24},{1,5},{5... | collective-permute-start | bytes 7077896 | tf_op jit(solution)/shard_map/ppermute | solution.py:26
  171.3 35.9 %collective-permute-start.15 = (bf16[2,128,768]{2,1,0:T(8,128)(2,1)}, bf16[2,128,768]{2,1,0:T(8,128)(2,1)}, u32[]{:S(2)}, u32[]{:S(2)}) collective-permute-start(bf16[2,128,768]{2,1,0:T(8,128)(2,1)} %get-tuple-element.134), channel_id=1, source_target_pairs={{0,1},{1,0},{2,3},{3,2},{4,5},{5,4},{6,7},{7,6},{8,9},{9,8},{10,11... | collective-permute-start | bytes 1179656 | tf_op jit(solution)/shard_map/ppermute | solution.py:26
  171.3 35.9 %collective-permute-start.14 = (bf16[2,128,768]{2,1,0:T(8,128)(2,1)}, bf16[2,128,768]{2,1,0:T(8,128)(2,1)}, u32[]{:S(2)}, u32[]{:S(2)}) collective-permute-start(bf16[2,128,768]{2,1,0:T(8,128)(2,1)} %get-tuple-element.135), channel_id=1, source_target_pairs={{0,2},{1,3},{2,0},{3,1},{4,6},{5,7},{6,4},{7,5},{8,10},{9,11},{10,... | collective-permute-start | bytes 1179656 | tf_op jit(solution)/shard_map/ppermute | solution.py:26
  174.5 32.7 %collective-permute-start.13 = (bf16[2,128,768]{2,1,0:T(8,128)(2,1)}, bf16[2,128,768]{2,1,0:T(8,128)(2,1)}, u32[]{:S(2)}, u32[]{:S(2)}) collective-permute-start(bf16[2,128,768]{2,1,0:T(8,128)(2,1)} %get-tuple-element.136), channel_id=1, source_target_pairs={{0,3},{1,2},{2,1},{3,0},{4,7},{5,6},{6,5},{7,4},{8,11},{9,10},{10,... | collective-permute-start | bytes 1179656 | tf_op jit(solution)/shard_map/ppermute | solution.py:26
  185.6 27.1 %collective-permute-start.10 = (bf16[2,2,2,96,768]{4,3,1,2,0:T(8,128)(2,1)S(1)}, bf16[2,2,2,96,768]{4,3,1,2,0:T(8,128)(2,1)S(1)}, u32[]{:S(2)}, u32[]{:S(2)}) collective-permute-start(bf16[2,2,2,96,768]{4,3,1,2,0:T(8,128)(2,1)S(1)} %bitcast.188), channel_id=1, source_target_pairs={{0,8},{4,12},{8,0},{12,4},{16,24},{20,28},{24,16},{28,20},{1,9},{5... | collective-permute-start | bytes 3538952 | tf_op jit(solution)/shard_map/ppermute | solution.py:26
  192.6 26.8 %collective-permute-start.12 = (bf16[2,2,2,48,1536]{4,3,1,2,0:T(8,128)(2,1)S(1)}, bf16[2,2,2,48,1536]{4,3,1,2,0:T(8,128)(2,1)S(1)}, u32[]{:S(2)}, u32[]{:S(2)}) collective-permute-start(bf16[2,2,2,48,1536]{4,3,1,2,0:T(8,128)(2,1)S(1)} %bitcast.189), channel_id=1, source_target_pairs={{0,16},{4,20},{8,24},{12,28},{16,0},{20,4},{24,8},{28,12},{1,17},{... | collective-permute-start | bytes 3538952 | tf_op jit(solution)/shard_map/ppermute | solution.py:26
  219.9 46.0 %collective-permute-start.17 = (bf16[2,2,48,1536]{3,2,0,1:T(8,128)(2,1)S(1)}, bf16[2,2,48,1536]{3,2,0,1:T(8,128)(2,1)S(1)}, u32[]{:S(2)}, u32[]{:S(2)}) collective-permute-start(bf16[2,2,48,1536]{3,2,0,1:T(8,128)(2,1)S(1)} %dynamic-slice_bitcast_fusion.1), channel_id=1, source_target_pairs={{0,8},{4,12},{8,0},{12,4},{16,24},{20,28},{24,16},{28,20},{1,9},{5... | collective-permute-start | bytes 1769480 | tf_op jit(solution)/shard_map/ppermute | solution.py:26
  221.4 44.7 %collective-permute-start.16 = (bf16[2,2,96,768]{3,2,0,1:T(8,128)(2,1)S(1)}, bf16[2,2,96,768]{3,2,0,1:T(8,128)(2,1)S(1)}, u32[]{:S(2)}, u32[]{:S(2)}) collective-permute-start(bf16[2,2,96,768]{3,2,0,1:T(8,128)(2,1)S(1)} %dynamic-slice_bitcast_fusion.2), channel_id=1, source_target_pairs={{0,16},{4,20},{8,24},{12,28},{16,0},{20,4},{24,8},{28,12},{1,17},{... | collective-permute-start | bytes 1769480 | tf_op jit(solution)/shard_map/ppermute | solution.py:26
  272.0 28.6 %collective-permute-start.18 = (bf16[384,2304]{1,0:T(8,128)(2,1)}, bf16[384,2304]{1,0:T(8,128)(2,1)}, u32[]{:S(2)}, u32[]{:S(2)}) collective-permute-start(bf16[384,2304]{1,0:T(8,128)(2,1)} %convolution_convert_fusion), channel_id=1, source_target_pairs={{0,4},{4,0},{8,12},{12,8},{16,20},{20,16},{24,28},{28,24},{1,5},{5... | collective-permute-start | bytes 5308424 | tf_op jit(solution)/shard_map/ppermute | solution.py:26
  282.6 18.1 %slice-start = ((s8[4718592]{0:T(1024)(128)(4,1)}), s8[4194304]{0:T(1024)(128)(4,1)S(1)}, s32[]{:S(2)}) async-start(s8[4718592]{0:T(1024)(128)(4,1)} %bitcast.170), calls=%async_computation.2 | async-start | bytes 8388608
  283.9 15.8 %copy-start.19 = (bf16[2,2,192,768]{3,2,0,1:T(8,128)(2,1)S(1)}, bf16[2,2,192,768]{3,2,0,1:T(8,128)(2,1)}, u32[]{:S(2)}) copy-start(bf16[2,2,192,768]{3,2,0,1:T(8,128)(2,1)} %pad_maximum_fusion.6) | copy-start | bytes 3538948
  283.9 16.8 %slice-start.1 = ((s8[4718592]{0:T(1024)(128)(4,1)}), s8[524288]{0:T(1024)(128)(4,1)S(1)}, s32[]{:S(2)}) async-start(s8[4718592]{0:T(1024)(128)(4,1)} %bitcast.170), calls=%async_computation.3 | async-start | bytes 1048576
  283.9 15.8 %collective-permute-start.19 = (bf16[2,192,768]{2,1,0:T(8,128)(2,1)S(1)}, bf16[2,192,768]{2,1,0:T(8,128)(2,1)S(1)}, u32[]{:S(2)}, u32[]{:S(2)}) collective-permute-start(bf16[2,192,768]{2,1,0:T(8,128)(2,1)S(1)} %dynamic-slice_bitcast_fusion), channel_id=1, source_target_pairs={{0,1},{1,0},{2,3},{3,2},{4,5},{5,4},{6,7},{7,6},{8,9},{9,8},{10,11... | collective-permute-start | bytes 1769480 | tf_op jit(solution)/shard_map/ppermute | solution.py:26
  290.1 10.6 %copy-start.34 = (bf16[512,768]{1,0:T(8,128)(2,1)S(1)}, bf16[512,768]{1,0:T(8,128)(2,1)}, u32[]{:S(2)}) copy-start(bf16[512,768]{1,0:T(8,128)(2,1)} %copy-done.32) | copy-start | bytes 2359300
  290.1 10.6 %copy-start.37 = (bf16[512,768]{1,0:T(8,128)(2,1)S(1)}, bf16[512,768]{1,0:T(8,128)(2,1)}, u32[]{:S(2)}) copy-start(bf16[512,768]{1,0:T(8,128)(2,1)} %copy-done.35) | copy-start | bytes 2359300
  300.7 5.0 copy-start.15
  324.5 8.1 %copy-start.52 = (pred[1024]{0:T(1024)(128)(4,1)S(1)}, pred[1024]{0:T(1024)(128)(4,1)}, u32[]{:S(2)}) copy-start(pred[1024]{0:T(1024)(128)(4,1)} %add_reduce_fusion) | copy-start | bytes 3076
  330.1 18.5 %collective-permute-start.20 = (bf16[768,768]{1,0:T(8,128)(2,1)}, bf16[768,768]{1,0:T(8,128)(2,1)}, u32[]{:S(2)}, u32[]{:S(2)}) collective-permute-start(bf16[768,768]{1,0:T(8,128)(2,1)} %get-tuple-element.175), channel_id=1, source_target_pairs={{0,4},{4,0},{8,12},{12,8},{16,20},{20,16},{24,28},{28,24},{1,5},{5... | collective-permute-start | bytes 3538952 | tf_op jit(solution)/shard_map/ppermute | solution.py:26
  331.1 16.7 %copy-start.23 = (bf16[2,192,768]{2,1,0:T(8,128)(2,1)S(1)}, bf16[2,192,768]{2,1,0:T(8,128)(2,1)}, u32[]{:S(2)}) copy-start(bf16[2,192,768]{2,1,0:T(8,128)(2,1)} %fusion.28) | copy-start | bytes 1769476
  331.1 16.7 %collective-permute-start.21 = (bf16[192,768]{1,0:T(8,128)(2,1)S(1)}, bf16[192,768]{1,0:T(8,128)(2,1)S(1)}, u32[]{:S(2)}, u32[]{:S(2)}) collective-permute-start(bf16[192,768]{1,0:T(8,128)(2,1)S(1)} %dynamic-slice_bitcast_fusion.10), channel_id=1, source_target_pairs={{0,2},{1,3},{2,0},{3,1},{4,6},{5,7},{6,4},{7,5},{8,10},{9,11},{10,... | collective-permute-start | bytes 884744 | tf_op jit(solution)/shard_map/ppermute | solution.py:26
  351.6 177.9 %all-gather.7.cloned.1.call-start = ((), (), s32[]{:S(2)}) async-start(), calls=%async_computation.1 | async-start | bytes 6082560 | tf_op jit(solution)/shard_map/all_gather | solution.py:115
  353.2 17.4 %collective-permute-start.27 = (bf16[2,2,2,48,768]{4,3,1,2,0:T(8,128)(2,1)S(1)}, bf16[2,2,2,48,768]{4,3,1,2,0:T(8,128)(2,1)S(1)}, u32[]{:S(2)}, u32[]{:S(2)}) collective-permute-start(bf16[2,2,2,48,768]{4,3,1,2,0:T(8,128)(2,1)S(1)} %bitcast.191), channel_id=1, source_target_pairs={{0,16},{4,20},{8,24},{12,28},{16,0},{20,4},{24,8},{28,12},{1,17},{... | collective-permute-start | bytes 1769480 | tf_op jit(solution)/shard_map/ppermute | solution.py:26
  354.0 24.7 %collective-permute-start.25 = (bf16[2,2,2,24,2304]{4,3,1,2,0:T(8,128)(2,1)S(1)}, bf16[2,2,2,24,2304]{4,3,1,2,0:T(8,128)(2,1)S(1)}, u32[]{:S(2)}, u32[]{:S(2)}) collective-permute-start(bf16[2,2,2,24,2304]{4,3,1,2,0:T(8,128)(2,1)S(1)} %bitcast.190), channel_id=1, source_target_pairs={{0,8},{4,12},{8,0},{12,4},{16,24},{20,28},{24,16},{28,20},{1,9},{5... | collective-permute-start | bytes 2654216 | tf_op jit(solution)/shard_map/ppermute | solution.py:26
  370.8 16.8 %collective-permute-start.28 = (bf16[2,2,48,768]{3,2,0,1:T(8,128)(2,1)S(1)}, bf16[2,2,48,768]{3,2,0,1:T(8,128)(2,1)S(1)}, u32[]{:S(2)}, u32[]{:S(2)}) collective-permute-start(bf16[2,2,48,768]{3,2,0,1:T(8,128)(2,1)S(1)} %dynamic-slice_bitcast_fusion.9), channel_id=1, source_target_pairs={{0,8},{4,12},{8,0},{12,4},{16,24},{20,28},{24,16},{28,20},{1,9},{5... | collective-permute-start | bytes 884744 | tf_op jit(solution)/shard_map/ppermute | solution.py:26
  379.0 13.9 %collective-permute-start.26 = (bf16[2,2,24,2304]{3,2,0,1:T(8,128)(2,1)S(1)}, bf16[2,2,24,2304]{3,2,0,1:T(8,128)(2,1)S(1)}, u32[]{:S(2)}, u32[]{:S(2)}) collective-permute-start(bf16[2,2,24,2304]{3,2,0,1:T(8,128)(2,1)S(1)} %dynamic-slice_bitcast_fusion.3), channel_id=1, source_target_pairs={{0,16},{4,20},{8,24},{12,28},{16,0},{20,4},{24,8},{28,12},{1,17},{... | collective-permute-start | bytes 1327112 | tf_op jit(solution)/shard_map/ppermute | solution.py:26
  393.2 12.0 %collective-permute-start.29 = (bf16[2,120,768]{2,1,0:T(8,128)(2,1)S(1)}, bf16[2,120,768]{2,1,0:T(8,128)(2,1)S(1)}, u32[]{:S(2)}, u32[]{:S(2)}) collective-permute-start(bf16[2,120,768]{2,1,0:T(8,128)(2,1)S(1)} %dynamic-slice_bitcast_fusion.7), channel_id=1, source_target_pairs={{0,1},{1,0},{2,3},{3,2},{4,5},{5,4},{6,7},{7,6},{8,9},{9,8},{10,11... | collective-permute-start | bytes 1105928 | tf_op jit(solution)/shard_map/ppermute | solution.py:26
  405.3 22.2 %collective-permute-start.30 = (bf16[120,768]{1,0:T(8,128)(2,1)S(1)}, bf16[120,768]{1,0:T(8,128)(2,1)S(1)}, u32[]{:S(2)}, u32[]{:S(2)}) collective-permute-start(bf16[120,768]{1,0:T(8,128)(2,1)S(1)} %dynamic-slice_bitcast_fusion.11), channel_id=1, source_target_pairs={{0,2},{1,3},{2,0},{3,1},{4,6},{5,7},{6,4},{7,5},{8,10},{9,11},{10,... | collective-permute-start | bytes 552968 | tf_op jit(solution)/shard_map/ppermute | solution.py:26
  445.1 20.7 %collective-permute-start.24 = (bf16[2,128,768]{2,1,0:T(8,128)(2,1)S(1)}, bf16[2,128,768]{2,1,0:T(8,128)(2,1)S(1)}, u32[]{:S(2)}, u32[]{:S(2)}) collective-permute-start(bf16[2,128,768]{2,1,0:T(8,128)(2,1)S(1)} %get-tuple-element.126), channel_id=1, source_target_pairs={{0,1},{1,0},{2,3},{3,2},{4,5},{5,4},{6,7},{7,6},{8,9},{9,8},{10,11... | collective-permute-start | bytes 1179656 | tf_op jit(solution)/shard_map/ppermute | solution.py:26
  445.1 32.6 %collective-permute-start.23 = (bf16[2,128,768]{2,1,0:T(8,128)(2,1)S(1)}, bf16[2,128,768]{2,1,0:T(8,128)(2,1)S(1)}, u32[]{:S(2)}, u32[]{:S(2)}) collective-permute-start(bf16[2,128,768]{2,1,0:T(8,128)(2,1)S(1)} %get-tuple-element.127), channel_id=1, source_target_pairs={{0,2},{1,3},{2,0},{3,1},{4,6},{5,7},{6,4},{7,5},{8,10},{9,11},{10,... | collective-permute-start | bytes 1179656 | tf_op jit(solution)/shard_map/ppermute | solution.py:26
  447.1 30.7 %collective-permute-start.22 = (bf16[2,128,768]{2,1,0:T(8,128)(2,1)S(1)}, bf16[2,128,768]{2,1,0:T(8,128)(2,1)S(1)}, u32[]{:S(2)}, u32[]{:S(2)}) collective-permute-start(bf16[2,128,768]{2,1,0:T(8,128)(2,1)S(1)} %get-tuple-element.128), channel_id=1, source_target_pairs={{0,3},{1,2},{2,1},{3,0},{4,7},{5,6},{6,5},{7,4},{8,11},{9,10},{10,... | collective-permute-start | bytes 1179656 | tf_op jit(solution)/shard_map/ppermute | solution.py:26
  (36 other events, 84.7 us)
Sparse Core Ops, SparseCore 0:
  351.8 91.8 all-gather.4
  447.1 82.3 all-gather.6

commit v3 on v1

v3 whole, which is shorter than its diff:
```python
import functools

import jax
import jax.numpy as jnp
from jax import lax
from jax.experimental import pallas as pl
from jax.experimental.pallas import tpu as pltpu
from jax.sharding import PartitionSpec as P

HEADS = 12
LANES = 128
NORM_EPS = 1e-06
ROOT_HALF = 0.7071067811865476
ROOT_TWO_PI = 2.5066282746310002
LOG2_E = 1.4426950408889634
F32 = jnp.float32
BF16 = jnp.bfloat16
VMEM_LIMIT = 60 * 2**20


def contract(a, b, da, db):
    return lax.dot_general(a, b, (((da,), (db,)), ((), ())), preferred_element_type=F32)


def call(kernel, *, grid, in_specs, out_specs, out_shape, scratch=(), prefetch=0, flops=0, moved=0, exps=0, share=1):
    return pl.pallas_call(
        kernel,
        grid_spec=pltpu.PrefetchScalarGridSpec(
            num_scalar_prefetch=prefetch,
            grid=grid,
            in_specs=in_specs,
            out_specs=out_specs,
            scratch_shapes=scratch,
        ),
        out_shape=out_shape,
        cost_estimate=pl.CostEstimate(
            flops=int(flops) // share, bytes_accessed=int(moved) // share, transcendentals=int(exps) // share
        ),
        compiler_params=pltpu.CompilerParams(vmem_limit_bytes=VMEM_LIMIT),
    )


def fixed(shape):
    return pl.BlockSpec(shape, lambda *_: (0,) * len(shape), pipeline_mode=pl.Buffered(1))


def shaped(shape, dtype):
    return jax.ShapeDtypeStruct(shape, dtype)


def norm_parts(values):
    centred = values - jnp.mean(values, -1, keepdims=True)
    spread = jnp.mean(centred * centred, -1, keepdims=True)
    inverse = lax.rsqrt(spread + NORM_EPS)
    return centred * inverse, inverse


def norm_backward(grad_norm, unit, inverse, gains):
    scaled = grad_norm * gains
    return inverse * (
        scaled
        - jnp.mean(scaled, -1, keepdims=True)
        - unit * jnp.mean(scaled * unit, -1, keepdims=True)
    )


def project_kernel(*refs, tm):
    blocks = refs[:tm]
    mask_ref, embed_ref, pos_ref, gain_ref, shift_ref, w_ref, bias_ref, filled_ref, turned_ref, joint_ref, normed_s = refs[tm:]

    @pl.when(pl.program_id(0) == 0)
    def _():
        seg = blocks[0].shape[0]
        embed, gain, shift = (r[...].astype(F32) for r in (embed_ref, gain_ref, shift_ref))
        for d in range(tm):
            rows = slice(d * seg, (d + 1) * seg)
            filled = jnp.where(mask_ref[rows] > 0.5, embed, blocks[d][...].astype(F32)) + pos_ref[rows].astype(F32)
            unit, _ = norm_parts(filled)
            normed = (unit * gain + shift).astype(BF16)
            filled_ref[rows] = filled
            normed_s[rows] = normed
            turned_ref[:, rows] = normed.T

    joint_ref[...] = (contract(normed_s[...], w_ref[...], 1, 0) + bias_ref[...].astype(F32)).astype(BF16)


def project(blocks, mask, embed, pos, gain, shift, w_qkv, bias):
    tm = len(blocks)
    seg, width = blocks[0].shape
    rows = tm * seg
    return call(
        functools.partial(project_kernel, tm=tm),
        grid=(3,),
        in_specs=[fixed((seg, width))] * tm
        + [fixed((rows, 1)), fixed((1, width)), fixed((rows, width)), fixed((1, width)), fixed((1, width))]
        + [pl.BlockSpec((width, width), lambda j: (0, j)), pl.BlockSpec((1, width), lambda j: (0, j))],
        out_specs=[
            pl.BlockSpec((rows, width), lambda j: (0, 0)),
            pl.BlockSpec((width, rows), lambda j: (0, 0)),
            pl.BlockSpec((rows, width), lambda j: (0, j)),
        ],
        out_shape=[shaped((rows, width), F32), shaped((width, rows), BF16), shaped((rows, 3 * width), BF16)],
        scratch=[pltpu.VMEM((rows, width), BF16)],
        flops=6 * rows * width * width,
        moved=20 * rows * width,
    )(*blocks, mask, embed, pos, gain, shift, w_qkv, bias)


def own_lanes(value, i, head):
    lane = lax.broadcasted_iota(jnp.int32, value.shape, 1)
    return jnp.where((lane >= i * head) & (lane < (i + 1) * head), value, jnp.zeros_like(value))


def attend_kernel(q_ref, k_ref, v_ref, o_ref, turned_ref, log_ref, *, head):
    factor = head**-0.5 * LOG2_E
    for pair in range(q_ref.shape[1] // LANES):
        lanes = slice(pair * LANES, (pair + 1) * LANES)
        q, k, v = q_ref[:, lanes], k_ref[:, lanes], v_ref[:, lanes]
        outs = []
        for i in range(LANES // head):
            scores = contract(k, own_lanes(q, i, head), 1, 1)
            peak = jnp.max(scores, 0, keepdims=True)
            raised = jnp.exp2((scores - peak) * factor)
            total = jnp.sum(raised, 0, keepdims=True)
            mixed = contract(v, raised.astype(BF16), 0, 0)
            outs.append(mixed[i * head : (i + 1) * head] * (1.0 / total))
            log_ref[pair, i : i + 1, :] = peak * factor + jnp.log2(total)
        turned = jnp.concatenate(outs, 0)
        turned_ref[lanes] = turned.astype(BF16)
        o_ref[:, lanes] = turned.T.astype(BF16)


def attend(joint, width):
    rows = joint.shape[0]
    head = width // HEADS
    pairs, per = width // LANES, LANES // head
    some = 2 if pairs % 2 == 0 else 1
    steps = pairs // some
    block = lambda off: pl.BlockSpec((rows, some * LANES), lambda h: (0, h + off))
    return call(
        functools.partial(attend_kernel, head=head),
        grid=(steps,),
        in_specs=[block(0), block(steps), block(2 * steps)],
        out_specs=[
            block(0),
            pl.BlockSpec((some * LANES, rows), lambda h: (h, 0)),
            pl.BlockSpec((some, per, rows), lambda h: (h, 0, 0)),
        ],
        out_shape=[shaped((rows, width), BF16), shaped((width, rows), BF16), shaped((pairs, per, rows), F32)],
        flops=16 * rows * rows * width,
        moved=8 * rows * width,
        exps=rows * rows * HEADS,
    )(joint, joint, joint)


def attend_back_kernel(side_ref, *refs, head, groups):
    per_clip = [refs[4 * c : 4 * c + 4] for c in range(groups)]
    g_ref, out_ref = refs[4 * groups :]
    scale = head**-0.5
    for c, (q_ref, k_ref, v_ref, log_ref) in enumerate(per_clip):
        rows = slice(c * q_ref.shape[0], (c + 1) * q_ref.shape[0])
        q, k, v, g = q_ref[...], k_ref[...], v_ref[...], g_ref[rows]
        grad_q, grad_k, grad_v = [], 0.0, 0.0
        for i in range(q.shape[1] // head):
            q_own, g_own = own_lanes(q, i, head), own_lanes(g, i, head)
            scores = contract(k, q_own, 1, 1)
            probs = jnp.exp2(scores * (scale * LOG2_E) - log_ref[0, i : i + 1, :])
            grad_probs = contract(v, g_own, 1, 1)
            delta = jnp.sum(probs * grad_probs, 0, keepdims=True)
            grad_scores = (probs * (grad_probs - delta)).astype(BF16)
            grad_q.append(contract(k, grad_scores, 0, 0)[i * head : (i + 1) * head])
            grad_k = grad_k + contract(grad_scores, q_own, 1, 0)
            grad_v = grad_v + contract(probs.astype(BF16), g_own, 1, 0)
        out_ref[0, rows] = (jnp.concatenate(grad_q, 0) * scale).T.astype(BF16)
        out_ref[1, rows] = (grad_k * scale).astype(BF16)
        out_ref[2, rows] = grad_v.astype(BF16)


def attend_back(side, joints, mix, logs):
    rows, width = mix.shape
    groups = len(joints)
    length = rows // groups
    head = width // HEADS
    pairs, per = width // LANES, LANES // head
    half = pairs // 2

    def block(off):
        return pl.BlockSpec((length, LANES), lambda h, s: (0, off + s[0] * half + h))

    clip = [block(0), block(pairs), block(2 * pairs), pl.BlockSpec((1, per, length), lambda h, s: (s[0] * half + h, 0, 0))]
    operands = []
    for joint, log_sum in zip(joints, logs):
        operands += [joint, joint, joint, log_sum]
    return call(
        functools.partial(attend_back_kernel, head=head, groups=groups),
        prefetch=1,
        share=16,
        grid=(half,),
        in_specs=clip * groups + [pl.BlockSpec((rows, LANES), lambda h, s: (0, s[0] * half + h))],
        out_specs=pl.BlockSpec((3, rows, LANES), lambda h, s: (0, 0, h)),
        out_shape=shaped((3, rows, width // 2), BF16),
        flops=20 * rows * length * width,
        moved=8 * rows * width,
        exps=rows * length * HEADS // 2,
    )(side, *operands, mix)


def gelu_parts(u):
    phi = 0.5 * (1.0 + lax.erf(u * ROOT_HALF))
    return u * phi, phi + u * jnp.exp(-0.5 * u * u) * (1.0 / ROOT_TWO_PI)


def forward_kernel(*refs, groups, chunk):
    filled, attended = refs[:groups], refs[groups : 2 * groups]
    (w_out_ref, out_bias_ref, gain_ref, shift_ref, down_bias_ref, w_up_ref, up_bias_ref, w_down_ref,
     hidden_ref, turned_ref, act_ref, slope_ref, block_ref, out_s, normed_s) = refs[2 * groups :]
    rows_all = out_s.shape[0]
    step, last = pl.program_id(0), pl.num_programs(0) - 1

    @pl.when(step == 0)
    def _():
        gain, shift = gain_ref[...].astype(F32), shift_ref[...].astype(F32)
        out_bias, down_bias = out_bias_ref[...].astype(F32), down_bias_ref[...].astype(F32)
        length = filled[0].shape[0]
        for c in range(groups):
            rows = slice(c * length, (c + 1) * length)
            hidden = filled[c][...] + contract(attended[c][...], w_out_ref[...], 1, 0) + out_bias
            unit, _ = norm_parts(hidden)
            normed = (unit * gain + shift).astype(BF16)
            hidden_ref[rows] = hidden
            normed_s[rows] = normed
            turned_ref[:, rows] = normed.T
            out_s[rows] = hidden + down_bias

    w_up, w_down = w_up_ref[...], w_down_ref[...]
    bias = up_bias_ref[...].astype(F32)
    for r in range(rows_all // chunk):
        rows = slice(r * chunk, (r + 1) * chunk)
        value, slope = gelu_parts(contract(normed_s[rows], w_up, 1, 0) + bias)
        act = value.astype(BF16)
        act_ref[:, rows] = act.T
        slope_ref[rows] = slope.astype(BF16)
        out_s[rows] += contract(act, w_down, 1, 0)

    @pl.when(step == last)
    def _():
        block_ref[...] = out_s[...].astype(BF16)


def forward(filled, attended, w_out, out_bias, gain, shift, down_bias, w_up, up_bias, w_down, tile, chunk):
    groups, (length, width) = len(filled), filled[0].shape
    rows, ff = groups * length, w_up.shape[1]
    vec = fixed((1, width))
    whole = pl.BlockSpec((rows, width), lambda j: (0, 0), pipeline_mode=pl.Buffered(1))
    column = pl.BlockSpec((rows, tile), lambda j: (0, j))
    return call(
        functools.partial(forward_kernel, groups=groups, chunk=chunk),
        grid=(ff // tile,),
        in_specs=[fixed((length, width))] * (2 * groups)
        + [fixed((width, width)), vec, vec, vec, vec]
        + [
            pl.BlockSpec((width, tile), lambda j: (0, j)),
            pl.BlockSpec((1, tile), lambda j: (0, j)),
            pl.BlockSpec((tile, width), lambda j: (j, 0)),
        ],
        out_specs=[whole, fixed((width, rows)), pl.BlockSpec((tile, rows), lambda j: (j, 0)), column, whole],
        out_shape=[shaped((rows, width), F32), shaped((width, rows), BF16)]
        + [shaped((ff, rows), BF16), shaped((rows, ff), BF16)]
        + [shaped((rows, width), BF16)],
        scratch=[pltpu.VMEM((rows, width), F32), pltpu.VMEM((rows, width), BF16)],
        flops=4 * rows * width * ff + 2 * rows * width * width,
        moved=14 * rows * width + 4 * rows * ff + 4 * width * ff,
        exps=rows * ff,
    )(*filled, *attended, w_out, out_bias, gain, shift, down_bias, w_up, up_bias, w_down)


def tile_back(turned_ref, cot_ref, act_ref, slope_ref, w_up_ref, w_down_ref, gup_s, norm_s, down_ref, up_ref, bias_ref, chunk):
    w_up, w_down = w_up_ref[...], w_down_ref[...]
    total = jnp.zeros(bias_ref.shape, F32)
    for r in range(cot_ref.shape[0] // chunk):
        rows = slice(r * chunk, (r + 1) * chunk)
        gup = (contract(cot_ref[rows], w_down, 1, 1) * slope_ref[rows].astype(F32)).astype(BF16)
        gup_s[rows] = gup
        total = total + jnp.sum(gup.astype(F32), 0, keepdims=True)
        norm_s[rows] += contract(gup, w_up, 1, 1)
    bias_ref[...] = total
    down_ref[...] = contract(act_ref[...], cot_ref[...], 1, 0).astype(BF16)
    up_ref[...] = contract(turned_ref[...], gup_s[...], 1, 0).astype(BF16)


def back_first_kernel(side_ref, turned_ref, cot_ref, act_ref, slope_ref, w_up_ref, w_down_ref, norm_ref, down_ref, up_ref, bias_ref, gup_s, *, chunk):
    @pl.when(pl.program_id(0) == 0)
    def _():
        norm_ref[...] = jnp.zeros_like(norm_ref)

    tile_back(turned_ref, cot_ref, act_ref, slope_ref, w_up_ref, w_down_ref, gup_s, norm_ref, down_ref, up_ref, bias_ref, chunk)


def back_last_kernel(side_ref, *refs, groups, chunk):
    attended = refs[:groups]
    (turned_ref, cot_ref, act_ref, slope_ref, w_up_ref, w_down_ref, w_out_ref, gain_ref, hidden_ref, norm_ref,
     down_ref, up_ref, bias_ref, grad_hidden_ref, mix_ref, grad_out_ref, sums_ref, gup_s, norm_s, branch_s) = refs[groups:]

    @pl.when(pl.program_id(0) == 0)
    def _():
        norm_s[...] = norm_ref[...]

    tile_back(turned_ref, cot_ref, act_ref, slope_ref, w_up_ref, w_down_ref, gup_s, norm_s, down_ref, up_ref, bias_ref, chunk)

    @pl.when(pl.program_id(0) == pl.num_programs(0) - 1)
    def _():
        gain = gain_ref[...].astype(F32)
        total = [jnp.zeros_like(gain) for _ in range(4)]
        w_out = w_out_ref[...]
        for r in range(norm_s.shape[0] // chunk):
            rows = slice(r * chunk, (r + 1) * chunk)
            unit, inverse = norm_parts(hidden_ref[rows])
            top, grad_norm = cot_ref[rows].astype(F32), norm_s[rows]
            grad_hidden = top + norm_backward(grad_norm, unit, inverse, gain)
            grad_hidden_ref[rows] = grad_hidden
            branch = grad_hidden.astype(BF16)
            branch_s[rows] = branch
            mix_ref[rows] = contract(branch, w_out, 1, 1).astype(BF16)
            parts = (branch.astype(F32), top, grad_norm * unit, grad_norm)
            total = [t + jnp.sum(p, 0, keepdims=True) for t, p in zip(total, parts)]
        sums_ref[...] = jnp.concatenate(total + [jnp.zeros_like(gain)] * 4, 0)
        length = attended[0].shape[1]
        grad_out = 0.0
        for c in range(groups):
            grad_out = grad_out + contract(attended[c][...], branch_s[c * length : (c + 1) * length], 1, 0)
        grad_out_ref[...] = grad_out.astype(BF16)


def back_specs(rows, width, half, tile):
    steps = half // tile
    column = lambda n: pl.BlockSpec((n, tile), lambda j, s: (0, s[0] * steps + j))
    ins = [fixed((width, rows)), fixed((rows, width))]
    ins += [pl.BlockSpec((tile, rows), lambda j, s: (s[0] * steps + j, 0)), column(rows), column(width)]
    ins.append(pl.BlockSpec((tile, width), lambda j, s: (s[0] * steps + j, 0)))
    outs = [
        pl.BlockSpec((tile, width), lambda j, s: (j, 0)),
        pl.BlockSpec((width, tile), lambda j, s: (0, j)),
        pl.BlockSpec((1, tile), lambda j, s: (0, j)),
    ]
    return ins, outs, [shaped((half, width), BF16), shaped((width, half), BF16), shaped((1, half), F32)]


def back_first(side, normed, cot, act, slope, w_up, w_down, tile, chunk):
    rows, width = cot.shape
    half = w_up.shape[1] // 2
    ins, outs, shapes = back_specs(rows, width, half, tile)
    return call(
        functools.partial(back_first_kernel, chunk=chunk),
        prefetch=1,
        grid=(half // tile,),
        in_specs=ins,
        out_specs=[fixed((rows, width))] + outs,
        out_shape=[shaped((rows, width), F32)] + shapes,
        scratch=[pltpu.VMEM((rows, tile), BF16)],
        flops=8 * rows * width * half,
        moved=8 * rows * width + 4 * rows * half + 8 * width * half,
    )(side, normed, cot, act, slope, w_up, w_down)


def back_last(side, attended, normed, cot, act, slope, w_up, w_down, w_out, gain, hidden, norm, tile, chunk):
    rows, width = cot.shape
    groups = len(attended)
    half = w_up.shape[1] // 2
    ins, outs, shapes = back_specs(rows, width, half, tile)
    whole = lambda n: fixed((n, width))
    return call(
        functools.partial(back_last_kernel, groups=groups, chunk=chunk),
        prefetch=1,
        grid=(half // tile,),
        in_specs=[fixed((width, rows // groups))] * groups + ins + [whole(width), whole(1), whole(rows), whole(rows)],
        out_specs=outs + [whole(rows), whole(rows), whole(width), whole(8)],
        out_shape=shapes
        + [shaped((rows, width), F32), shaped((rows, width), BF16), shaped((width, width), BF16), shaped((8, width), F32)],
        scratch=[pltpu.VMEM((rows, tile), BF16), pltpu.VMEM((rows, width), F32), pltpu.VMEM((rows, width), BF16)],
        flops=8 * rows * width * half + 4 * rows * width * width,
        moved=20 * rows * width + 4 * rows * half + 8 * width * half,
    )(side, *attended, normed, cot, act, slope, w_up, w_down, w_out, gain, hidden, norm)


def joint_part(normed, grad_ref, grad_w_ref, bias_ref):
    length = normed[0].shape[1]
    grad_w = 0.0
    for c, normed_ref in enumerate(normed):
        grad_w = grad_w + contract(normed_ref[...], grad_ref[0, c * length : (c + 1) * length], 1, 0)
    grad_w_ref[...] = grad_w.astype(BF16)
    bias_ref[0] = jnp.sum(grad_ref[0].astype(F32), 0, keepdims=True)


def joint_first_kernel(side_ref, *refs, groups):
    normed, (grad_ref, weight_ref, grad_w_ref, bias_ref, acc_ref) = refs[:groups], refs[groups:]
    joint_part(normed, grad_ref, grad_w_ref, bias_ref)
    part = contract(grad_ref[0], weight_ref[...], 1, 1)

    @pl.when(pl.program_id(0) == 0)
    def _():
        acc_ref[...] = part

    @pl.when(pl.program_id(0) > 0)
    def _():
        acc_ref[...] += part


def joint_last_kernel(side_ref, *refs, groups, chunk, tm):
    normed, (grad_ref, weight_ref, acc_ref, grad_hidden_ref, gain_ref) = refs[:groups], refs[groups : groups + 5]
    refs = refs[groups + 5 :]
    filled, masks = refs[:groups], refs[groups : 2 * groups]
    (other_bias_ref, sums_ref, up_other_ref, up_own_ref, grad_w_ref, input_ref, rest_ref,
     acc_s, pos_s, bias_s) = refs[2 * groups :]
    core, me = side_ref[0], side_ref[1]
    length, half = normed[0].shape[1], grad_w_ref.shape[1]
    step = pl.program_id(0)
    joint_part(normed, grad_ref, grad_w_ref, bias_s.at[pl.ds(step, 1)])

    @pl.when(step == 0)
    def _():
        acc_s[...] = acc_ref[...] + contract(grad_ref[0], weight_ref[...], 1, 1)

    @pl.when(step == 1)
    def _():
        acc_s[...] += contract(grad_ref[0], weight_ref[...], 1, 1)

    @pl.when(step == 2)
    def _():
        gain = gain_ref[...].astype(F32)
        weight = weight_ref[...]
        total = [jnp.zeros_like(gain) for _ in range(3)]
        for c in range(groups):
            for r in range(length // chunk):
                clip = slice(r * chunk, (r + 1) * chunk)
                rows = slice(c * length + r * chunk, c * length + (r + 1) * chunk)
                grad_norm = acc_s[rows] + contract(grad_ref[0, rows], weight, 1, 1)
                unit, inverse = norm_parts(filled[c][clip])
                grad_filled = grad_hidden_ref[rows] + norm_backward(grad_norm, unit, inverse, gain)
                masked = masks[c][clip] > 0.5
                input_ref[rows] = jnp.where(masked, 0.0, grad_filled).astype(BF16)
                parts = (grad_norm * unit, grad_norm, jnp.where(masked, grad_filled, 0.0))
                total = [t + jnp.sum(p, 0, keepdims=True) for t, p in zip(total, parts)]
                pos_s[clip] = grad_filled if c == 0 else pos_s[clip] + grad_filled
        seg = length // tm
        for d in range(tm):
            at = pl.multiple_of((me ^ d) * seg, seg)
            rest_ref[pl.ds(at, seg)] = pos_s[d * seg : (d + 1) * seg].astype(BF16)

        def both(other, mine):
            return jnp.where(core == 0, jnp.concatenate([mine, other], 1), jnp.concatenate([other, mine], 1))

        width = gain.shape[1]
        up = both(up_other_ref[...], up_own_ref[...])
        sums = sums_ref[...]
        lines = [both(other_bias_ref[i], bias_s[i]) for i in (0, 2)] + [sums[0:1]]
        lines += [up[:, i * width : (i + 1) * width] for i in range(up.shape[1] // width)]
        lines += [sums[1:2], total[0], total[1], sums[2:3], sums[3:4], total[2]]
        lines.append(jnp.zeros((rest_ref.shape[0] - length - len(lines), width), F32))
        rest_ref[length:] = jnp.concatenate(lines, 0).astype(BF16)


def joint_specs(groups, rows, width):
    half = width // 2
    return [fixed((width, rows // groups))] * groups + [
        pl.BlockSpec((1, rows, half), lambda i, s: (i, 0, 0)),
        pl.BlockSpec((width, half), lambda i, s: (0, 2 * i + s[0])),
    ]


def joint_first(side, normed, grads, w_qkv):
    _, rows, half = grads.shape
    groups, width = len(normed), 2 * half
    return call(
        functools.partial(joint_first_kernel, groups=groups),
        prefetch=1,
        share=16,
        grid=(3,),
        in_specs=joint_specs(groups, rows, width),
        out_specs=[
            pl.BlockSpec((width, half), lambda i, s: (0, i)),
            pl.BlockSpec((1, 1, half), lambda i, s: (i, 0, 0)),
            fixed((rows, width)),
        ],
        out_shape=[shaped((width, 3 * half), BF16), shaped((3, 1, half), F32), shaped((rows, width), F32)],
        flops=6 * rows * width * width,
        moved=12 * rows * width,
    )(side, *normed, grads, w_qkv)


def joint_last(side, normed, grads, w_qkv, acc, grad_hidden, gain, filled, masks, bias, sums, up_other, up_own, tm, chunk):
    _, rows, half = grads.shape
    groups, width = len(normed), 2 * half
    length = rows // groups
    return call(
        functools.partial(joint_last_kernel, groups=groups, chunk=chunk, tm=tm),
        prefetch=1,
        share=16,
        grid=(3,),
        in_specs=joint_specs(groups, rows, width)
        + [fixed((rows, width))] * 2
        + [fixed((1, width))]
        + [fixed((length, width))] * groups
        + [fixed((length, 1))] * groups
        + [fixed((3, 1, half)), fixed((8, width)), fixed(up_other.shape), fixed(up_own.shape)],
        out_specs=[pl.BlockSpec((width, half), lambda i, s: (0, i)), fixed((rows, width)), fixed((width, width))],
        out_shape=[shaped((width, 3 * half), BF16), shaped((rows, width), BF16), shaped((width, width), BF16)],
        scratch=[
            pltpu.VMEM((rows, width), F32),
            pltpu.VMEM((length, width), F32),
            pltpu.VMEM((3, 1, half), F32),
        ],
        flops=6 * rows * width * width,
        moved=24 * rows * width,
    )(side, *normed, grads, w_qkv, acc, grad_hidden, gain, *filled, *masks, bias, sums, up_other, up_own)


def cores_in_order(here_ref, own_ref, other_ref):
    low = here_ref[1] == 0
    own, other = own_ref[0], other_ref[0]
    return [jnp.where(low, own, other).astype(F32), jnp.where(low, other, own).astype(F32)]


def place_one_kernel(here_ref, down_own_ref, up_own_ref, down_other_ref, up_other_ref, down_ref, up_ref):
    width = down_ref.shape[2]
    for core, share in enumerate(cores_in_order(here_ref, down_own_ref, down_other_ref)):
        for part in range(share.shape[1] // width):
            down_ref[core, part * share.shape[0] : (part + 1) * share.shape[0]] = share[:, part * width : (part + 1) * width]
    for core, share in enumerate(cores_in_order(here_ref, up_own_ref, up_other_ref)):
        up_ref[:, core * share.shape[1] : (core + 1) * share.shape[1]] = share


def place_two_kernel(here_ref, qkv_own_ref, own_ref, qkv_other_ref, other_ref, qkv_ref, out_ref, rest_ref):
    width = out_ref.shape[1]
    half = width // 2
    for core, share in enumerate(cores_in_order(here_ref, qkv_own_ref, qkv_other_ref)):
        for i in range(3):
            qkv_ref[:, i * width + core * half : i * width + (core + 1) * half] = share[:, i * half : (i + 1) * half]
    out_ref[...], rest_ref[...] = cores_in_order(here_ref, own_ref, other_ref)


def spot_bits(order, tm):
    return [bits_of(bit) if axis == "tm" else bits_of(tm) + bits_of(bit) - 1 for axis, bit in order]


def place(kernel, here, gathered, orders, tm, shapes):
    steps = gathered[0].shape[0]

    def share(value, order):
        bits = spot_bits(order, tm)

        def index(j, here):
            away = j ^ here[0]
            return sum(((away >> b) & 1) << k for k, b in enumerate(bits)), 0, 0

        return pl.BlockSpec((1,) + value.shape[1:], index)

    def cut(shape):
        block = shape[:-2] + (shape[-2] // steps, shape[-1])
        return pl.BlockSpec(block, lambda j, here: (0,) * (len(shape) - 2) + (j, 0))

    return call(
        kernel,
        prefetch=1,
        grid=(steps,),
        in_specs=[share(v, o) for v, o in zip(gathered, orders * 2)],
        out_specs=[cut(s) for s in shapes],
        out_shape=[shaped(s, F32) for s in shapes],
        moved=sum(6 * v.size for v in gathered),
    )(here, *gathered)


def in_order(here, gathered, orders, tm):
    out = []
    half = len(gathered) // 2
    for own, other, order in zip(gathered[:half], gathered[half:], orders):
        bits = spot_bits(order, tm)
        away = jnp.arange(own.shape[0], dtype=jnp.int32) ^ here[0]
        index = sum(((away >> b) & 1) << k for k, b in enumerate(bits))
        own, other = (jnp.take(x, index, axis=0).astype(F32) for x in (own, other))
        low = here[1] == 0
        out.append(jnp.stack([jnp.where(low, own, other), jnp.where(low, other, own)]))
    return out


def bits_of(size):
    return size.bit_length() - 1


def axis_bits(axis):
    return [(axis, 1 << b) for b in range(bits_of(lax.axis_size(axis)))]


def own_bit(axis, bit):
    return (lax.axis_index(axis) // bit) % 2


def hop(value, axis, bit):
    size = lax.axis_size(axis)
    return lax.ppermute(value, axis, [(i, i ^ bit) for i in range(size)])


def tie(*values):
    return lax.optimization_barrier(values)


def take_clips(values):
    tm = lax.axis_size("tm")
    me = lax.axis_index("tm")
    out = []
    for d in range(tm):
        block = lax.dynamic_index_in_dim(values, me ^ d, 1, keepdims=False)
        out.append(hop(block, "tm", d) if d else block)
    return out


def send_clips(values):
    blocks = jnp.split(values, lax.axis_size("tm"), 1)
    return [hop(block, "tm", d) if d else block for d, block in enumerate(blocks)]


def all_clips(blocks, shape):
    return jnp.stack(unshuffle(blocks), 1).reshape(shape)


def unshuffle(blocks):
    me = lax.axis_index("tm")
    blocks = list(blocks)
    for b in range(bits_of(len(blocks))):
        odd = ((me >> b) & 1) == 1
        blocks = [jnp.where(odd, blocks[i ^ (1 << b)], blocks[i]) for i in range(len(blocks))]
    return blocks


def add_low(a, b):
    return (a.astype(F32) + b.astype(F32)).astype(BF16)


def split_share(value):
    count = bits_of(lax.axis_size("clips")) + bits_of(lax.axis_size("tm")) - 1
    return value.reshape((2,) * count + (value.shape[0] >> count, value.shape[1]))


def side_by_side(value, parts):
    return jnp.concatenate(jnp.split(value, parts, -2), -1)


class Sum:
    def __init__(self, folds):
        self.folds = folds
        clip_bits, self.time_bits = axis_bits("clips")[1:], axis_bits("tm")
        self.names = clip_bits[::-1] + self.time_bits[::-1]
        self.orders = (clip_bits, clip_bits[1:] + clip_bits[:1])
        self.rounds = len(clip_bits) + len(self.time_bits)

    def halves(self, pair, names, name):
        at = names.index(name)
        mine = own_bit(*name)
        pick = lambda x, i: lax.dynamic_index_in_dim(x, i, at, keepdims=False)
        return [add_low(*(pick(x, i) for x in pair)) for i in (1 - mine, mine)]

    def split(self, index, state):
        sides = len(self.orders[0])
        if index < sides:
            out = []
            for pair, order in zip(state, self.orders):
                names = [n for n in self.names if n not in order[:index]]
                away, kept = self.halves(pair, names, order[index])
                out.append((kept, away))
            return out
        name = self.time_bits[index - sides]
        names = self.time_bits[index - sides :][::-1]
        parts = [self.halves(pair, names, name) for pair in state]
        if len(state) > 1:
            parts = [[side_by_side(x, n) if n > 1 else x for x in p] for p, n in zip(parts, self.folds)]
        away, kept = (jnp.concatenate(x, -1) if len(x) > 1 else x[0] for x in zip(*parts))
        return [(kept, away)]

    def send(self, index, state):
        sides = len(self.orders[0])
        names = [o[index] for o in self.orders] if index < sides else [self.time_bits[index - sides]]
        return [(kept, hop(away, *name)) for (kept, away), name in zip(state, names)]

    def scatter(self, index, state):
        return self.send(index, self.split(index, state))

    def share(self, state):
        return add_low(*state[0])

    def gather_orders(self):
        return [self.time_bits[::-1] + order[::-1] for order in self.orders]

    def gather(self, index, state, cut):
        if index < len(self.time_bits):
            return [(state[0], hop(state[0], *self.time_bits[::-1][index]))]
        names = [order[::-1][index - len(self.time_bits)] for order in self.orders]
        return [(value, hop(value, *name)) for value, name in zip(state, names)]

    def join(self, index, state, cut):
        out = [jnp.concatenate(pair, 0) for pair in state]
        if index == len(self.time_bits) - 1:
            return [out[0][..., :cut], out[0][..., cut:]]
        return out


def on_device(
    patches, mask_index, mask_count, w_qkv, q_bias, v_bias, w_out, out_bias, w_up, up_bias,
    w_down, down_bias, norm1_scale, norm1_shift, norm2_scale, norm2_shift, mask_embed, pos_embed,
    cotangent,
):
    clip_count, seg, width = patches.shape
    ff = w_up.shape[1]
    tm = lax.axis_size("tm")
    me = lax.axis_index("tm")
    length = seg * tm
    groups = clip_count // tm
    by_group = (groups, tm, seg, width)
    tile, chunk = 512, 512

    arrived = [[b[0] for b in take_clips(patches.reshape(by_group)[g : g + 1])] for g in range(groups)]

    row = lambda x: x.reshape(1, -1)
    joint_bias = row(jnp.concatenate([q_bias, jnp.zeros_like(q_bias), v_bias]))
    out_bias, up_bias, down_bias, gain1, shift1, gain2, shift2, embed = map(
        row, (out_bias, up_bias, down_bias, norm1_scale, norm1_shift, norm2_scale, norm2_shift, mask_embed)
    )
    starts = (me ^ jnp.arange(tm, dtype=jnp.int32)) * seg
    places = (starts[:, None] + jnp.arange(seg, dtype=jnp.int32)[None, :]).reshape(length)
    pos = jnp.concatenate([lax.dynamic_slice_in_dim(pos_embed, (me ^ d) * seg, seg, 0) for d in range(tm)], 0)
    slots = jnp.arange(mask_index.shape[1], dtype=jnp.int32)
    masks = []
    for g in range(groups):
        index_row = lax.dynamic_index_in_dim(mask_index, g * tm + me, 0, keepdims=False)
        count = lax.dynamic_index_in_dim(mask_count, g * tm + me, 0, keepdims=False)
        hit = (places[:, None] == index_row[None, :]) & (slots < count)[None, :]
        masks.append(jnp.any(hit, axis=1, keepdims=True).astype(F32))

    filled, normed_one, joints, attended, turned, logs = [], [], [], [], [], []
    for g in range(groups):
        if g:
            *blocks, last = tie(*arrived[g], attended[-1])
            attended[-1] = last
        else:
            blocks = arrived[g]
        f, n, j = project(blocks, masks[g], embed, pos, gain1, shift1, w_qkv, joint_bias)
        a, a_turned, log_sum = attend(j, width)
        for kept, value in zip((filled, normed_one, joints, attended, turned, logs), (f, n, j, a, a_turned, log_sum)):
            kept.append(value)
        if not g:
            tied, joints[0] = tie(cotangent, j)
            cot = take_clips(tied.reshape(by_group))

    core = own_bit("clips", 1).astype(jnp.int32)
    kept_side = jnp.stack([core, me.astype(jnp.int32)])
    away_side = jnp.stack([1 - core, me.astype(jnp.int32)])
    here = jnp.stack([(lax.axis_index("clips") // 2 * tm + me).astype(jnp.int32), core])
    hidden, normed_two, act, slope, block_out = forward(
        filled, attended, w_out, out_bias, gain2, shift2, down_bias, w_up, up_bias, w_down, 768, length * groups
    )
    cot = jnp.concatenate(cot, 1).reshape(groups * length, width)
    cot, block_out = tie(cot, block_out)
    norm_acc, down, up, up_sums_away = back_first(away_side, normed_two, cot, act, slope, w_up, w_down, tile, chunk)
    down_got, up_got = hop(down, "clips", 1), hop(up, "clips", 1)
    down, up, up_sums, grad_hidden, mix, grad_out, sums_two = back_last(
        kept_side, turned, normed_two, cot, act, slope, w_up, w_down, w_out, gain2, hidden, norm_acc, tile, chunk
    )
    one = Sum((2, 1))

    def after(values, *states):
        flat = [x for state in states for pair in state for x in pair]
        tied = list(tie(*values, *flat))
        values, flat = tied[: len(values)], tied[len(values) :]
        back = [[tuple(flat.pop(0) for _ in pair) for pair in state] for state in states]
        return (values, *back)

    state = [tuple(split_share(x) for x in pair) for pair in ((down, down_got), (up, up_got))]
    state = one.split(0, state)
    (mix, block_out), state = after((mix, block_out), state)
    state = one.send(0, state)
    block_out = send_clips(block_out.reshape(groups, length, width))
    grads = attend_back(away_side, joints, mix, logs)
    qkv, bias_sums, acc = joint_first(away_side, normed_one, grads, w_qkv)
    qkv_got = hop(qkv, "clips", 1)
    (acc,), state = after((acc,), state)
    state = one.split(1, state)
    (mix, acc), state = after((mix, acc), state)
    state = one.send(1, state)
    grads = attend_back(kept_side, joints, mix, logs)
    (grads,), state = after((grads,), state)
    state = one.split(2, state)
    tied, state = after((grads, *block_out), state)
    grads, block_out = tied[0], tied[1:]
    state = one.send(2, state)
    qkv, input_grad, rest = joint_last(
        kept_side, normed_one, grads, w_qkv, acc, grad_hidden, gain1, filled, masks, bias_sums, sums_two,
        up_sums_away, up_sums, tm, chunk
    )
    rest_away = jnp.where(core == 1, grad_out, rest)
    rest_kept = jnp.where(core == 1, rest, grad_out)
    rest_got = hop(rest_away, "clips", 1)
    two = Sum((1, 1))
    pairs = [tuple(split_share(x) for x in pair) for pair in ((qkv, qkv_got), (rest_kept, rest_got))]
    cut_one, cut_two = ff // 2, 3 * width // 2
    share_rows = pairs[0][0].shape[-2]

    def scatter_steps(group, first):
        steps = [lambda s, i=i: group.split(i, s) for i in range(first, group.rounds)]
        return [(split, lambda s, i=i: group.send(i, s)) for i, split in zip(range(first, group.rounds), steps)]

    def gather_steps(group, cut):
        def prepare(i):
            if i == 0:
                return lambda s: [(group.share(s)[None],)]
            return lambda s: [(x,) for x in group.join(i - 1, s, cut)]

        return [
            (prepare(i), lambda s, i=i: group.gather(i, [x for (x,) in s], cut)) for i in range(group.rounds)
        ]

    def core_steps(group, cut):
        return [
            (
                lambda s: [(x,) for x in group.join(group.rounds - 1, s, cut)],
                lambda s: [(x, hop(x, "clips", 1)) for (x,) in s],
            )
        ]

    steps_one = scatter_steps(one, 3) + gather_steps(one, cut_one) + core_steps(one, cut_one)
    steps_two = scatter_steps(two, 0) + gather_steps(two, cut_two) + core_steps(two, cut_two)
    outputs = []
    for index in range(max(len(steps_one), len(steps_two))):
        active = [steps[index] if index < len(steps) else None for steps in (steps_one, steps_two)]
        states = [step[0](x) if step else x for step, x in zip(active, (state, pairs))]
        live = [x for x, step in zip(states, active) if step]
        if index == 3:
            (input_grad,), *live = after((input_grad,), *live)
            sent = send_clips(input_grad.reshape(groups, length, width))
        elif index == len(steps_two) - 1:
            tied, *live = after((*sent, *outputs), *live)
            sent, outputs = tied[: len(sent)], tied[len(sent) :]
        else:
            _, *live = after((), *live)
        live = iter(live)
        state, pairs = (step[1](next(live)) if step else x for step, x in zip(active, states))
        if index == len(steps_one) - 1:
            one_all = [own for own, _ in state] + [other for _, other in state]
            if share_rows % 8 == 0:
                outputs = place(
                    place_one_kernel, here, one_all, one.gather_orders(), tm, ((2, ff // 2, width), (width, ff))
                )
    two_all = [own for own, _ in pairs] + [other for _, other in pairs]
    block_out, input_grad = all_clips(block_out, patches.shape), all_clips(sent, patches.shape)

    orders_one, orders_two = one.gather_orders(), two.gather_orders()
    if share_rows % 8 == 0:
        down_sum, up_sum = outputs
        qkv_sum, out_sum, rest = place(
            place_two_kernel, here, two_all, orders_two, tm, ((width, 3 * width), (width, width), (width, width))
        )
        down_sum = down_sum.reshape(ff, width)
    else:
        downs, ups = in_order(here, one_all, orders_one, tm)
        qkvs, rests = in_order(here, two_all, orders_two, tm)
        down_sum = jnp.stack(jnp.split(downs, 2, -1), 2).reshape(ff, width)
        up_sum = jnp.concatenate(list(ups.reshape(2, width, ff // 2)), 1)
        qkv_sum = jnp.stack(list(qkvs.reshape(2, width, 3, width // 2)), 2).reshape(width, 3 * width)
        out_sum, rest = rests.reshape(2, width, width)
    v = []
    at = length
    for n in (1, 1, 1, ff // width, 1, 1, 1, 1, 1, 1):
        v.append(rest[at : at + n].reshape(-1))
        at += n
    return (block_out, input_grad, qkv_sum, v[0], v[1], out_sum, v[2], up_sum, v[3], down_sum, v[4],
            v[5], v[6], v[7], v[8], v[9], rest[:length])


def solution(mesh):
    rows = P("clips", "tm", None)
    in_specs = (rows, P("clips", None), P("clips")) + (P(),) * 15 + (rows,)
    out_specs = (rows, rows) + (P(),) * 15
    return jax.shard_map(on_device, mesh=mesh, in_specs=in_specs, out_specs=out_specs, check_vma=False)
```

time: 624 us -> 452 us (0.72)
  Pallas kernels: 0 us -> 181 us
  matrix products: 146 us -> 0 us
  other arithmetic: 126 us -> 26.9 us
  local copies, waits for them, and re-layouts: 103 us -> 33.1 us
  starting transfers between devices: 92.8 us -> 67.5 us
  waiting for transfers between devices: 145 us -> 134 us
    pallas_call x0 -> x13, Pallas kernels: none -> 181 us  [the longest x2 28.7 us: attend_back(): call(functools.partial(attend_back_kernel, head=head, groups=groups), pre...]
    dot_general x28 -> x0, matrix products: 146 us -> none  [the longest x4 42.2 us: dot_tn(): lax.dot_general(a, b, (((0,), (0,)), ((), ())), preferred_element_type=F32)]
    convert_element_type x37 -> x20, other arithmetic: 50.4 us -> 9.03 us  [the longest x18 9.02 us: add_low(): return (a.astype(F32) + b.astype(F32)).astype(BF16)]
    concatenate x2, local copies, waits for them, and re-layouts: 34.9 us -> 0.07 us  [join(): out = [jnp.concatenate(pair, 0) for pair in state]]
    reduce_sum x20 -> x0, other arithmetic: 30.5 us -> none  [the longest x8 11.5 us: on_device(): jnp.sum(top, 0)]
    ppermute x60 -> x47, starting transfers between devices: 92.8 us -> 67.5 us  [hop(): return lax.ppermute(value, axis, [(i, i ^ bit) for i in range(size)])]
    unnamed x297 -> x52, local copies, waits for them, and re-layouts: 25.5 us -> 2.15 us
    ppermute x60 -> x47, waiting for transfers between devices: 145 us -> 134 us  [hop(): return lax.ppermute(value, axis, [(i, i ^ bit) for i in range(size)])]
  transfers between devices with their start and end apart: 60 -> 47, of which waited for: 30 -> 20; matrix products, arithmetic and copies ran while one was open for 28% -> 9% of each run, Pallas kernels for 0% -> 34%
where the time goes in v3:
time: 452 us; the launch traced here: 444 us
  Pallas kernels  181 us (40%)
  waiting for transfers between devices  134 us (30%)
  starting transfers between devices  67.5 us (15%)
  local copies, waits for them, and re-layouts  33.1 us (7%)
  other arithmetic  26.9 us (6%)
    ppermute x47, waiting for transfers between devices, hop(): return lax.ppermute(value, axis, [(i, i ^ bit) for i in range(size)])  134 us
    ppermute x47, starting transfers between devices, hop(): return lax.ppermute(value, axis, [(i, i ^ bit) for i in range(size)])  67.5 us
    pallas_call x2, Pallas kernels, attend_back(): call(functools.partial(attend_back_kernel, head=head, groups=groups), pre...  28.7 us
    pallas_call x2, Pallas kernels, place(): call(kernel, prefetch=1, grid=(steps,), in_specs=[share(v, o) for v, o in...  28.4 us
    pallas_call x1, Pallas kernels, back_last(): call(functools.partial(back_last_kernel, groups=groups, chunk=chunk), pre...  25.2 us
    pallas_call x1, Pallas kernels, forward(): call(functools.partial(forward_kernel, groups=groups, chunk=chunk), grid=...  24.6 us
    pallas_call x2, Pallas kernels, attend(): call(functools.partial(attend_kernel, head=head), grid=(steps,), in_specs...  17.9 us
    pallas_call x1, Pallas kernels, back_first(): call(functools.partial(back_first_kernel, chunk=chunk), prefetch=1, grid=...  15.7 us
  transfers between devices with their start and end apart: 47, of which 20 were waited for; matrix products, arithmetic and copies ran while one was open for 9% of the time, Pallas kernels for 34%

profile of v3, /device:TPU:0, one launch (start us, length us, event | category | flops | bytes accessed | tf_op | source)
XLA Modules:
  0.0 443.6 jit_solution(5322854073591771954)
XLA Ops:
  0.7 1.5 fusion.32
  3.0 3.1 collective-permute-start
  6.1 2.6 collective-permute-start.1
  10.3 3.5 collective-permute-start.4
  26.4 7.1 %shard_map.314 = (f32[512,768]{1,0:T(8,128)}, bf16[768,512]{1,0:T(8,128)(2,1)}, bf16[512,2304]{1,0:T(8,128)(2,1)}) custom-call(bf16[128,768]{1,0:T(8,128)(2,1)} %get-tuple-element.325.refs_0_, bf16[128,768]{1,0:T(8,128)(2,1)} %bitcast.139, bf16[128,768]{1,0:T(8,128)(2,1)} %bitcast.140, bf16[128,768]{1,0:T(8,128)(2,1)} %bitcast.5.refs_3_, ...), custom_call_target="tpu_custom_call" | custom-call | flops 1811939328 | bytes 7864320 | tf_op jit(solution)/shard_map/pallas_call | solution.py:91
  33.6 10.3 %collective-permute-start.6 = (bf16[2,128,768]{2,1,0:T(8,128)(2,1)S(1)}, bf16[2,128,768]{2,1,0:T(8,128)(2,1)S(1)}, u32[]{:S(2)}, u32[]{:S(2)}) collective-permute-start(bf16[2,128,768]{2,1,0:T(8,128)(2,1)S(1)} %get-tuple-element.295), channel_id=1, source_target_pairs={{0,1},{1,0},{2,3},{3,2},{4,5},{5,4},{6,7},{7,6},{8,9},{9,8},{10,11... | collective-permute-start | bytes 1179656 | tf_op jit(solution)/shard_map/ppermute | solution.py:599
  45.0 9.0 %shard_map.315 = (bf16[512,768]{1,0:T(8,128)(2,1)}, bf16[768,512]{1,0:T(8,128)(2,1)}, f32[6,2,512]{2,1,0:T(2,128)}) custom-call(bf16[512,2304]{1,0:T(8,128)(2,1)} %get-tuple-element.132.q_ref.k_ref.v_ref.refs_0_.refs_1_.refs_2_, bf16[512,2304]{1,0:T(8,128)(2,1)} %get-tuple-element.132.q_ref.k_ref.v_ref.refs_0_.refs_1_.refs_2_, ...), custom_call_target="tpu_custom_call" | custom-call | flops 3221225472 | bytes 3145728 | tf_op jit(solution)/shard_map/pallas_call | solution.py:140
  53.9 1.5 collective-permute-start.8
  56.1 7.0 %shard_map.316 = (f32[512,768]{1,0:T(8,128)}, bf16[768,512]{1,0:T(8,128)(2,1)}, bf16[512,2304]{1,0:T(8,128)(2,1)}) custom-call(bf16[128,768]{1,0:T(8,128)(2,1)} %get-tuple-element.135.refs_0_, bf16[128,768]{1,0:T(8,128)(2,1)} %bitcast.11.refs_1_, bf16[128,768]{1,0:T(8,128)(2,1)} %bitcast.12.refs_2_, bf16[128,768]{1,0:T(8,128)(2,1)} %bitcast.141, ...), custom_call_target="tpu_custom_call" | custom-call | flops 1811939328 | bytes 7864320 | tf_op jit(solution)/shard_map/pallas_call | solution.py:91
  63.1 9.0 %shard_map.317 = (bf16[512,768]{1,0:T(8,128)(2,1)}, bf16[768,512]{1,0:T(8,128)(2,1)}, f32[6,2,512]{2,1,0:T(2,128)}) custom-call(bf16[512,2304]{1,0:T(8,128)(2,1)} %get-tuple-element.139.q_ref.k_ref.v_ref.refs_4_.refs_5_.refs_6_, bf16[512,2304]{1,0:T(8,128)(2,1)} %get-tuple-element.139.q_ref.k_ref.v_ref.refs_4_.refs_5_.refs_6_, ...), custom_call_target="tpu_custom_call" | custom-call | flops 3221225472 | bytes 3145728 | tf_op jit(solution)/shard_map/pallas_call | solution.py:140
  72.1 24.6 %shard_map.318 = (f32[1024,768]{1,0:T(8,128)}, bf16[768,1024]{1,0:T(8,128)(2,1)}, bf16[3072,1024]{1,0:T(8,128)(2,1)}, bf16[1024,3072]{1,0:T(8,128)(2,1)}, bf16[1024,768]{1,0:T(8,128)(2,1)}) custom-call(f32[512,768]{1,0:T(8,128)} %get-tuple-element.143.refs_0_.refs_7_, f32[512,768]{1,0:T(8,128)} %get-tuple-element.144.refs_1_.refs_8_, ...), custom_call_target="tpu_custom_call" | custom-call | flops 10871635968 | bytes 33030144 | tf_op jit(solution)/shard_map/pallas_call | solution.py:256
  98.1 15.7 %shard_map.319 = (f32[1024,768]{1,0:T(8,128)}, bf16[1536,768]{1,0:T(8,128)(2,1)}, bf16[768,1536]{1,0:T(8,128)(2,1)}, f32[1,1536]{1,0:T(1,128)}) custom-call(s32[2]{0:T(128)} %get-tuple-element.339.side_ref, bf16[768,1024]{1,0:T(8,128)(2,1)} %get-tuple-element.147.turned_ref.refs_2_, bf16[1024,768]{1,0:T(8,128)(2,1)} %bitcast.128, ...), custom_call_target="tpu_custom_call" | custom-call | flops 9663676416 | bytes 22020096 | tf_op jit(solution)/shard_map/pallas_call | solution.py:352
  114.3 25.2 %shard_map.320 = (bf16[1536,768]{1,0:T(8,128)(2,1)}, bf16[768,1536]{1,0:T(8,128)(2,1)}, f32[1,1536]{1,0:T(1,128)}, f32[1024,768]{1,0:T(8,128)}, bf16[1024,768]{1...) custom-call(s32[2]{0:T(128)} %get-tuple-element.338.side_ref, bf16[768,512]{1,0:T(8,128)(2,1)} %get-tuple-element.141.refs_0_, ...), custom_call_target="tpu_custom_call" | custom-call | flops 12079595520 | bytes 31457280 | tf_op jit(solution)/shard_map/pallas_call | solution.py:371
  139.5 1.9 constant_dynamic-slice_fusion.13
  142.1 1.9 constant_dynamic-slice_fusion.8
  147.5 1.5 collective-permute-start.11
  149.0 1.5 collective-permute-start.12
  150.5 14.5 %shard_map.321.refs_2_ = bf16[3,1024,384]{2,1,0:T(8,128)(2,1)} custom-call(s32[2]{0:T(128)} %get-tuple-element.339.side_ref, bf16[512,2304]{1,0:T(8,128)(2,1)} %get-tuple-element.132.q_ref.k_ref.v_ref.refs_0_.refs_1_.refs_2_, bf16[512,2304]{1,0:T(8,128)(2,1)} %get-tuple-element.132.q_ref.k_ref.v_ref.refs_0_.refs_1_.refs_2_, ...), custom_call_target="tpu_custom_call" | custom-call | flops 503316480 | bytes 393216 | tf_op jit(solution)/shard_map/pallas_call | solution.py:194
  165.0 10.5 %shard_map.322 = (bf16[768,1152]{1,0:T(8,128)(2,1)}, f32[3,1,384]{2,1,0:T(1,128)}, f32[1024,768]{1,0:T(8,128)}) custom-call(s32[2]{0:T(128)} %get-tuple-element.339.side_ref, bf16[768,512]{1,0:T(8,128)(2,1)} %get-tuple-element.162.refs_0_, bf16[768,512]{1,0:T(8,128)(2,1)} %get-tuple-element.163.refs_1_, bf16[3,1024,384]{2,1,0:T(8,128)(2,1)} %shard_map.321.refs_2_, ...), custom_call_target="tpu_custom_call" | custom-call | flops 226492416 | bytes 589824 | tf_op jit(solution)/shard_map/pallas_call | solution.py:473
  177.0 1.5 fusion.9
  178.5 2.3 fusion.7
  180.9 1.5 collective-permute-start.13
  182.9 2.4 fusion.31
  186.4 2.0 collective-permute-start.16
  189.7 14.2 %shard_map.323.refs_2_ = bf16[3,1024,384]{2,1,0:T(8,128)(2,1)} custom-call(s32[2]{0:T(128)} %get-tuple-element.338.side_ref, bf16[512,2304]{1,0:T(8,128)(2,1)} %get-tuple-element.132.q_ref.k_ref.v_ref.refs_0_.refs_1_.refs_2_, bf16[512,2304]{1,0:T(8,128)(2,1)} %get-tuple-element.132.q_ref.k_ref.v_ref.refs_0_.refs_1_.refs_2_, ...), custom_call_target="tpu_custom_call" | custom-call | flops 503316480 | bytes 393216 | tf_op jit(solution)/shard_map/pallas_call | solution.py:194
  204.6 11.9 %collective-permute-done.16 = bf16[2,128,768]{2,1,0:T(8,128)(2,1)} collective-permute-done((bf16[2,128,768]{2,1,0:T(8,128)(2,1)}, bf16[2,128,768]{2,1,0:T(8,128)(2,1)}, u32[]{:S(2)}, u32[]{:S(2)}) %collective-permute-start.16) | collective-permute-done | bytes 393248 | tf_op jit(solution)/shard_map/ppermute | solution.py:599
  216.5 15.5 %shard_map.324 = (bf16[768,1152]{1,0:T(8,128)(2,1)}, bf16[1024,768]{1,0:T(8,128)(2,1)}, bf16[768,768]{1,0:T(8,128)(2,1)}) custom-call(s32[2]{0:T(128)} %get-tuple-element.338.side_ref, bf16[768,512]{1,0:T(8,128)(2,1)} %get-tuple-element.162.refs_0_, bf16[768,512]{1,0:T(8,128)(2,1)} %get-tuple-element.163.refs_1_, bf16[3,1024,384]{2,1,0:T(8,128)(2,1)} %shard_map.323.refs_2_, ...), custom_call_target="tpu_custom_call" | custom-call | flops 226492416 | bytes 1179648 | tf_op jit(solution)/shard_map/pallas_call | solution.py:494
  232.1 1.6 broadcast_select_fusion.1
  234.0 1.6 constant_dynamic-slice_fusion.4
  235.6 6.2 %collective-permute-start.18 = (bf16[2,48,3072]{2,1,0:T(8,128)(2,1)S(1)}, bf16[2,48,3072]{2,1,0:T(8,128)(2,1)S(1)}, u32[]{:S(2)}, u32[]{:S(2)}) collective-permute-start(bf16[2,48,3072]{2,1,0:T(8,128)(2,1)S(1)} %pad_maximum_fusion.12), channel_id=1, source_target_pairs={{0,1},{1,0},{2,3},{3,2},{4,5},{5,4},{6,7},{7,6},{8,9},{9,8},{10,11... | collective-permute-start | bytes 1769480 | tf_op jit(solution)/shard_map/ppermute | solution.py:599
  242.3 13.3 %collective-permute-done.18 = bf16[2,48,3072]{2,1,0:T(8,128)(2,1)S(1)} collective-permute-done((bf16[2,48,3072]{2,1,0:T(8,128)(2,1)S(1)}, bf16[2,48,3072]{2,1,0:T(8,128)(2,1)S(1)}, u32[]{:S(2)}, u32[]{:S(2)}) %collective-permute-start.18) | collective-permute-done | bytes 589856 | tf_op jit(solution)/shard_map/ppermute | solution.py:599
  256.2 2.8 collective-permute-start.21
  259.0 1.4 collective-permute-start.22
  260.9 11.3 %collective-permute-done.21 = bf16[48,3072]{1,0:T(8,128)(2,1)S(1)} collective-permute-done((bf16[48,3072]{1,0:T(8,128)(2,1)S(1)}, bf16[48,3072]{1,0:T(8,128)(2,1)S(1)}, u32[]{:S(2)}, u32[]{:S(2)}) %collective-permute-start.21) | collective-permute-done | bytes 294944 | tf_op jit(solution)/shard_map/ppermute | solution.py:599
  272.3 2.3 collective-permute-done.23
  274.8 5.0 %collective-permute-done.22 = bf16[2,2,2,48,1152]{4,3,1,2,0:T(8,128)(2,1)S(1)} collective-permute-done((bf16[2,2,2,48,1152]{4,3,1,2,0:T(8,128)(2,1)S(1)}, bf16[2,2,2,48,1152]{4,3,1,2,0:T(8,128)(2,1)S(1)}, u32[]{:S(2)}, u32[]{:S(2)}) %collective-permute-start.22) | collective-permute-done | bytes 884768 | tf_op jit(solution)/shard_map/ppermute | solution.py:599
  280.0 1.5 collective-permute-start.26
  282.5 4.8 %collective-permute-done.26 = bf16[2,2,48,768]{3,2,0,1:T(8,128)(2,1)S(1)} collective-permute-done((bf16[2,2,48,768]{3,2,0,1:T(8,128)(2,1)S(1)}, bf16[2,2,48,768]{3,2,0,1:T(8,128)(2,1)S(1)}, u32[]{:S(2)}, u32[]{:S(2)}) %collective-permute-start.26) | collective-permute-done | bytes 294944 | tf_op jit(solution)/shard_map/ppermute | solution.py:599
  287.4 8.3 %collective-permute-done.24 = bf16[1,48,3072]{2,1,0:T(8,128)(2,1)S(1)} collective-permute-done((bf16[1,48,3072]{2,1,0:T(8,128)(2,1)S(1)}, bf16[1,48,3072]{2,1,0:T(8,128)(2,1)S(1)}, u32[]{:S(2)}, u32[]{:S(2)}) %collective-permute-start.24) | collective-permute-done | bytes 294944 | tf_op jit(solution)/shard_map/ppermute | solution.py:599
  296.0 2.0 collective-permute-start.27
  298.1 9.4 %collective-permute-done.28 = bf16[2,48,1920]{2,1,0:T(8,128)(2,1)S(1)} collective-permute-done((bf16[2,48,1920]{2,1,0:T(8,128)(2,1)S(1)}, bf16[2,48,1920]{2,1,0:T(8,128)(2,1)S(1)}, u32[]{:S(2)}, u32[]{:S(2)}) %collective-permute-start.28) | collective-permute-done | bytes 368672 | tf_op jit(solution)/shard_map/ppermute | solution.py:599
  307.6 11.1 %collective-permute-done.27 = bf16[2,48,3072]{2,1,0:T(8,128)(2,1)S(1)} collective-permute-done((bf16[2,48,3072]{2,1,0:T(8,128)(2,1)S(1)}, bf16[2,48,3072]{2,1,0:T(8,128)(2,1)S(1)}, u32[]{:S(2)}, u32[]{:S(2)}) %collective-permute-start.27) | collective-permute-done | bytes 589856 | tf_op jit(solution)/shard_map/ppermute | solution.py:599
  320.2 8.8 %collective-permute-done.34 = bf16[48,1920]{1,0:T(8,128)(2,1)S(1)} collective-permute-done((bf16[48,1920]{1,0:T(8,128)(2,1)S(1)}, bf16[48,1920]{1,0:T(8,128)(2,1)S(1)}, u32[]{:S(2)}, u32[]{:S(2)}) %collective-permute-start.34) | collective-permute-done | bytes 184352 | tf_op jit(solution)/shard_map/ppermute | solution.py:599
  329.0 4.0 collective-permute-done.33
  334.1 1.4 collective-permute-start.35
  335.5 2.4 collective-permute-start.37
  337.9 6.0 %collective-permute-done.37 = bf16[1,48,1920]{2,1,0:T(8,128)(2,1)S(1)} collective-permute-done((bf16[1,48,1920]{2,1,0:T(8,128)(2,1)S(1)}, bf16[1,48,1920]{2,1,0:T(8,128)(2,1)S(1)}, u32[]{:S(2)}, u32[]{:S(2)}) %collective-permute-start.37) | collective-permute-done | bytes 184352 | tf_op jit(solution)/shard_map/ppermute | solution.py:599
  343.9 15.1 %collective-permute-done.36 = bf16[8,48,1536]{2,1,0:T(8,128)(2,1)S(1)} collective-permute-done((bf16[8,48,1536]{2,1,0:T(8,128)(2,1)S(1)}, bf16[8,48,1536]{2,1,0:T(8,128)(2,1)S(1)}, u32[]{:S(2)}, u32[]{:S(2)}) %collective-permute-start.36) | collective-permute-done | bytes 1179680 | tf_op jit(solution)/shard_map/ppermute | solution.py:599
  359.2 1.8 pad_maximum_fusion.down_own_ref
  362.6 5.9 %collective-permute-done.40 = bf16[2,48,1920]{2,1,0:T(8,128)(2,1)S(1)} collective-permute-done((bf16[2,48,1920]{2,1,0:T(8,128)(2,1)S(1)}, bf16[2,48,1920]{2,1,0:T(8,128)(2,1)S(1)}, u32[]{:S(2)}, u32[]{:S(2)}) %collective-permute-start.40) | collective-permute-done | bytes 368672 | tf_op jit(solution)/shard_map/ppermute | solution.py:599
  368.6 1.4 collective-permute-start.41
  371.4 8.0 %collective-permute-done.42 = bf16[4,48,768]{2,1,0:T(8,128)(2,1)S(1)} collective-permute-done((bf16[4,48,768]{2,1,0:T(8,128)(2,1)S(1)}, bf16[4,48,768]{2,1,0:T(8,128)(2,1)S(1)}, u32[]{:S(2)}, u32[]{:S(2)}) %collective-permute-start.42) | collective-permute-done | bytes 294944 | tf_op jit(solution)/shard_map/ppermute | solution.py:599
  380.4 1.5 collective-permute-start.43
  382.9 2.4 fusion.30
  385.3 1.4 collective-permute-start.29
  386.8 5.3 %collective-permute-done.44 = bf16[8,48,768]{2,1,0:T(8,128)(2,1)} collective-permute-done((bf16[8,48,768]{2,1,0:T(8,128)(2,1)}, bf16[8,48,768]{2,1,0:T(8,128)(2,1)}, u32[]{:S(2)}, u32[]{:S(2)}) %collective-permute-start.44) | collective-permute-done | bytes 589856 | tf_op jit(solution)/shard_map/ppermute | solution.py:599
  392.1 2.4 collective-permute-start.30
  395.8 2.5 collective-permute-start.31
  399.7 3.0 pad_maximum_fusion.2.qkv_own_ref
  402.7 15.5 %shard_map.325 = (f32[2,1536,768]{2,1,0:T(8,128)}, f32[768,3072]{1,0:T(8,128)}) custom-call(s32[2]{0:T(128)} %pad_add_fusion.2.here_ref, bf16[16,48,1536]{2,1,0:T(8,128)(2,1)} %pad_maximum_fusion.down_own_ref, bf16[16,48,1536]{2,1,0:T(8,128)(2,1)} %copy-done, bf16[16,48,1536]{2,1,0:T(8,128)(2,1)} %collective-permute-done.38.down_other_ref, ...), custom_call_target="tpu_custom_call" | custom-call | bytes 28311552 | tf_op jit(solution)/shard_map/pallas_call | solution.py:561
  418.8 1.5 select_bitcast_fusion.7
  424.6 12.9 %shard_map.326 = (f32[768,2304]{1,0:T(8,128)}, f32[768,768]{1,0:T(8,128)}, f32[768,768]{1,0:T(8,128)}) custom-call(s32[2]{0:T(128)} %pad_add_fusion.2.here_ref, bf16[16,48,1152]{2,1,0:T(8,128)(2,1)} %pad_maximum_fusion.2.qkv_own_ref, bf16[16,48,768]{2,1,0:T(8,128)(2,1)} %copy-done.2, bf16[16,48,1152]{2,1,0:T(8,128)(2,1)} %collective-permute-done.45.qkv_other_ref, ...), custom_call_target="tpu_custom_call" | custom-call | bytes 17694720 | tf_op jit(solution)/shard_map/pallas_call | solution.py:561
  437.5 2.7 slice.69
  440.1 1.7 slice_reduce_fusion
  (187 shorter events, 48.5 us)
Async XLA Ops:
  2.2 11.7 %copy-start.12 = (s32[8]{0:T(128)S(1)}, s32[8]{0:T(128)}, u32[]{:S(2)}) copy-start(s32[8]{0:T(128)} %param.21) | copy-start | bytes 100
  2.2 21.8 %copy-start.10 = (bf16[512,768]{1,0:T(8,128)(2,1)S(1)}, bf16[512,768]{1,0:T(8,128)(2,1)}, u32[]{:S(2)}) copy-start(bf16[512,768]{1,0:T(8,128)(2,1)} %param.36) | copy-start | bytes 2359300
  2.9 14.8 %copy-start.13 = (bf16[768]{0:T(1024)(128)(2,1)S(1)}, bf16[768]{0:T(1024)(128)(2,1)}, u32[]{:S(2)}) copy-start(bf16[768]{0:T(1024)(128)(2,1)} %param.31) | copy-start | bytes 4612
  2.9 15.4 %copy-start.20 = (bf16[768]{0:T(1024)(128)(2,1)S(1)}, bf16[768]{0:T(1024)(128)(2,1)}, u32[]{:S(2)}) copy-start(bf16[768]{0:T(1024)(128)(2,1)} %param.24) | copy-start | bytes 4612
  2.9 15.4 %copy-start.21 = (bf16[768]{0:T(1024)(128)(2,1)S(1)}, bf16[768]{0:T(1024)(128)(2,1)}, u32[]{:S(2)}) copy-start(bf16[768]{0:T(1024)(128)(2,1)} %param.23) | copy-start | bytes 4612
  2.9 16.1 %copy-start.14 = (bf16[768]{0:T(1024)(128)(2,1)S(1)}, bf16[768]{0:T(1024)(128)(2,1)}, u32[]{:S(2)}) copy-start(bf16[768]{0:T(1024)(128)(2,1)} %param.35) | copy-start | bytes 4612
  2.9 16.6 %copy-start.15 = (bf16[768]{0:T(1024)(128)(2,1)S(1)}, bf16[768]{0:T(1024)(128)(2,1)}, u32[]{:S(2)}) copy-start(bf16[768]{0:T(1024)(128)(2,1)} %param.32) | copy-start | bytes 4612
  3.0 18.1 %copy-start.16 = (bf16[768]{0:T(1024)(128)(2,1)S(1)}, bf16[768]{0:T(1024)(128)(2,1)}, u32[]{:S(2)}) copy-start(bf16[768]{0:T(1024)(128)(2,1)} %param.33) | copy-start | bytes 4612
  3.0 18.7 %copy-start.11 = (bf16[3072]{0:T(1024)(128)(2,1)S(1)}, bf16[3072]{0:T(1024)(128)(2,1)}, u32[]{:S(2)}) copy-start(bf16[3072]{0:T(1024)(128)(2,1)} %param.28) | copy-start | bytes 18436
  3.0 19.3 %copy-start.17 = (bf16[768]{0:T(1024)(128)(2,1)S(1)}, bf16[768]{0:T(1024)(128)(2,1)}, u32[]{:S(2)}) copy-start(bf16[768]{0:T(1024)(128)(2,1)} %param.26) | copy-start | bytes 4612
  3.0 19.8 %copy-start.18 = (bf16[768]{0:T(1024)(128)(2,1)S(1)}, bf16[768]{0:T(1024)(128)(2,1)}, u32[]{:S(2)}) copy-start(bf16[768]{0:T(1024)(128)(2,1)} %param.34) | copy-start | bytes 4612
  3.0 20.4 %copy-start.19 = (bf16[768]{0:T(1024)(128)(2,1)S(1)}, bf16[768]{0:T(1024)(128)(2,1)}, u32[]{:S(2)}) copy-start(bf16[768]{0:T(1024)(128)(2,1)} %param.30) | copy-start | bytes 4612
  3.0 22.6 %collective-permute-start = (bf16[1,128,768]{2,1,0:T(8,128)(2,1)S(1)}, bf16[1,128,768]{2,1,0:T(8,128)(2,1)S(1)}, u32[]{:S(2)}, u32[]{:S(2)}) collective-permute-start(bf16[1,128,768]{2,1,0:T(8,128)(2,1)S(1)} %get-tuple-element.324), channel_id=1, source_target_pairs={{0,1},{1,0},{2,3},{3,2},{4,5},{5,4},{6,7},{7,6},{8,9},{9,8},{10,11... | collective-permute-start | bytes 589832 | tf_op jit(solution)/shard_map/ppermute | solution.py:599
  6.1 19.6 %collective-permute-start.1 = (bf16[1,128,768]{2,1,0:T(8,128)(2,1)S(1)}, bf16[1,128,768]{2,1,0:T(8,128)(2,1)S(1)}, u32[]{:S(2)}, u32[]{:S(2)}) collective-permute-start(bf16[1,128,768]{2,1,0:T(8,128)(2,1)S(1)} %get-tuple-element.323), channel_id=1, source_target_pairs={{0,2},{1,3},{2,0},{3,1},{4,6},{5,7},{6,4},{7,5},{8,10},{9,11},{10,... | collective-permute-start | bytes 589832 | tf_op jit(solution)/shard_map/ppermute | solution.py:599
  8.7 17.0 %collective-permute-start.2 = (bf16[1,128,768]{2,1,0:T(8,128)(2,1)S(1)}, bf16[1,128,768]{2,1,0:T(8,128)(2,1)}, u32[]{:S(2)}, u32[]{:S(2)}) collective-permute-start(bf16[1,128,768]{2,1,0:T(8,128)(2,1)S(1)} %get-tuple-element.322), channel_id=1, source_target_pairs={{0,3},{1,2},{2,1},{3,0},{4,7},{5,6},{6,5},{7,4},{8,11},{9,10},{10,... | collective-permute-start | bytes 589832 | tf_op jit(solution)/shard_map/ppermute | solution.py:599
  9.4 44.5 %collective-permute-start.3 = (bf16[1,128,768]{2,1,0:T(8,128)(2,1)S(1)}, bf16[1,128,768]{2,1,0:T(8,128)(2,1)}, u32[]{:S(2)}, u32[]{:S(2)}) collective-permute-start(bf16[1,128,768]{2,1,0:T(8,128)(2,1)S(1)} %get-tuple-element.316), channel_id=1, source_target_pairs={{0,1},{1,0},{2,3},{3,2},{4,5},{5,4},{6,7},{7,6},{8,9},{9,8},{10,11... | collective-permute-start | bytes 589832 | tf_op jit(solution)/shard_map/ppermute | solution.py:599
  10.3 45.1 %collective-permute-start.4 = (bf16[1,128,768]{2,1,0:T(8,128)(2,1)S(1)}, bf16[1,128,768]{2,1,0:T(8,128)(2,1)}, u32[]{:S(2)}, u32[]{:S(2)}) collective-permute-start(bf16[1,128,768]{2,1,0:T(8,128)(2,1)S(1)} %get-tuple-element.315), channel_id=1, source_target_pairs={{0,2},{1,3},{2,0},{3,1},{4,6},{5,7},{6,4},{7,5},{8,10},{9,11},{10,... | collective-permute-start | bytes 589832 | tf_op jit(solution)/shard_map/ppermute | solution.py:599
  25.7 29.8 %collective-permute-start.5 = (bf16[1,128,768]{2,1,0:T(8,128)(2,1)S(1)}, bf16[1,128,768]{2,1,0:T(8,128)(2,1)S(1)}, u32[]{:S(2)}, u32[]{:S(2)}) collective-permute-start(bf16[1,128,768]{2,1,0:T(8,128)(2,1)S(1)} %get-tuple-element.314), channel_id=1, source_target_pairs={{0,3},{1,2},{2,1},{3,0},{4,7},{5,6},{6,5},{7,4},{8,11},{9,10},{10,... | collective-permute-start | bytes 589832 | tf_op jit(solution)/shard_map/ppermute | solution.py:599
  26.4 7.1 %copy-start.7 = (bf16[8,128,768]{2,1,0:T(8,128)(2,1)S(1)}, bf16[8,128,768]{2,1,0:T(8,128)(2,1)}, u32[]{:S(2)}) copy-start(bf16[8,128,768]{2,1,0:T(8,128)(2,1)} %param.37) | copy-start | bytes 4718596
  33.6 63.1 %collective-permute-start.6 = (bf16[2,128,768]{2,1,0:T(8,128)(2,1)S(1)}, bf16[2,128,768]{2,1,0:T(8,128)(2,1)S(1)}, u32[]{:S(2)}, u32[]{:S(2)}) collective-permute-start(bf16[2,128,768]{2,1,0:T(8,128)(2,1)S(1)} %get-tuple-element.295), channel_id=1, source_target_pairs={{0,1},{1,0},{2,3},{3,2},{4,5},{5,4},{6,7},{7,6},{8,9},{9,8},{10,11... | collective-permute-start | bytes 1179656 | tf_op jit(solution)/shard_map/ppermute | solution.py:599
  43.9 52.8 %collective-permute-start.7 = (bf16[2,128,768]{2,1,0:T(8,128)(2,1)S(1)}, bf16[2,128,768]{2,1,0:T(8,128)(2,1)S(1)}, u32[]{:S(2)}, u32[]{:S(2)}) collective-permute-start(bf16[2,128,768]{2,1,0:T(8,128)(2,1)S(1)} %get-tuple-element.294), channel_id=1, source_target_pairs={{0,2},{1,3},{2,0},{3,1},{4,6},{5,7},{6,4},{7,5},{8,10},{9,11},{10,... | collective-permute-start | bytes 1179656 | tf_op jit(solution)/shard_map/ppermute | solution.py:599
  53.9 42.8 %collective-permute-start.8 = (bf16[2,128,768]{2,1,0:T(8,128)(2,1)S(1)}, bf16[2,128,768]{2,1,0:T(8,128)(2,1)S(1)}, u32[]{:S(2)}, u32[]{:S(2)}) collective-permute-start(bf16[2,128,768]{2,1,0:T(8,128)(2,1)S(1)} %get-tuple-element.293), channel_id=1, source_target_pairs={{0,3},{1,2},{2,1},{3,0},{4,7},{5,6},{6,5},{7,4},{8,11},{9,10},{10,... | collective-permute-start | bytes 1179656 | tf_op jit(solution)/shard_map/ppermute | solution.py:599
  113.7 28.3 %collective-permute-start.10 = (bf16[768,1536]{1,0:T(8,128)(2,1)}, bf16[768,1536]{1,0:T(8,128)(2,1)}, u32[]{:S(2)}, u32[]{:S(2)}) collective-permute-start(bf16[768,1536]{1,0:T(8,128)(2,1)} %get-tuple-element.160), channel_id=1, source_target_pairs={{0,4},{4,0},{8,12},{12,8},{16,20},{20,16},{24,28},{28,24},{1,5},{5... | collective-permute-start | bytes 7077896 | tf_op jit(solution)/shard_map/ppermute | solution.py:599
  113.8 30.2 %collective-permute-start.9 = (bf16[1536,768]{1,0:T(8,128)(2,1)}, bf16[1536,768]{1,0:T(8,128)(2,1)S(1)}, u32[]{:S(2)}, u32[]{:S(2)}) collective-permute-start(bf16[1536,768]{1,0:T(8,128)(2,1)} %get-tuple-element.158), channel_id=1, source_target_pairs={{0,4},{4,0},{8,12},{12,8},{16,20},{20,16},{24,28},{28,24},{1,5},{5... | collective-permute-start | bytes 7077896 | tf_op jit(solution)/shard_map/ppermute | solution.py:599
  147.5 28.3 %collective-permute-start.11 = (bf16[2,2,2,96,768]{4,3,1,2,0:T(8,128)(2,1)}, bf16[2,2,2,96,768]{4,3,1,2,0:T(8,128)(2,1)}, u32[]{:S(2)}, u32[]{:S(2)}) collective-permute-start(bf16[2,2,2,96,768]{4,3,1,2,0:T(8,128)(2,1)} %fusion.1), channel_id=1, source_target_pairs={{0,8},{4,12},{8,0},{12,4},{16,24},{20,28},{24,16},{28,20},{1,9},{5... | collective-permute-start | bytes 3538952 | tf_op jit(solution)/shard_map/ppermute | solution.py:599
  149.0 28.0 %collective-permute-start.12 = (bf16[2,2,2,48,1536]{4,3,1,2,0:T(8,128)(2,1)}, bf16[2,2,2,48,1536]{4,3,1,2,0:T(8,128)(2,1)}, u32[]{:S(2)}, u32[]{:S(2)}) collective-permute-start(bf16[2,2,2,48,1536]{4,3,1,2,0:T(8,128)(2,1)} %fusion.3), channel_id=1, source_target_pairs={{0,16},{4,20},{8,24},{12,28},{16,0},{20,4},{24,8},{28,12},{1,17},{... | collective-permute-start | bytes 3538952 | tf_op jit(solution)/shard_map/ppermute | solution.py:599
  180.9 23.1 %collective-permute-start.13 = (bf16[2,2,96,768]{3,2,0,1:T(8,128)(2,1)}, bf16[2,2,96,768]{3,2,0,1:T(8,128)(2,1)S(1)}, u32[]{:S(2)}, u32[]{:S(2)}) collective-permute-start(bf16[2,2,96,768]{3,2,0,1:T(8,128)(2,1)} %get-tuple-element.176), channel_id=1, source_target_pairs={{0,16},{4,20},{8,24},{12,28},{16,0},{20,4},{24,8},{28,12},{1,17},{... | collective-permute-start | bytes 1769480 | tf_op jit(solution)/shard_map/ppermute | solution.py:599
  182.4 21.7 %collective-permute-start.14 = (bf16[2,2,48,1536]{3,2,0,1:T(8,128)(2,1)S(1)}, bf16[2,2,48,1536]{3,2,0,1:T(8,128)(2,1)S(1)}, u32[]{:S(2)}, u32[]{:S(2)}) collective-permute-start(bf16[2,2,48,1536]{3,2,0,1:T(8,128)(2,1)S(1)} %get-tuple-element.178), channel_id=1, source_target_pairs={{0,8},{4,12},{8,0},{12,4},{16,24},{20,28},{24,16},{28,20},{1,9},{5... | collective-permute-start | bytes 1769480 | tf_op jit(solution)/shard_map/ppermute | solution.py:599
  185.4 19.2 %collective-permute-start.15 = (bf16[2,128,768]{2,1,0:T(8,128)(2,1)}, bf16[2,128,768]{2,1,0:T(8,128)(2,1)}, u32[]{:S(2)}, u32[]{:S(2)}) collective-permute-start(bf16[2,128,768]{2,1,0:T(8,128)(2,1)} %get-tuple-element.290), channel_id=1, source_target_pairs={{0,1},{1,0},{2,3},{3,2},{4,5},{5,4},{6,7},{7,6},{8,9},{9,8},{10,11... | collective-permute-start | bytes 1179656 | tf_op jit(solution)/shard_map/ppermute | solution.py:599
  186.4 30.1 %collective-permute-start.16 = (bf16[2,128,768]{2,1,0:T(8,128)(2,1)}, bf16[2,128,768]{2,1,0:T(8,128)(2,1)}, u32[]{:S(2)}, u32[]{:S(2)}) collective-permute-start(bf16[2,128,768]{2,1,0:T(8,128)(2,1)} %get-tuple-element.289), channel_id=1, source_target_pairs={{0,2},{1,3},{2,0},{3,1},{4,6},{5,7},{6,4},{7,5},{8,10},{9,11},{10,... | collective-permute-start | bytes 1179656 | tf_op jit(solution)/shard_map/ppermute | solution.py:599
  188.4 28.1 %collective-permute-start.17 = (bf16[2,128,768]{2,1,0:T(8,128)(2,1)S(1)}, bf16[2,128,768]{2,1,0:T(8,128)(2,1)}, u32[]{:S(2)}, u32[]{:S(2)}) collective-permute-start(bf16[2,128,768]{2,1,0:T(8,128)(2,1)S(1)} %get-tuple-element.288), channel_id=1, source_target_pairs={{0,3},{1,2},{2,1},{3,0},{4,7},{5,6},{6,5},{7,4},{8,11},{9,10},{10,... | collective-permute-start | bytes 1179656 | tf_op jit(solution)/shard_map/ppermute | solution.py:599
  204.0 30.0 %collective-permute-start.19 = (bf16[768,1152]{1,0:T(8,128)(2,1)}, bf16[768,1152]{1,0:T(8,128)(2,1)}, u32[]{:S(2)}, u32[]{:S(2)}) collective-permute-start(bf16[768,1152]{1,0:T(8,128)(2,1)} %get-tuple-element.200), channel_id=1, source_target_pairs={{0,4},{4,0},{8,12},{12,8},{16,20},{20,16},{24,28},{28,24},{1,5},{5... | collective-permute-start | bytes 5308424 | tf_op jit(solution)/shard_map/ppermute | solution.py:599
  216.5 15.5 %copy-start.9 = (bf16[768,768]{1,0:T(8,128)(2,1)S(1)}, bf16[768,768]{1,0:T(8,128)(2,1)}, u32[]{:S(2)}) copy-start(bf16[768,768]{1,0:T(8,128)(2,1)} %get-tuple-element.202) | copy-start | bytes 3538948
  233.6 22.2 %collective-permute-start.20 = (bf16[768,768]{1,0:T(8,128)(2,1)S(1)}, bf16[768,768]{1,0:T(8,128)(2,1)S(1)}, u32[]{:S(2)}, u32[]{:S(2)}) collective-permute-start(bf16[768,768]{1,0:T(8,128)(2,1)S(1)} %get-tuple-element.257), channel_id=1, source_target_pairs={{0,4},{4,0},{8,12},{12,8},{16,20},{20,16},{24,28},{28,24},{1,5},{5... | collective-permute-start | bytes 3538952 | tf_op jit(solution)/shard_map/ppermute | solution.py:599
  235.6 20.0 %collective-permute-start.18 = (bf16[2,48,3072]{2,1,0:T(8,128)(2,1)S(1)}, bf16[2,48,3072]{2,1,0:T(8,128)(2,1)S(1)}, u32[]{:S(2)}, u32[]{:S(2)}) collective-permute-start(bf16[2,48,3072]{2,1,0:T(8,128)(2,1)S(1)} %pad_maximum_fusion.12), channel_id=1, source_target_pairs={{0,1},{1,0},{2,3},{3,2},{4,5},{5,4},{6,7},{7,6},{8,9},{9,8},{10,11... | collective-permute-start | bytes 1769480 | tf_op jit(solution)/shard_map/ppermute | solution.py:599
  256.2 16.0 %collective-permute-start.21 = (bf16[48,3072]{1,0:T(8,128)(2,1)S(1)}, bf16[48,3072]{1,0:T(8,128)(2,1)S(1)}, u32[]{:S(2)}, u32[]{:S(2)}) collective-permute-start(bf16[48,3072]{1,0:T(8,128)(2,1)S(1)} %get-tuple-element.204), channel_id=1, source_target_pairs={{0,2},{1,3},{2,0},{3,1},{4,6},{5,7},{6,4},{7,5},{8,10},{9,11},{10,... | collective-permute-start | bytes 884744 | tf_op jit(solution)/shard_map/ppermute | solution.py:599
  259.0 20.8 %collective-permute-start.22 = (bf16[2,2,2,48,1152]{4,3,1,2,0:T(8,128)(2,1)S(1)}, bf16[2,2,2,48,1152]{4,3,1,2,0:T(8,128)(2,1)S(1)}, u32[]{:S(2)}, u32[]{:S(2)}) collective-permute-start(bf16[2,2,2,48,1152]{4,3,1,2,0:T(8,128)(2,1)S(1)} %fusion.5), channel_id=1, source_target_pairs={{0,8},{4,12},{8,0},{12,4},{16,24},{20,28},{24,16},{28,20},{1,9},{5... | collective-permute-start | bytes 2654216 | tf_op jit(solution)/shard_map/ppermute | solution.py:599
  260.4 14.2 %collective-permute-start.23 = (bf16[2,2,2,48,768]{4,3,1,2,0:T(8,128)(2,1)S(1)}, bf16[2,2,2,48,768]{4,3,1,2,0:T(8,128)(2,1)S(1)}, u32[]{:S(2)}, u32[]{:S(2)}) collective-permute-start(bf16[2,2,2,48,768]{4,3,1,2,0:T(8,128)(2,1)S(1)} %fusion.11), channel_id=1, source_target_pairs={{0,16},{4,20},{8,24},{12,28},{16,0},{20,4},{24,8},{28,12},{1,17},{... | collective-permute-start | bytes 1769480 | tf_op jit(solution)/shard_map/ppermute | solution.py:599
  280.0 7.3 %collective-permute-start.26 = (bf16[2,2,48,768]{3,2,0,1:T(8,128)(2,1)S(1)}, bf16[2,2,48,768]{3,2,0,1:T(8,128)(2,1)S(1)}, u32[]{:S(2)}, u32[]{:S(2)}) collective-permute-start(bf16[2,2,48,768]{3,2,0,1:T(8,128)(2,1)S(1)} %get-tuple-element.213), channel_id=1, source_target_pairs={{0,8},{4,12},{8,0},{12,4},{16,24},{20,28},{24,16},{28,20},{1,9},{5... | collective-permute-start | bytes 884744 | tf_op jit(solution)/shard_map/ppermute | solution.py:599
  281.5 14.2 %collective-permute-start.24 = (bf16[1,48,3072]{2,1,0:T(8,128)(2,1)S(1)}, bf16[1,48,3072]{2,1,0:T(8,128)(2,1)S(1)}, u32[]{:S(2)}, u32[]{:S(2)}) collective-permute-start(bf16[1,48,3072]{2,1,0:T(8,128)(2,1)S(1)} %fusion.20), channel_id=1, source_target_pairs={{0,2},{1,3},{2,0},{3,1},{4,6},{5,7},{6,4},{7,5},{8,10},{9,11},{10,... | collective-permute-start | bytes 884744 | tf_op jit(solution)/shard_map/ppermute | solution.py:599
  282.0 13.7 %collective-permute-start.25 = (bf16[2,2,48,1152]{3,2,0,1:T(8,128)(2,1)S(1)}, bf16[2,2,48,1152]{3,2,0,1:T(8,128)(2,1)S(1)}, u32[]{:S(2)}, u32[]{:S(2)}) collective-permute-start(bf16[2,2,48,1152]{3,2,0,1:T(8,128)(2,1)S(1)} %get-tuple-element.211), channel_id=1, source_target_pairs={{0,16},{4,20},{8,24},{12,28},{16,0},{20,4},{24,8},{28,12},{1,17},{... | collective-permute-start | bytes 1327112 | tf_op jit(solution)/shard_map/ppermute | solution.py:599
  295.9 11.6 %collective-permute-start.28 = (bf16[2,48,1920]{2,1,0:T(8,128)(2,1)S(1)}, bf16[2,48,1920]{2,1,0:T(8,128)(2,1)S(1)}, u32[]{:S(2)}, u32[]{:S(2)}) collective-permute-start(bf16[2,48,1920]{2,1,0:T(8,128)(2,1)S(1)} %pad_maximum_fusion.16), channel_id=1, source_target_pairs={{0,1},{1,0},{2,3},{3,2},{4,5},{5,4},{6,7},{7,6},{8,9},{9,8},{10,11... | collective-permute-start | bytes 1105928 | tf_op jit(solution)/shard_map/ppermute | solution.py:599
  296.0 22.7 %collective-permute-start.27 = (bf16[2,48,3072]{2,1,0:T(8,128)(2,1)S(1)}, bf16[2,48,3072]{2,1,0:T(8,128)(2,1)S(1)}, u32[]{:S(2)}, u32[]{:S(2)}) collective-permute-start(bf16[2,48,3072]{2,1,0:T(8,128)(2,1)S(1)} %pad_maximum_fusion.13), channel_id=1, source_target_pairs={{0,1},{1,0},{2,3},{3,2},{4,5},{5,4},{6,7},{7,6},{8,9},{9,8},{10,11... | collective-permute-start | bytes 1769480 | tf_op jit(solution)/shard_map/ppermute | solution.py:599
  318.9 10.1 %collective-permute-start.34 = (bf16[48,1920]{1,0:T(8,128)(2,1)S(1)}, bf16[48,1920]{1,0:T(8,128)(2,1)S(1)}, u32[]{:S(2)}, u32[]{:S(2)}) collective-permute-start(bf16[48,1920]{1,0:T(8,128)(2,1)S(1)} %get-tuple-element.221), channel_id=1, source_target_pairs={{0,2},{1,3},{2,0},{3,1},{4,6},{5,7},{6,4},{7,5},{8,10},{9,11},{10,... | collective-permute-start | bytes 552968 | tf_op jit(solution)/shard_map/ppermute | solution.py:599
  319.1 13.9 %collective-permute-start.33 = (bf16[4,48,1536]{2,1,0:T(8,128)(2,1)S(1)}, bf16[4,48,1536]{2,1,0:T(8,128)(2,1)S(1)}, u32[]{:S(2)}, u32[]{:S(2)}) collective-permute-start(bf16[4,48,1536]{2,1,0:T(8,128)(2,1)S(1)} %get-tuple-element.219), channel_id=1, source_target_pairs={{0,8},{4,12},{8,0},{12,4},{16,24},{20,28},{24,16},{28,20},{1,9},{5... | collective-permute-start | bytes 1769480 | tf_op jit(solution)/shard_map/ppermute | solution.py:599
  319.7 13.7 %collective-permute-start.32 = (bf16[4,48,1536]{2,1,0:T(8,128)(2,1)S(1)}, bf16[4,48,1536]{2,1,0:T(8,128)(2,1)S(1)}, u32[]{:S(2)}, u32[]{:S(2)}) collective-permute-start(bf16[4,48,1536]{2,1,0:T(8,128)(2,1)S(1)} %get-tuple-element.218), channel_id=1, source_target_pairs={{0,16},{4,20},{8,24},{12,28},{16,0},{20,4},{24,8},{28,12},{1,17},{... | collective-permute-start | bytes 1769480 | tf_op jit(solution)/shard_map/ppermute | solution.py:599
  333.5 25.5 %collective-permute-start.36 = (bf16[8,48,1536]{2,1,0:T(8,128)(2,1)S(1)}, bf16[8,48,1536]{2,1,0:T(8,128)(2,1)S(1)}, u32[]{:S(2)}, u32[]{:S(2)}) collective-permute-start(bf16[8,48,1536]{2,1,0:T(8,128)(2,1)S(1)} %pad_maximum_fusion.7), channel_id=1, source_target_pairs={{0,16},{4,20},{8,24},{12,28},{16,0},{20,4},{24,8},{28,12},{1,17},{... | collective-permute-start | bytes 3538952 | tf_op jit(solution)/shard_map/ppermute | solution.py:599
  334.1 25.2 %collective-permute-start.35 = (bf16[8,48,1536]{2,1,0:T(8,128)(2,1)S(1)}, bf16[8,48,1536]{2,1,0:T(8,128)(2,1)S(1)}, u32[]{:S(2)}, u32[]{:S(2)}) collective-permute-start(bf16[8,48,1536]{2,1,0:T(8,128)(2,1)S(1)} %pad_maximum_fusion.6), channel_id=1, source_target_pairs={{0,8},{4,12},{8,0},{12,4},{16,24},{20,28},{24,16},{28,20},{1,9},{5... | collective-permute-start | bytes 3538952 | tf_op jit(solution)/shard_map/ppermute | solution.py:599
  335.5 8.4 %collective-permute-start.37 = (bf16[1,48,1920]{2,1,0:T(8,128)(2,1)S(1)}, bf16[1,48,1920]{2,1,0:T(8,128)(2,1)S(1)}, u32[]{:S(2)}, u32[]{:S(2)}) collective-permute-start(bf16[1,48,1920]{2,1,0:T(8,128)(2,1)S(1)} %fusion.27), channel_id=1, source_target_pairs={{0,2},{1,3},{2,0},{3,1},{4,6},{5,7},{6,4},{7,5},{8,10},{9,11},{10,... | collective-permute-start | bytes 552968 | tf_op jit(solution)/shard_map/ppermute | solution.py:599
  361.0 7.5 %collective-permute-start.40 = (bf16[2,48,1920]{2,1,0:T(8,128)(2,1)S(1)}, bf16[2,48,1920]{2,1,0:T(8,128)(2,1)S(1)}, u32[]{:S(2)}, u32[]{:S(2)}) collective-permute-start(bf16[2,48,1920]{2,1,0:T(8,128)(2,1)S(1)} %pad_maximum_fusion.17), channel_id=1, source_target_pairs={{0,1},{1,0},{2,3},{3,2},{4,5},{5,4},{6,7},{7,6},{8,9},{9,8},{10,11... | collective-permute-start | bytes 1105928 | tf_op jit(solution)/shard_map/ppermute | solution.py:599
  362.1 40.6 %collective-permute-start.38 = (bf16[16,48,1536]{2,1,0:T(8,128)(2,1)}, bf16[16,48,1536]{2,1,0:T(8,128)(2,1)}, u32[]{:S(2)}, u32[]{:S(2)}) collective-permute-start(bf16[16,48,1536]{2,1,0:T(8,128)(2,1)} %pad_maximum_fusion.down_own_ref), channel_id=1, source_target_pairs={{0,4},{4,0},{8,12},{12,8},{16,20},{20,16},{24,28},{28,24},{1,5},{5... | collective-permute-start | bytes 7077896 | tf_op jit(solution)/shard_map/ppermute | solution.py:599
  362.1 40.6 %collective-permute-start.39 = (bf16[16,48,1536]{2,1,0:T(8,128)(2,1)S(1)}, bf16[16,48,1536]{2,1,0:T(8,128)(2,1)}, u32[]{:S(2)}, u32[]{:S(2)}) collective-permute-start(bf16[16,48,1536]{2,1,0:T(8,128)(2,1)S(1)} %pad_maximum_fusion.1.up_own_ref), channel_id=1, source_target_pairs={{0,4},{4,0},{8,12},{12,8},{16,20},{20,16},{24,28},{28,24},{1,5},{5... | collective-permute-start | bytes 7077896 | tf_op jit(solution)/shard_map/ppermute | solution.py:599
  368.6 11.6 %collective-permute-start.41 = (bf16[4,48,1152]{2,1,0:T(8,128)(2,1)S(1)}, bf16[4,48,1152]{2,1,0:T(8,128)(2,1)S(1)}, u32[]{:S(2)}, u32[]{:S(2)}) collective-permute-start(bf16[4,48,1152]{2,1,0:T(8,128)(2,1)S(1)} %slice.72), channel_id=1, source_target_pairs={{0,16},{4,20},{8,24},{12,28},{16,0},{20,4},{24,8},{28,12},{1,17},{... | collective-permute-start | bytes 1327112 | tf_op jit(solution)/shard_map/ppermute | solution.py:599
  370.0 9.3 %collective-permute-start.42 = (bf16[4,48,768]{2,1,0:T(8,128)(2,1)S(1)}, bf16[4,48,768]{2,1,0:T(8,128)(2,1)S(1)}, u32[]{:S(2)}, u32[]{:S(2)}) collective-permute-start(bf16[4,48,768]{2,1,0:T(8,128)(2,1)S(1)} %slice.73), channel_id=1, source_target_pairs={{0,8},{4,12},{8,0},{12,4},{16,24},{20,28},{24,16},{28,20},{1,9},{5... | collective-permute-start | bytes 884744 | tf_op jit(solution)/shard_map/ppermute | solution.py:599
  380.4 15.5 %collective-permute-start.43 = (bf16[8,48,1152]{2,1,0:T(8,128)(2,1)S(1)}, bf16[8,48,1152]{2,1,0:T(8,128)(2,1)}, u32[]{:S(2)}, u32[]{:S(2)}) collective-permute-start(bf16[8,48,1152]{2,1,0:T(8,128)(2,1)S(1)} %pad_maximum_fusion.9), channel_id=1, source_target_pairs={{0,8},{4,12},{8,0},{12,4},{16,24},{20,28},{24,16},{28,20},{1,9},{5... | collective-permute-start | bytes 2654216 | tf_op jit(solution)/shard_map/ppermute | solution.py:599
  381.9 10.2 %collective-permute-start.44 = (bf16[8,48,768]{2,1,0:T(8,128)(2,1)}, bf16[8,48,768]{2,1,0:T(8,128)(2,1)}, u32[]{:S(2)}, u32[]{:S(2)}) collective-permute-start(bf16[8,48,768]{2,1,0:T(8,128)(2,1)} %pad_maximum_fusion.14), channel_id=1, source_target_pairs={{0,16},{4,20},{8,24},{12,28},{16,0},{20,4},{24,8},{28,12},{1,17},{... | collective-permute-start | bytes 1769480 | tf_op jit(solution)/shard_map/ppermute | solution.py:599
  385.3 14.3 %copy-start.4 = (bf16[8,48,1152]{2,1,0:T(8,128)(2,1)S(1)}, bf16[8,48,1152]{2,1,0:T(8,128)(2,1)}, u32[]{:S(2)}) copy-start(bf16[8,48,1152]{2,1,0:T(8,128)(2,1)} %copy-done.3) | copy-start | bytes 2654212
  385.3 32.8 %collective-permute-start.29 = (bf16[2,128,768]{2,1,0:T(8,128)(2,1)}, bf16[2,128,768]{2,1,0:T(8,128)(2,1)}, u32[]{:S(2)}, u32[]{:S(2)}) collective-permute-start(bf16[2,128,768]{2,1,0:T(8,128)(2,1)} %get-tuple-element.282), channel_id=1, source_target_pairs={{0,1},{1,0},{2,3},{3,2},{4,5},{5,4},{6,7},{7,6},{8,9},{9,8},{10,11... | collective-permute-start | bytes 1179656 | tf_op jit(solution)/shard_map/ppermute | solution.py:599
  392.1 26.1 %collective-permute-start.30 = (bf16[2,128,768]{2,1,0:T(8,128)(2,1)}, bf16[2,128,768]{2,1,0:T(8,128)(2,1)}, u32[]{:S(2)}, u32[]{:S(2)}) collective-permute-start(bf16[2,128,768]{2,1,0:T(8,128)(2,1)} %get-tuple-element.281), channel_id=1, source_target_pairs={{0,2},{1,3},{2,0},{3,1},{4,6},{5,7},{6,4},{7,5},{8,10},{9,11},{10,... | collective-permute-start | bytes 1179656 | tf_op jit(solution)/shard_map/ppermute | solution.py:599
  395.8 22.3 %collective-permute-start.31 = (bf16[2,128,768]{2,1,0:T(8,128)(2,1)S(1)}, bf16[2,128,768]{2,1,0:T(8,128)(2,1)}, u32[]{:S(2)}, u32[]{:S(2)}) collective-permute-start(bf16[2,128,768]{2,1,0:T(8,128)(2,1)S(1)} %get-tuple-element.280), channel_id=1, source_target_pairs={{0,3},{1,2},{2,1},{3,0},{4,7},{5,6},{6,5},{7,4},{8,11},{9,10},{10,... | collective-permute-start | bytes 1179656 | tf_op jit(solution)/shard_map/ppermute | solution.py:599
  399.7 18.6 %copy-start.2 = (bf16[16,48,768]{2,1,0:T(8,128)(2,1)}, bf16[16,48,768]{2,1,0:T(8,128)(2,1)S(1)}, u32[]{:S(2)}) copy-start(bf16[16,48,768]{2,1,0:T(8,128)(2,1)S(1)} %pad_maximum_fusion.8.own_ref) | copy-start | bytes 3538948
  402.7 15.5 %copy-start.1 = (bf16[16,48,1152]{2,1,0:T(8,128)(2,1)S(1)}, bf16[16,48,1152]{2,1,0:T(8,128)(2,1)}, u32[]{:S(2)}) copy-start(bf16[16,48,1152]{2,1,0:T(8,128)(2,1)} %pad_maximum_fusion.2.qkv_own_ref) | copy-start | bytes 5308420
  418.2 6.4 %collective-permute-start.45 = (bf16[16,48,1152]{2,1,0:T(8,128)(2,1)S(1)}, bf16[16,48,1152]{2,1,0:T(8,128)(2,1)}, u32[]{:S(2)}, u32[]{:S(2)}) collective-permute-start(bf16[16,48,1152]{2,1,0:T(8,128)(2,1)S(1)} %copy-done.1), channel_id=1, source_target_pairs={{0,4},{4,0},{8,12},{12,8},{16,20},{20,16},{24,28},{28,24},{1,5},{5... | collective-permute-start | bytes 5308424 | tf_op jit(solution)/shard_map/ppermute | solution.py:599
  418.3 6.3 %collective-permute-start.46 = (bf16[16,48,768]{2,1,0:T(8,128)(2,1)S(1)}, bf16[16,48,768]{2,1,0:T(8,128)(2,1)}, u32[]{:S(2)}, u32[]{:S(2)}) collective-permute-start(bf16[16,48,768]{2,1,0:T(8,128)(2,1)S(1)} %pad_maximum_fusion.8.own_ref), channel_id=1, source_target_pairs={{0,4},{4,0},{8,12},{12,8},{16,20},{20,16},{24,28},{28,24},{1,5},{5... | collective-permute-start | bytes 3538952 | tf_op jit(solution)/shard_map/ppermute | solution.py:599
  (8 other events, 15.4 us)
